TPU v7x, 768 devices: a whole 4x8x12 slice. The times are simulated.
768 devices in a mesh: edata: 4 (over x), expert: 16 (over y, core), tensor: 12 (over z).
Axes of the slice: x: 4, y: 8, z: 12, core: 2. Of those that a mesh axis runs over, the one named last changes fastest.
Arguments:
- grad_out: bfloat16 [2048, 4096], P(('edata', 'expert')), may hold values from -6 to 6
- gates: bfloat16 [2048, 8], P(('edata', 'expert')), may hold values from 0.019897461 to 0.5
- expert_ids: int32 [2048, 8], P(('edata', 'expert')), may hold values from 0 to 31, all different within a row; in each aligned block of 32 rows (0 to 31, 32 to 63, ...) at most 12 rows name the same one
- hidden: bfloat16 [4, 16, 32, 12, 1536], P('edata', None, 'expert', None, 'tensor'), may hold values from -0.19921875 to 0.19921875
- down_weight: bfloat16 [32, 1536, 4096], P('expert', 'tensor'), may hold values from -0.15625 to 0.15625
- moment_one: bfloat16 [4096, 32, 1536], P('edata', 'expert', 'tensor'), may hold values from -0.119628906 to 0.119628906
- moment_two: float32 [4096, 32, 1536], P('edata', 'expert', 'tensor'), may hold values from 0.0001 to 0.01
Outputs:
- grad_hidden: bfloat16 [4, 16, 32, 12, 1536], P('edata', None, 'expert', None, 'tensor')
- grad_gates: float32 [2048, 8], P(('edata', 'expert'))
- new_weight: bfloat16 [4096, 32, 1536], P('edata', 'expert', 'tensor')
- new_moment_one: bfloat16 [4096, 32, 1536], P('edata', 'expert', 'tensor')
- new_moment_two: float32 [4096, 32, 1536], P('edata', 'expert', 'tensor')
Inputs may be any that keep to these rules, and one draw needn't show every extreme that they name: `expert_ids`: each row names 8 different experts. Among the rows of one source block of 32 tokens no expert is named more than 12 times, and in every draw some expert is named exactly 12 times by some block.
All inputs are finite; a program needn't handle non-finite values.
Results may differ from a plain program's by a relative error of at most 0.012.
Values may be sent and summed in bfloat16 or wider, within the bound.
No kernel may reach another device: no remote copies, remote signals or barrier semaphores. Data moves between devices by JAX's collectives and lax.ppermute only.
A program may use at most 128 MiB of HBM per device.

v0:
```python
import jax
import jax.numpy as jnp
from jax import lax
from jax.sharding import PartitionSpec as P

beta_one = 0.9
beta_two = 0.999
adam_eps = 1e-08
learn_rate = 0.01
corr_two = 0.6323045752


def route_slots(expert_ids, experts, capacity):
    flat_ids = expert_ids.reshape(-1)
    onehot = (flat_ids[:, None] == jnp.arange(experts, dtype=jnp.int32)[None, :]).astype(jnp.int32)
    before = jnp.sum((jnp.cumsum(onehot, axis=0) - onehot) * onehot, axis=1)
    slot_index = flat_ids * capacity + before
    return slot_index[None, :] == jnp.arange(experts * capacity, dtype=jnp.int32)[:, None]


def shards(grad_out, gates, expert_ids, hidden, down_weight, moment_one, moment_two):
    token_count, choices_per = expert_ids.shape
    groups = lax.axis_size("expert")
    held_experts = down_weight.shape[0]
    experts = groups * held_experts
    capacity = hidden.shape[3]
    model_width = grad_out.shape[1]
    group_rows = held_experts * capacity
    placed = route_slots(expert_ids, experts, capacity)
    per_token = jnp.any(
        placed.reshape(experts * capacity, token_count, choices_per), axis=2
    ).astype(jnp.bfloat16)
    slot_gates = jnp.sum(
        jnp.where(
            placed, gates.reshape(-1).astype(jnp.float32)[None, :], jnp.zeros((), jnp.float32)
        ),
        axis=1,
    ).astype(jnp.bfloat16)
    send_rows = jnp.dot(per_token, grad_out, preferred_element_type=jnp.float32).astype(
        jnp.bfloat16
    )
    send_rows = send_rows.reshape(groups, group_rows, model_width)
    send_gate = slot_gates.reshape(groups, group_rows)
    arrived, arrived_gate = (
        lax.all_to_all(send_rows, "expert", split_axis=0, concat_axis=0, tiled=True),
        lax.all_to_all(send_gate, "expert", split_axis=0, concat_axis=0, tiled=True),
    )
    arrived = arrived.reshape(groups, held_experts, capacity, model_width)
    gate_scale = arrived_gate.reshape(groups, held_experts, capacity, 1).astype(jnp.float32)
    saved = hidden[0]
    upstream = jnp.einsum(
        "secd,efd->secf", arrived, down_weight, preferred_element_type=jnp.float32
    )
    grad_hidden = (gate_scale * upstream).astype(jnp.bfloat16)[None]
    gate_part = jnp.sum(saved.astype(jnp.float32) * upstream, axis=3)
    gate_total = lax.psum(gate_part, "tensor")
    gate_home = lax.all_to_all(
        gate_total.reshape(groups, group_rows), "expert", split_axis=0, concat_axis=0, tiled=True
    )
    slot_grad = gate_home.reshape(experts * capacity)
    grad_gates = jnp.sum(
        jnp.where(placed, slot_grad[:, None], jnp.zeros((), jnp.float32)), axis=0
    ).reshape(token_count, choices_per)
    weighted = (gate_scale * arrived.astype(jnp.float32)).astype(jnp.bfloat16)
    replicas = lax.axis_size("edata")
    shard_width = model_width // replicas
    grad = lax.psum_scatter(
        jnp.einsum("secd,secf->def", weighted, saved, preferred_element_type=jnp.float32).astype(
            jnp.bfloat16
        ),
        "edata",
        scatter_dimension=0,
        tiled=True,
    ).astype(jnp.float32)
    offset = lax.axis_index("edata") * shard_width
    weight_shard = lax.dynamic_slice_in_dim(down_weight, offset, shard_width, 2)
    weight_shard = jnp.transpose(weight_shard, (2, 0, 1)).astype(jnp.float32)
    moment_new = beta_one * moment_one.astype(jnp.float32) + (1.0 - beta_one) * grad
    second_new = beta_two * moment_two + (1.0 - beta_two) * grad * grad
    update = moment_new / (jnp.sqrt(second_new / corr_two) + adam_eps)
    weight_new = (weight_shard - learn_rate * update).astype(jnp.bfloat16)
    return (grad_hidden, grad_gates, weight_new, moment_new.astype(jnp.bfloat16), second_new)


def solution(mesh):
    return jax.shard_map(
        shards,
        mesh=mesh,
        in_specs=(
            P(("edata", "expert"), None),
            P(("edata", "expert"), None),
            P(("edata", "expert"), None),
            P("edata", None, "expert", None, "tensor"),
            P("expert", "tensor", None),
            P("edata", "expert", "tensor"),
            P("edata", "expert", "tensor"),
        ),
        out_specs=(
            P("edata", None, "expert", None, "tensor"),
            P(("edata", "expert"), None),
            P("edata", "expert", "tensor"),
            P("edata", "expert", "tensor"),
            P("edata", "expert", "tensor"),
        ),
        check_vma=False,
    )
```

profile of v0, /device:TPU:1, one launch (start us, length us, event | category | flops | bytes accessed | tf_op | source)
XLA Modules:
  0.0 200.0 jit_solution(818426786891981036)
XLA Ops:
  7.2 0.0 copy-start
  7.2 0.9 copy.59
  8.1 0.1 eq.46
  8.2 0.1 reshape.97
  8.3 0.6 reduce-window.6
  8.9 0.2 slice_reduce_fusion
  9.1 0.1 fusion.18
  9.2 0.1 reduce_sum.40
  9.3 0.2 fusion.12
  9.5 2.0 convolution_convert_fusion
  11.5 86.5 %all_to_all.20 = bf16[16,24,4096]{2,1,0:T(8,128)(2,1)S(1)} all-to-all(bf16[16,24,4096]{2,1,0:T(8,128)(2,1)S(1)} %bitcast.57), channel_id=1, replica_groups=mesh['edata'=4,'expert'=16,'tensor'=12] {'expert'}, dimensions={0} | all-to-all | bytes 6291456 | tf_op jit(solution)/shard_map/all_to_all | solution.py:45
  98.0 0.0 copy-start.2
  98.0 1.7 copy.66
  99.7 0.0 copy-start.1
  99.7 0.0 copy-start.3
  99.8 1.6 copy-done.1
  101.4 0.0 copy-done
  101.4 0.0 copy-done.2
  101.4 1.0 multiply_reduce_fusion
  102.5 0.1 copy.81
  102.5 24.1 %psum.7 = f32[16,1,24]{2,0,1:T(8,128)} all-reduce(f32[16,1,24]{2,0,1:T(8,128)S(1)} %copy.81), channel_id=1, replica_groups=mesh['edata'=4,'expert'=16,'tensor'=12] {'tensor'}, use_global_device_ids=true, to_apply=%region_6.7 | all-reduce | flops 384 | bytes 3072 | tf_op jit(solution)/shard_map/psum | solution.py:56
  126.7 8.4 %all-to-all-start.2 = ((f32[16,1,24]{2,1,0:T(1,128)}), f32[16,1,24]{2,1,0:T(1,128)S(1)}, u32[]{:S(2)}, u32[]{:S(2)}) async-start(f32[16,1,24]{2,1,0:T(1,128)} %bitcast.8), calls=%async_computation.2 | async-start | bytes 16384 | tf_op jit(solution)/shard_map/all_to_all | solution.py:57
  135.1 0.0 reduce-scatter.2.cloned.1.call-start
  135.1 0.0 copy-done.3
  135.1 0.1 copy.62
  135.2 0.1 reshape.102
  135.3 6.7 %all-to-all-done.2 = f32[16,1,24]{2,1,0:T(1,128)S(1)} async-done(((f32[16,1,24]{2,1,0:T(1,128)}), f32[16,1,24]{2,1,0:T(1,128)S(1)}, u32[]{:S(2)}, u32[]{:S(2)}) %all-to-all-start.2) | async-done | bytes 1568 | tf_op jit(solution)/shard_map/all_to_all | solution.py:57
  142.0 0.5 broadcast.36
  142.5 0.7 reduce.9
  143.2 0.1 broadcast_in_dim.34
  143.3 0.2 select_reduce_fusion
  143.5 0.1 convert_element_type.106
  143.6 10.1 %all_to_all.21 = bf16[16,1,24]{2,1,0:T(2,128)(2,1)S(1)} all-to-all(bf16[16,1,24]{2,1,0:T(2,128)(2,1)S(1)} %convert_element_type.106), channel_id=1, replica_groups=mesh['edata'=4,'expert'=16,'tensor'=12] {'expert'}, dimensions={0} | all-to-all | bytes 1536 | tf_op jit(solution)/shard_map/all_to_all | solution.py:46
  153.7 0.1 reshape.103
  153.8 0.1 copy.64
  153.9 5.1 %fusion.1 = bf16[4096,2,128]{2,0,1:T(8,128)(2,1)} fusion(bf16[16,2,12,4096]{3,0,2,1:T(8,128)(2,1)} %bitcast.59, f32[16,2,12]{0,2,1:T(8,128)S(1)} %copy.64, bf16[1,16,2,12,128]{4,2,3,1,0:T(2,128)(2,1)S(1)} %copy-done.2), kind=kOutput, calls=%fused_computation.4 | convolution fusion | flops 408420352 | bytes 5342720 | tf_op jit(solution)/shard_map/secd,secf->def/dot_general | solution.py:68
  159.0 0.0 reduce-scatter.2.cloned.1.call-update
  159.1 0.3 copy.82
  159.4 0.1 reshape.101
  159.4 0.7 copy.75
  160.1 0.1 fusion.13
  160.2 0.7 copy.74
  161.0 25.4 %reduce-scatter.2.cloned.1.call-done = bf16[1024,2,128]{2,0,1:T(8,128)(2,1)} async-done(((bf16[4096,2,128]{2,0,1:T(8,128)(2,1)}), bf16[1024,2,128]{2,0,1:T(8,128)(2,1)}) %reduce-scatter.2.cloned.1.call-update) | async-done | bytes 524304 | tf_op jit(solution)/shard_map/reduce_scatter | solution.py:67
  186.4 2.4 %fusion.9 = (f32[1024,2,128]{2,0,1:T(8,128)S(1)}, bf16[1024,2,128]{2,0,1:T(8,128)(2,1)S(1)}, bf16[1024,2,128]{2,0,1:T(8,128)(2,1)S(1)}) fusion(bf16[1024,2,128]{2,0,1:T(8,128)(2,1)} %reduce-scatter.2.cloned.1.call-done, f32[1024,2,128]{2,1,0:T(2,128)} %param.13, bf16[1024,2,128]{2,1,0:T(2,128)(2,1)} %param.12, bf16[2,128,1024]{1,2,0:T(8,128)(2,1)S(1)} %copy.82), kind=kLoop, calls=%fused_computation.12 | loop fusion | flops 4456448 | bytes 4718592 | tf_op jit(solution)/shard_map/add | solution.py:79
  188.7 1.8 copy.78
  190.5 1.3 copy.76
  191.9 1.3 copy.77
  (8 shorter events, 0.1 us)
Async XLA Ops:
  7.2 94.2 %copy-start = (bf16[2,128,4096]{2,1,0:T(8,128)(2,1)S(1)}, bf16[2,128,4096]{2,1,0:T(8,128)(2,1)}, u32[]{:S(2)}) copy-start(bf16[2,128,4096]{2,1,0:T(8,128)(2,1)} %param.11) | copy-start | bytes 6291460
  98.0 3.4 %copy-start.2 = (bf16[1,16,2,12,128]{4,2,3,1,0:T(2,128)(2,1)S(1)}, bf16[1,16,2,12,128]{4,2,3,1,0:T(2,128)(2,1)}, u32[]{:S(2)}) copy-start(bf16[1,16,2,12,128]{4,2,3,1,0:T(2,128)(2,1)} %param.10) | copy-start | bytes 294916
  99.7 1.7 copy-start.1
  99.7 35.4 %copy-start.3 = (bf16[32,8]{0,1:T(8,128)(2,1)S(1)}, bf16[32,8]{0,1:T(8,128)(2,1)}, u32[]{:S(2)}) copy-start(bf16[32,8]{0,1:T(8,128)(2,1)} %param.8) | copy-start | bytes 1540
  126.7 15.3 %all-to-all-start.2 = ((f32[16,1,24]{2,1,0:T(1,128)}), f32[16,1,24]{2,1,0:T(1,128)S(1)}, u32[]{:S(2)}, u32[]{:S(2)}) async-start(f32[16,1,24]{2,1,0:T(1,128)} %bitcast.8), calls=%async_computation.2 | async-start | bytes 16384 | tf_op jit(solution)/shard_map/all_to_all | solution.py:57
  135.1 51.3 %reduce-scatter.2.cloned.1.call-start = ((), (), s32[]{:S(2)}) async-start(), calls=%async_computation.4 | async-start | bytes 2621440 | tf_op jit(solution)/shard_map/reduce_scatter | solution.py:67
Sparse Core Ops, SparseCore 0:
  159.1 27.1 reduce-scatter.1
where the time goes:
time: 200 us
  blocking collectives  121 us (60%)
  waiting for transfers between devices  32.1 us (16%)
  between operations  14.2 us (7%)
  local copies, waits for them, and re-layouts  12.1 us (6%)
  starting transfers between devices  8.44 us (4%)
  matrix products  8.12 us (4%)
  other arithmetic  4.36 us (2%)
    all_to_all x1, blocking collectives, shards(): lax.all_to_all(send_rows, 'expert', split_axis=0, concat_axis=0, tiled=True)  86.5 us
    reduce_scatter x1, waiting for transfers between devices, shards(): lax.psum_scatter(jnp.einsum('secd,secf->def', weighted, saved, preferred_...  25.4 us
    psum x1, blocking collectives, shards(): gate_total = lax.psum(gate_part, 'tensor')  24.1 us
    all_to_all x1, blocking collectives, shards(): lax.all_to_all(send_gate, 'expert', split_axis=0, concat_axis=0, tiled=True)  10.1 us
    unnamed x15, local copies, waits for them, and re-layouts  8.71 us
    all_to_all x1, starting transfers between devices, shards(): lax.all_to_all(gate_total.reshape(groups, group_rows), 'expert', split_ax...  8.4 us
    all_to_all x1, waiting for transfers between devices, shards(): lax.all_to_all(gate_total.reshape(groups, group_rows), 'expert', split_ax...  6.7 us
    dot_general x1, matrix products, shards(): jnp.einsum('secd,secf->def', weighted, saved, preferred_element_type=jnp....  5.09 us
  transfers between devices with their start and end apart: 2, of which 2 were waited for; matrix products, arithmetic and copies ran while one was open for 1% of the time, Pallas kernels for 0%

commit v1 on v0

v1 whole, which is shorter than its diff:
```python
import functools

import jax
import jax.numpy as jnp
from jax import lax
from jax.experimental import pallas as pl
from jax.experimental.pallas import tpu as pltpu
from jax.sharding import Mesh, PartitionSpec as P

beta_one = 0.9
beta_two = 0.999
adam_eps = 1e-08
learn_rate = 0.01
corr_two = 0.6323045752

F32 = jnp.float32
BF16 = jnp.bfloat16
LANES = 128
PARAMS = pltpu.CompilerParams(vmem_limit_bytes=40 * 1024 * 1024)


def dot(a, b, over, precision=None):
    return lax.dot_general(
        a, b, (((over[0],), (over[1],)), ((), ())), precision=precision, preferred_element_type=F32
    )


def expert_base():
    return ((lax.axis_index("ey") * 2 + lax.axis_index("core")) * 2).astype(F32)


def routed(meta, base, tokens, rows):
    count = meta.shape[0]
    meta = meta.astype(F32)
    ids, gates = meta[:, :8], meta[:, 8:16]
    hits = [ids == base + e for e in range(2)]
    named = [jnp.sum(jnp.where(h, 1.0, 0.0), axis=1, keepdims=True) for h in hits]
    gate = [jnp.sum(jnp.where(h, gates, 0.0), axis=1, keepdims=True) for h in hits]
    lane = lax.broadcasted_iota(jnp.int32, (count, LANES), 1)
    marks = jnp.where(lane == 0, named[0], jnp.where(lane == 1, named[1], 0.0)).astype(BF16)
    row_i = lax.broadcasted_iota(jnp.int32, (count, count), 0)
    col_i = lax.broadcasted_iota(jnp.int32, (count, count), 1)
    earlier = ((row_i // tokens == col_i // tokens) & (col_i < row_i)).astype(F32).astype(BF16)
    rank = dot(earlier, marks, (1, 0))
    block = (lax.broadcasted_iota(jnp.int32, (count, 1), 0) // tokens).astype(F32)
    slot_rows = (count // tokens) * rows
    slot_lane = lax.broadcasted_iota(jnp.int32, (count, slot_rows), 1).astype(F32)
    keys = [
        jnp.where(named[e] > 0.5, block * rows + 2.0 * rank[:, e : e + 1] + e, -1.0)
        for e in range(2)
    ]
    onehot = ((slot_lane == keys[0]) | (slot_lane == keys[1])).astype(F32).astype(BF16)
    return onehot, gate


def by_expert(hid):
    odd = lax.broadcasted_iota(jnp.int32, hid.shape, 0) % 2
    hid = hid.astype(F32)
    return jnp.concatenate(
        [jnp.where(odd == 0, hid, 0.0), jnp.where(odd == 1, hid, 0.0)], axis=1
    ).astype(BF16)


def gate_lanes(gate):
    return jnp.concatenate([jnp.broadcast_to(g, (g.shape[0], LANES)) for g in gate], axis=1)


def own_kernel(tokens, rows, width, part, mine, theirs, weight, hid, grad_hidden, gate_part, grad):
    core = lax.axis_index("core")
    base = expert_base()
    column = pl.multiple_of(lax.axis_index("edata") * part, LANES)
    total = None
    gates_out = None
    count = mine.shape[0]
    slots = count // tokens * rows
    for rel, ref in enumerate((mine, theirs)):
        side = core if rel == 0 else 1 - core
        onehot, gate = routed(ref[:, width : width + LANES], base, tokens, rows)
        saved = dot(onehot, by_expert(hid[rel * slots : (rel + 1) * slots, :]), (1, 0))
        up = dot(ref[:, :width], weight[...], (1, 1))
        scale = gate_lanes(gate)
        picked = dot(onehot, (scale * up).astype(BF16), (0, 0))
        even = lax.broadcasted_iota(jnp.int32, (slots, LANES), 0) % 2 == 0
        picked = jnp.where(even, picked[:, :LANES], picked[:, LANES:]).astype(BF16)
        for block in range(count // tokens):
            grad_hidden[block, side] = picked[block * rows : (block + 1) * rows]
        prod = saved * up
        column_e = [
            jnp.sum(prod[:, e * LANES : (e + 1) * LANES], axis=1, keepdims=True) for e in range(2)
        ]
        lane = lax.broadcasted_iota(jnp.int32, (count, LANES), 1)
        tok = lax.broadcasted_iota(jnp.int32, (count, LANES), 0) % tokens
        spread = jnp.zeros((count, LANES), F32)
        for e in range(2):
            spread = jnp.where(lane == (side * 2 + e) * tokens + tok, column_e[e], spread)
        block_of = lax.broadcasted_iota(jnp.int32, (count // tokens, count), 1) // tokens
        block_row = lax.broadcasted_iota(jnp.int32, (count // tokens, count), 0)
        pick = (block_of == block_row).astype(F32)
        piece = dot(pick, spread, (1, 0), lax.Precision.HIGHEST)
        gates_out = piece if gates_out is None else gates_out + piece
        scaled = (scale * saved).astype(BF16)
        term = dot(ref[:, pl.ds(column, part)], scaled, (0, 0))
        total = term if total is None else total + term
    gate_part[...] = gates_out
    grad[...] = total


def adam_kernel(
    tokens, rows, part, mine, theirs, grad, hid, weight, one, two,
    new_weight, new_one, new_two, grad_rows, weight_rows,
):
    base = expert_base()
    total = grad[...]
    blocks = mine.shape[0]
    others = mine.shape[1] // tokens
    slots = blocks * rows
    for rel, ref in enumerate((mine, theirs)):
        for other in range(others):
            at = pl.ds(other * tokens, tokens)
            meta = ref[:, at, part : part + LANES].reshape(blocks * tokens, LANES)
            onehot, gate = routed(meta, base, tokens, rows)
            saved = dot(
                onehot, by_expert(hid[other, rel * slots : (rel + 1) * slots, :]), (1, 0)
            )
            scaled = (gate_lanes(gate) * saved).astype(BF16)
            toks = ref[:, at, :part].reshape(blocks * tokens, part)
            total = total + dot(toks, scaled, (0, 0))
    column = pl.multiple_of(lax.axis_index("edata") * part, LANES)
    for e in range(2):
        grad_rows[pl.ds(e, part, 2), :] = total[:, e * LANES : (e + 1) * LANES]
        piece = weight[e * LANES : (e + 1) * LANES, pl.ds(column, part)].astype(F32)
        weight_rows[pl.ds(e, part, 2), :] = piece.T
    g = grad_rows[...]
    first = beta_one * one[...].astype(F32) + (1.0 - beta_one) * g
    second = beta_two * two[...] + (1.0 - beta_two) * g * g
    update = first / (jnp.sqrt(second / corr_two) + adam_eps)
    new_weight[...] = (weight_rows[...] - learn_rate * update).astype(BF16)
    new_one[...] = first.astype(BF16)
    new_two[...] = second


def cost(tokens, terms, moved):
    return pl.CostEstimate(flops=2 * tokens * terms, bytes_accessed=moved, transcendentals=0)


def shards(grad_out, gates, expert_ids, hidden, down_weight, moment_one, moment_two):
    tokens, width = grad_out.shape
    choices = gates.shape[1]
    blocks, replicas = lax.axis_size("ey"), lax.axis_size("edata")
    held, capacity = hidden.shape[2], hidden.shape[3]
    rows = held * capacity
    part = width // replicas
    index, core = lax.axis_index("edata"), lax.axis_index("core")
    swap = [(0, 1), (1, 0)]

    meta = jnp.concatenate(
        [expert_ids.astype(BF16), gates, jnp.zeros((tokens, LANES - 2 * choices), BF16)], axis=1
    )
    own = lax.all_gather(jnp.concatenate([grad_out, meta], axis=1), "ey", axis=0, tiled=True)
    own_other = lax.ppermute(own, "core", swap)

    to_replicas = jnp.stack(
        [
            jnp.concatenate([grad_out[:, j * part : (j + 1) * part], meta], axis=1)
            for j in range(replicas)
        ]
    )
    from_replicas = lax.all_to_all(to_replicas, "edata", 0, 0, tiled=True)
    rest = lax.dynamic_slice_in_dim(
        jnp.concatenate([from_replicas, from_replicas[:-1]], axis=0), index + 1, replicas - 1, 0
    ).reshape((replicas - 1) * tokens, part + LANES)
    saved = jnp.transpose(hidden[0], (0, 2, 1, 3)).reshape(blocks, 2, rows, LANES)
    saved = jnp.where(core == 0, saved, saved[:, ::-1])
    saved = jnp.transpose(saved, (1, 0, 2, 3)).reshape(2 * blocks * rows, LANES)
    saved_all = lax.all_to_all(
        jnp.broadcast_to(saved[None], (replicas,) + saved.shape), "edata", 0, 0, tiled=True
    )
    saved_rest = lax.dynamic_slice_in_dim(
        jnp.concatenate([saved_all, saved_all[:-1]], axis=0), index + 1, replicas - 1, 0
    )

    rest, saved_rest = lax.optimization_barrier((rest, saved_rest))
    rest = lax.all_gather(rest, "ey", axis=0)

    weight = down_weight.reshape(held * LANES, width)
    grad_hidden, gate_part, grad = pl.pallas_call(
        functools.partial(own_kernel, tokens, rows, width, part),
        out_shape=(
            jax.ShapeDtypeStruct((blocks, 2, rows, LANES), BF16),
            jax.ShapeDtypeStruct((blocks, LANES), F32),
            jax.ShapeDtypeStruct((part, held * LANES), F32),
        ),
        compiler_params=PARAMS,
        cost_estimate=cost(2 * blocks * tokens, (width + part) * held * LANES, 8 << 20),
        name="own_tokens",
    )(own, own_other, weight, saved)

    planes = lax.axis_size("tensor")
    gate_all = lax.all_to_all(
        jnp.broadcast_to(gate_part[None], (planes,) + gate_part.shape), "tensor", 0, 0, tiled=True
    )
    gate_sum = jnp.sum(gate_all, axis=0)
    rest, grad, gate_sum = lax.optimization_barrier((rest, grad, gate_sum))
    rest_other = lax.ppermute(rest, "core", swap)
    gate_sum = gate_sum.reshape(2 * blocks, 1, held * tokens)
    gate_home = lax.all_to_all(gate_sum, ("ey", "core"), 0, 0, tiled=True)
    by_token = gate_home.reshape(2 * blocks * held, tokens)
    experts = lax.broadcasted_iota(jnp.int32, (2 * blocks * held, tokens, choices), 0)
    grad_gates = jnp.sum(
        jnp.where(experts == expert_ids[None], by_token[:, :, None], 0.0), axis=0
    )

    flat = (part * held, LANES)
    new_weight, new_one, new_two = pl.pallas_call(
        functools.partial(adam_kernel, tokens, rows, part),
        out_shape=(
            jax.ShapeDtypeStruct(flat, BF16),
            jax.ShapeDtypeStruct(flat, BF16),
            jax.ShapeDtypeStruct(flat, F32),
        ),
        scratch_shapes=[pltpu.VMEM(flat, F32), pltpu.VMEM(flat, F32)],
        compiler_params=PARAMS,
        cost_estimate=cost(
            2 * blocks * tokens * (replicas - 1), part * held * LANES, 12 << 20
        ),
        name="adam",
    )(
        rest, rest_other, grad, saved_rest, weight,
        moment_one.reshape(flat), moment_two.reshape(flat),
    )
    grad_hidden = jnp.transpose(
        grad_hidden.reshape(1, 2 * blocks, capacity, held, LANES), (0, 1, 3, 2, 4)
    )
    shape = moment_one.shape
    return (
        grad_hidden, grad_gates, new_weight.reshape(shape), new_one.reshape(shape),
        new_two.reshape(shape),
    )


def solution(mesh):
    replicas, groups, planes = mesh.devices.shape
    fine = Mesh(
        mesh.devices.reshape(replicas, groups // 2, 2, planes), ("edata", "ey", "core", "tensor")
    )
    expert = ("ey", "core")
    block = P(("edata", "ey", "core"), None)
    state = P("edata", expert, "tensor")
    saved = P("edata", None, expert, None, "tensor")
    return jax.shard_map(
        shards,
        mesh=fine,
        in_specs=(block, block, block, saved, P(expert, "tensor", None), state, state),
        out_specs=(saved, block, state, state, state),
        check_vma=False,
    )
```

time: 200 us -> 146 us (0.73)
  blocking collectives: 121 us -> 30.6 us
  waiting for transfers between devices: 32.1 us -> 53.5 us
  starting transfers between devices: 8.44 us -> 20.8 us
  Pallas kernels: 0 us -> 11.1 us
  matrix products: 8.12 us -> 0 us
    all_to_all x2, blocking collectives: 96.6 us -> 30.6 us  [the longest x1 19.4 us: shards(): lax.all_to_all(jnp.broadcast_to(gate_part[None], (planes,) + gate_part.sh...]
    all_gather x0 -> x2, waiting for transfers between devices: none -> 37.2 us  [the longest x1 26.3 us: shards(): lax.all_gather(jnp.concatenate([grad_out, meta], axis=1), 'ey', axis=0, t...]
    reduce_scatter x1 -> x0, waiting for transfers between devices: 25.4 us -> none  [shards(): lax.psum_scatter(jnp.einsum('secd,secf->def', weighted, saved, preferred_...]
    psum x1 -> x0, blocking collectives: 24.1 us -> none  [shards(): gate_total = lax.psum(gate_part, 'tensor')]
    ppermute x0 -> x2, starting transfers between devices: none -> 12.5 us  [the longest x1 6.25 us: shards(): rest_other = lax.ppermute(rest, 'core', swap)]
    pallas_call x0 -> x2, Pallas kernels: none -> 11.1 us  [the longest x1 7.24 us: shards(): pl.pallas_call(functools.partial(adam_kernel, tokens, rows, part), out_sh...]
    dot_general x3 -> x0, matrix products: 8.12 us -> none  [the longest x1 5.09 us: shards(): jnp.einsum('secd,secf->def', weighted, saved, preferred_element_type=jnp....]
    all_to_all x1 -> x2, waiting for transfers between devices: 6.7 us -> 12.2 us  [the longest x1 6.53 us: shards(): lax.all_to_all(jnp.broadcast_to(saved[None], (replicas,) + saved.shape),...]
  transfers between devices with their start and end apart: 2 -> 6, of which waited for: 2 -> 5; matrix products, arithmetic and copies ran while one was open for 1% -> 4% of each run, Pallas kernels for 0% -> 3%
where the time goes in v1:
time: 146 us
  waiting for transfers between devices  53.5 us (37%)
  blocking collectives  30.6 us (21%)
  starting transfers between devices  20.8 us (14%)
  between operations  14.1 us (10%)
  local copies, waits for them, and re-layouts  12.5 us (9%)
  Pallas kernels  11.1 us (8%)
  other arithmetic  3.02 us (2%)
    all_gather x1, waiting for transfers between devices, shards(): lax.all_gather(jnp.concatenate([grad_out, meta], axis=1), 'ey', axis=0, t...  26.3 us
    all_to_all x1, blocking collectives, shards(): lax.all_to_all(jnp.broadcast_to(gate_part[None], (planes,) + gate_part.sh...  19.4 us
    all_to_all x1, blocking collectives, shards(): gate_home = lax.all_to_all(gate_sum, ('ey', 'core'), 0, 0, tiled=True)  11.2 us
    all_gather x1, waiting for transfers between devices, shards(): rest = lax.all_gather(rest, 'ey', axis=0)  10.9 us
    unnamed x20, local copies, waits for them, and re-layouts  7.86 us
    pallas_call x1, Pallas kernels, shards(): pl.pallas_call(functools.partial(adam_kernel, tokens, rows, part), out_sh...  7.24 us
    all_to_all x1, waiting for transfers between devices, shards(): lax.all_to_all(jnp.broadcast_to(saved[None], (replicas,) + saved.shape),...  6.53 us
    ppermute x1, starting transfers between devices, shards(): rest_other = lax.ppermute(rest, 'core', swap)  6.25 us
  transfers between devices with their start and end apart: 6, of which 5 were waited for; matrix products, arithmetic and copies ran while one was open for 4% of the time, Pallas kernels for 3%

profile of v1, /device:TPU:1, one launch (start us, length us, event | category | flops | bytes accessed | tf_op | source)
XLA Modules:
  0.0 145.6 jit_solution(8089468615506728379)
XLA Ops:
  7.2 0.0 copy-start.7
  7.2 0.0 all-gather.4.cloned.1.call-start
  7.2 0.8 copy.30
  8.0 0.8 copy.31
  8.8 1.7 %concatenate.27 = bf16[32,4224]{1,0:T(8,128)(2,1)} concatenate(bf16[32,4096]{1,0:T(8,128)(2,1)} %param.7, bf16[32,8]{1,0:T(8,128)(2,1)S(1)} %convert_element_type.3, bf16[32,8]{1,0:T(8,128)(2,1)S(1)} %copy.31, bf16[32,112]{1,0:T(8,128)(2,1)S(1)} %broadcast_in_dim.29), dimensions={1} | concatenate | bytes 540672 | tf_op jit(solution)/shard_map/concatenate | solution.py:159
  10.5 0.0 all-gather.4.cloned.1.call-update
  10.5 1.0 fusion.2
  11.5 0.1 concatenate.31
  11.6 0.1 concatenate.30
  11.7 0.1 concatenate.29
  11.8 0.1 concatenate.28
  11.9 0.8 pad_maximum_fusion
  12.6 4.8 %all-to-all-start = ((bf16[4,32,1152]{2,1,0:T(8,128)(2,1)}), bf16[4,32,1152]{2,1,0:T(8,128)(2,1)S(1)}, u32[]{:S(2)}, u32[]{:S(2)}) async-start(bf16[4,32,1152]{2,1,0:T(8,128)(2,1)} %pad_maximum_fusion), calls=%async_computation | async-start | bytes 589824 | tf_op jit(solution)/shard_map/all_to_all | solution.py:168
  17.5 0.0 copy-done.7
  17.5 5.7 %all-to-all-done = bf16[4,32,1152]{2,1,0:T(8,128)(2,1)S(1)} async-done(((bf16[4,32,1152]{2,1,0:T(8,128)(2,1)}), bf16[4,32,1152]{2,1,0:T(8,128)(2,1)S(1)}, u32[]{:S(2)}, u32[]{:S(2)}) %all-to-all-start) | async-done | bytes 294944 | tf_op jit(solution)/shard_map/all_to_all | solution.py:168
  23.2 0.0 copy-start
  23.2 0.8 broadcast_in_dim.30
  24.0 3.5 %all-to-all-start.1 = ((bf16[4,384,128]{2,1,0:T(8,128)(2,1)}), bf16[4,384,128]{2,1,0:T(8,128)(2,1)S(1)}, u32[]{:S(2)}, u32[]{:S(2)}) async-start(bf16[4,384,128]{2,1,0:T(8,128)(2,1)} %broadcast_in_dim.30), calls=%async_computation.1 | async-start | bytes 786432 | tf_op jit(solution)/shard_map/all_to_all | solution.py:175
  27.5 0.0 all-gather.6.cloned.1.call-start
  27.5 0.8 fusion.1
  28.3 6.5 %all-to-all-done.1 = bf16[4,384,128]{2,1,0:T(8,128)(2,1)S(1)} async-done(((bf16[4,384,128]{2,1,0:T(8,128)(2,1)}), bf16[4,384,128]{2,1,0:T(8,128)(2,1)S(1)}, u32[]{:S(2)}, u32[]{:S(2)}) %all-to-all-start.1) | async-done | bytes 393248 | tf_op jit(solution)/shard_map/all_to_all | solution.py:175
  34.9 0.1 fusion.hid
  35.0 0.0 all-gather.6.cloned.1.call-update
  35.0 26.3 %all-gather.4.cloned.1.call-done.mine = bf16[256,4224]{1,0:T(8,128)(2,1)} async-done(((bf16[32,4224]{1,0:T(8,128)(2,1)}), bf16[256,4224]{1,0:T(8,128)(2,1)}) %all-gather.4.cloned.1.call-update) | async-done | bytes 2162704 | tf_op jit(solution)/shard_map/all_gather | solution.py:159
  61.3 6.2 %collective-permute-start = (bf16[256,4224]{1,0:T(8,128)(2,1)}, bf16[256,4224]{1,0:T(8,128)(2,1)S(1)}, u32[]{:S(2)}, u32[]{:S(2)}) collective-permute-start(bf16[256,4224]{1,0:T(8,128)(2,1)} %all-gather.4.cloned.1.call-done.mine), channel_id=1, source_target_pairs={{0,12},{12,0},{1,13},{13,1},{2,14},{14,2},{3,15},{15,3},{4,16},{16... | collective-permute-start | bytes 6488072 | tf_op jit(solution)/shard_map/ppermute | solution.py:160
  67.6 4.1 %collective-permute-done.theirs = bf16[256,4224]{1,0:T(8,128)(2,1)S(1)} collective-permute-done((bf16[256,4224]{1,0:T(8,128)(2,1)}, bf16[256,4224]{1,0:T(8,128)(2,1)S(1)}, u32[]{:S(2)}, u32[]{:S(2)}) %collective-permute-start) | collective-permute-done | bytes 2162720 | tf_op jit(solution)/shard_map/ppermute | solution.py:160
  71.6 0.0 copy-done
  71.6 0.0 copy-start.1
  71.6 1.6 %copy-done.1 = bf16[256,4224]{1,0:T(8,128)(2,1)S(1)} copy-done((bf16[256,4224]{1,0:T(8,128)(2,1)S(1)}, bf16[256,4224]{1,0:T(8,128)(2,1)}, u32[]{:S(2)}) %copy-start.1) | copy-done | bytes 2162712
  73.2 0.0 copy-start.8
  73.2 0.0 copy-start.3
  73.3 3.8 %own_tokens.1 = (bf16[8,2,24,128]{3,2,1,0:T(8,128)(2,1)}, f32[8,128]{1,0:T(8,128)S(1)}, f32[1024,256]{1,0:T(8,128)S(1)}) custom-call(bf16[256,4224]{1,0:T(8,128)(2,1)S(1)} %copy-done.1, bf16[256,4224]{1,0:T(8,128)(2,1)S(1)} %collective-permute-done.theirs, bf16[256,4096]{1,0:T(8,128)(2,1)S(1)} %bitcast.24, bf16[384,128]{1,0:T(8,128)(2,1)S(1)} %bitcast.30), custom_call_target="tpu_custom_call" | custom-call | flops 1342177280 | bytes 8388608 | tf_op jit(solution)/shard_map/own_tokens/pallas_call | solution.py:186
  77.1 0.0 copy-start.4
  77.1 1.0 copy-done.4
  78.1 19.4 %all_to_all.20 = f32[12,8,128]{2,1,0:T(8,128)S(1)} all-to-all(f32[12,8,128]{2,1,0:T(8,128)S(1)} %broadcast_in_dim.31), channel_id=1, replica_groups=mesh['edata'=4,'ey'=8,'core'=2,'tensor'=12] {'tensor'}, dimensions={0} | all-to-all | bytes 98304 | tf_op jit(solution)/shard_map/all_to_all | solution.py:199
  97.4 10.9 %all-gather.6.cloned.1.call-done = bf16[768,1152]{1,0:T(8,128)(2,1)} async-done(((bf16[96,1152]{1,0:T(8,128)(2,1)}), bf16[768,1152]{1,0:T(8,128)(2,1)}) %all-gather.6.cloned.1.call-update) | async-done | bytes 1769488 | tf_op jit(solution)/shard_map/all_gather | solution.py:183
  108.4 6.3 %collective-permute-start.1 = (bf16[8,96,1152]{2,1,0:T(8,128)(2,1)}, bf16[8,96,1152]{2,1,0:T(8,128)(2,1)}, u32[]{:S(2)}, u32[]{:S(2)}) collective-permute-start(bf16[8,96,1152]{2,1,0:T(8,128)(2,1)} %bitcast.26), channel_id=1, source_target_pairs={{0,12},{12,0},{1,13},{13,1},{2,14},{14,2},{3,15},{15,3},{4,16},{16... | collective-permute-start | bytes 5308424 | tf_op jit(solution)/shard_map/ppermute | solution.py:204
  114.6 0.1 reshape.52
  114.7 11.2 %all_to_all.21 = f32[16,1,64]{2,1,0:T(1,128)S(1)} all-to-all(f32[16,1,64]{2,1,0:T(1,128)S(1)} %bitcast.38), channel_id=1, replica_groups=mesh['edata'=4,'ey'=8,'core'=2,'tensor'=12] {'ey','core'}, dimensions={0} | all-to-all | bytes 8192 | tf_op jit(solution)/shard_map/all_to_all | solution.py:206
  125.9 0.5 broadcast.5
  126.4 0.7 reduce.3
  127.1 0.1 broadcast_in_dim.32
  127.2 0.0 copy-done.8
  127.2 0.6 select_reduce_fusion
  127.8 0.0 collective-permute-done.1.theirs
  127.8 0.0 copy-done.3
  127.8 0.0 copy-start.2
  127.8 1.5 %copy-done.2 = bf16[768,1152]{1,0:T(8,128)(2,1)S(1)} copy-done((bf16[768,1152]{1,0:T(8,128)(2,1)S(1)}, bf16[768,1152]{1,0:T(8,128)(2,1)}, u32[]{:S(2)}) %copy-start.2) | copy-done | bytes 1769496
  129.3 0.0 copy-start.5
  129.3 1.2 copy-done.5
  130.5 0.0 copy-start.6
  130.5 1.0 copy-done.6
  131.6 7.2 %adam.1 = (bf16[2048,128]{1,0:T(8,128)(2,1)}, bf16[2048,128]{1,0:T(8,128)(2,1)}, f32[2048,128]{1,0:T(8,128)}) custom-call(bf16[8,96,1152]{2,1,0:T(8,128)(2,1)S(1)} %bitcast.27, bf16[8,96,1152]{2,1,0:T(8,128)(2,1)} %collective-permute-done.1.theirs, f32[1024,256]{1,0:T(8,128)S(1)} %copy-done.5, bf16[3,384,128]{2,1,0:T(8,128)(2,1)S(1)} %fusion.hid, ...), custom_call_target="tpu_custom_call" | custom-call | flops 805306368 | bytes 12582912 | tf_op jit(solution)/shard_map/adam/pallas_call | solution.py:214
  (8 shorter events, 0.1 us)
Async XLA Ops:
  7.2 10.3 %copy-start.7 = (bf16[1,16,2,12,128]{4,2,3,1,0:T(2,128)(2,1)S(1)}, bf16[1,16,2,12,128]{4,2,3,1,0:T(2,128)(2,1)}, u32[]{:S(2)}) copy-start(bf16[1,16,2,12,128]{4,2,3,1,0:T(2,128)(2,1)} %param.10) | copy-start | bytes 294916
  7.2 54.2 %all-gather.4.cloned.1.call-start = ((), (), s32[]{:S(2)}) async-start(), calls=%async_computation.4 | async-start | bytes 2433024 | tf_op jit(solution)/shard_map/all_gather | solution.py:159
  12.6 10.5 %all-to-all-start = ((bf16[4,32,1152]{2,1,0:T(8,128)(2,1)}), bf16[4,32,1152]{2,1,0:T(8,128)(2,1)S(1)}, u32[]{:S(2)}, u32[]{:S(2)}) async-start(bf16[4,32,1152]{2,1,0:T(8,128)(2,1)} %pad_maximum_fusion), calls=%async_computation | async-start | bytes 589824 | tf_op jit(solution)/shard_map/all_to_all | solution.py:168
  23.2 48.4 %copy-start = (bf16[2,128,4096]{2,1,0:T(8,128)(2,1)S(1)}, bf16[2,128,4096]{2,1,0:T(8,128)(2,1)}, u32[]{:S(2)}) copy-start(bf16[2,128,4096]{2,1,0:T(8,128)(2,1)} %param.11) | copy-start | bytes 6291460
  24.0 10.9 %all-to-all-start.1 = ((bf16[4,384,128]{2,1,0:T(8,128)(2,1)}), bf16[4,384,128]{2,1,0:T(8,128)(2,1)S(1)}, u32[]{:S(2)}, u32[]{:S(2)}) async-start(bf16[4,384,128]{2,1,0:T(8,128)(2,1)} %broadcast_in_dim.30), calls=%async_computation.1 | async-start | bytes 786432 | tf_op jit(solution)/shard_map/all_to_all | solution.py:175
  27.5 80.9 %all-gather.6.cloned.1.call-start = ((), (), s32[]{:S(2)}) async-start(), calls=%async_computation.5 | async-start | bytes 1990656 | tf_op jit(solution)/shard_map/all_gather | solution.py:183
  61.3 10.3 %collective-permute-start = (bf16[256,4224]{1,0:T(8,128)(2,1)}, bf16[256,4224]{1,0:T(8,128)(2,1)S(1)}, u32[]{:S(2)}, u32[]{:S(2)}) collective-permute-start(bf16[256,4224]{1,0:T(8,128)(2,1)} %all-gather.4.cloned.1.call-done.mine), channel_id=1, source_target_pairs={{0,12},{12,0},{1,13},{13,1},{2,14},{14,2},{3,15},{15,3},{4,16},{16... | collective-permute-start | bytes 6488072 | tf_op jit(solution)/shard_map/ppermute | solution.py:160
  71.6 1.6 %copy-start.1 = (bf16[256,4224]{1,0:T(8,128)(2,1)S(1)}, bf16[256,4224]{1,0:T(8,128)(2,1)}, u32[]{:S(2)}) copy-start(bf16[256,4224]{1,0:T(8,128)(2,1)} %all-gather.4.cloned.1.call-done.mine) | copy-start | bytes 6488068
  73.2 53.9 %copy-start.8 = (s32[32,8]{0,1:T(8,128)S(1)}, s32[32,8]{0,1:T(8,128)}, u32[]{:S(2)}) copy-start(s32[32,8]{0,1:T(8,128)} %param.9) | copy-start | bytes 3076
  73.2 54.6 %copy-start.3 = (f32[1024,2,128]{2,1,0:T(2,128)S(1)}, f32[1024,2,128]{2,1,0:T(2,128)}, u32[]{:S(2)}) copy-start(f32[1024,2,128]{2,1,0:T(2,128)} %param.13) | copy-start | bytes 3145732
  77.1 1.0 copy-start.4
  108.4 19.4 %collective-permute-start.1 = (bf16[8,96,1152]{2,1,0:T(8,128)(2,1)}, bf16[8,96,1152]{2,1,0:T(8,128)(2,1)}, u32[]{:S(2)}, u32[]{:S(2)}) collective-permute-start(bf16[8,96,1152]{2,1,0:T(8,128)(2,1)} %bitcast.26), channel_id=1, source_target_pairs={{0,12},{12,0},{1,13},{13,1},{2,14},{14,2},{3,15},{15,3},{4,16},{16... | collective-permute-start | bytes 5308424 | tf_op jit(solution)/shard_map/ppermute | solution.py:204
  127.8 1.5 %copy-start.2 = (bf16[768,1152]{1,0:T(8,128)(2,1)S(1)}, bf16[768,1152]{1,0:T(8,128)(2,1)}, u32[]{:S(2)}) copy-start(bf16[768,1152]{1,0:T(8,128)(2,1)} %all-gather.6.cloned.1.call-done) | copy-start | bytes 5308420
  129.3 1.2 copy-start.5
  130.5 1.0 copy-start.6
Sparse Core Ops, SparseCore 0:
  11.0 50.3 all-gather.3
  63.7 44.6 all-gather.5

commit v2 on v1

--- a/solution.py
+++ b/solution.py
@@ -65,44 +65,59 @@
     return jnp.concatenate([jnp.broadcast_to(g, (g.shape[0], LANES)) for g in gate], axis=1)
 
 
-def own_kernel(tokens, rows, width, part, mine, theirs, weight, hid, grad_hidden, gate_part, grad):
-    core = lax.axis_index("core")
+def own_kernel(tokens, rows, width, *refs):
+    mine, theirs = refs[:9], refs[9:14]
+    weight, hid, grad_hidden, gate_part, grad, toks = refs[14:]
+    core, line = lax.axis_index("core"), lax.axis_index("ey")
     base = expert_base()
-    column = pl.multiple_of(lax.axis_index("edata") * part, LANES)
-    total = None
+    blocks = grad_hidden.shape[0]
+    count = blocks * tokens
+    at = 0
+    for ref in mine + theirs:
+        toks[at : at + ref.shape[0], :] = ref[...]
+        at += ref.shape[0]
+    where = [(line + step) % blocks for step in arrival(blocks)]
     gates_out = None
-    count = mine.shape[0]
-    slots = count // tokens * rows
-    for rel, ref in enumerate((mine, theirs)):
+    scaled = []
+    for rel in range(2):
         side = core if rel == 0 else 1 - core
-        onehot, gate = routed(ref[:, width : width + LANES], base, tokens, rows)
-        saved = dot(onehot, by_expert(hid[rel * slots : (rel + 1) * slots, :]), (1, 0))
-        up = dot(ref[:, :width], weight[...], (1, 1))
+        here = slice(rel * count, (rel + 1) * count)
+        onehot, gate = routed(toks[here, width : width + LANES], base, tokens, rows)
+        slots = jnp.concatenate([hid[block, side].astype(F32) for block in where], axis=0)
+        saved = dot(onehot, by_expert(slots), (1, 0))
+        up = dot(toks[here, :width], weight[...], (1, 1))
         scale = gate_lanes(gate)
+        scaled.append((scale * saved).astype(BF16))
         picked = dot(onehot, (scale * up).astype(BF16), (0, 0))
-        even = lax.broadcasted_iota(jnp.int32, (slots, LANES), 0) % 2 == 0
-        picked = jnp.where(even, picked[:, :LANES], picked[:, LANES:]).astype(BF16)
-        for block in range(count // tokens):
-            grad_hidden[block, side] = picked[block * rows : (block + 1) * rows]
+        even = lax.broadcasted_iota(jnp.int32, (blocks * rows, LANES), 0) % 2 == 0
+        picked = jnp.where(even, picked[:, :LANES], picked[:, LANES:])
+        for order, block in enumerate(where):
+            grad_hidden[block, side] = picked[order * rows : (order + 1) * rows].astype(BF16)
         prod = saved * up
-        column_e = [
-            jnp.sum(prod[:, e * LANES : (e + 1) * LANES], axis=1, keepdims=True) for e in range(2)
-        ]
         lane = lax.broadcasted_iota(jnp.int32, (count, LANES), 1)
         tok = lax.broadcasted_iota(jnp.int32, (count, LANES), 0) % tokens
         spread = jnp.zeros((count, LANES), F32)
         for e in range(2):
-            spread = jnp.where(lane == (side * 2 + e) * tokens + tok, column_e[e], spread)
-        block_of = lax.broadcasted_iota(jnp.int32, (count // tokens, count), 1) // tokens
-        block_row = lax.broadcasted_iota(jnp.int32, (count // tokens, count), 0)
-        pick = (block_of == block_row).astype(F32)
+            total = jnp.sum(prod[:, e * LANES : (e + 1) * LANES], axis=1, keepdims=True)
+            spread = jnp.where(lane == (side * 2 + e) * tokens + tok, total, spread)
+        order = lax.broadcasted_iota(jnp.int32, (blocks, count), 1) // tokens
+        away = jnp.where(order % 2 == 1, -((order + 1) // 2), order // 2)
+        row = lax.broadcasted_iota(jnp.int32, (blocks, count), 0)
+        pick = ((line + away + blocks) % blocks == row).astype(F32)
         piece = dot(pick, spread, (1, 0), lax.Precision.HIGHEST)
         gates_out = piece if gates_out is None else gates_out + piece
-        scaled = (scale * saved).astype(BF16)
-        term = dot(ref[:, pl.ds(column, part)], scaled, (0, 0))
-        total = term if total is None else total + term
     gate_part[...] = gates_out
-    grad[...] = total
+    scaled = jnp.concatenate(scaled, axis=0)
+    part = grad.shape[0]
+    column = pl.multiple_of(lax.axis_index("edata") * part, LANES)
+    grad[...] = dot(toks[:, pl.ds(column, part)], scaled, (0, 0))
+
+
+def arrival(blocks):
+    steps = [0]
+    for away in range(1, blocks // 2):
+        steps += [blocks - away, away]
+    return steps + [blocks // 2]
 
 
 def adam_kernel(
@@ -143,22 +158,36 @@
     return pl.CostEstimate(flops=2 * tokens * terms, bytes_accessed=moved, transcendentals=0)
 
 
+def gathered(own, between):
+    size, half = lax.axis_size("ey"), own.shape[0] // 2
+    ahead = [(i, (i + 1) % size) for i in range(size)]
+    back = [(i, (i - 1) % size) for i in range(size)]
+    swap = [(0, 1), (1, 0)]
+    mine, theirs = [own], [lax.ppermute(own, "core", swap)]
+    up = down = own
+    for step in range(1, size // 2):
+        up, down = lax.ppermute(up, "ey", ahead), lax.ppermute(down, "ey", back)
+        up, down = between(step, up, down)
+        mine += [up, down]
+        theirs.append(lax.ppermute(jnp.concatenate([up, down], axis=0), "core", swap))
+    up, down = lax.ppermute(up[:half], "ey", ahead), lax.ppermute(down[half:], "ey", back)
+    mine += [up, down]
+    theirs.append(lax.ppermute(jnp.concatenate([up, down], axis=0), "core", swap))
+    return mine, theirs
+
+
 def shards(grad_out, gates, expert_ids, hidden, down_weight, moment_one, moment_two):
     tokens, width = grad_out.shape
     choices = gates.shape[1]
-    blocks, replicas = lax.axis_size("ey"), lax.axis_size("edata")
+    blocks, replicas, planes = (lax.axis_size(n) for n in ("ey", "edata", "tensor"))
     held, capacity = hidden.shape[2], hidden.shape[3]
     rows = held * capacity
     part = width // replicas
     index, core = lax.axis_index("edata"), lax.axis_index("core")
-    swap = [(0, 1), (1, 0)]
 
     meta = jnp.concatenate(
         [expert_ids.astype(BF16), gates, jnp.zeros((tokens, LANES - 2 * choices), BF16)], axis=1
     )
-    own = lax.all_gather(jnp.concatenate([grad_out, meta], axis=1), "ey", axis=0, tiled=True)
-    own_other = lax.ppermute(own, "core", swap)
-
     to_replicas = jnp.stack(
         [
             jnp.concatenate([grad_out[:, j * part : (j + 1) * part], meta], axis=1)
@@ -166,50 +195,50 @@
         ]
     )
     from_replicas = lax.all_to_all(to_replicas, "edata", 0, 0, tiled=True)
-    rest = lax.dynamic_slice_in_dim(
-        jnp.concatenate([from_replicas, from_replicas[:-1]], axis=0), index + 1, replicas - 1, 0
-    ).reshape((replicas - 1) * tokens, part + LANES)
     saved = jnp.transpose(hidden[0], (0, 2, 1, 3)).reshape(blocks, 2, rows, LANES)
-    saved = jnp.where(core == 0, saved, saved[:, ::-1])
-    saved = jnp.transpose(saved, (1, 0, 2, 3)).reshape(2 * blocks * rows, LANES)
-    saved_all = lax.all_to_all(
-        jnp.broadcast_to(saved[None], (replicas,) + saved.shape), "edata", 0, 0, tiled=True
-    )
-    saved_rest = lax.dynamic_slice_in_dim(
-        jnp.concatenate([saved_all, saved_all[:-1]], axis=0), index + 1, replicas - 1, 0
-    )
-
-    rest, saved_rest = lax.optimization_barrier((rest, saved_rest))
-    rest = lax.all_gather(rest, "ey", axis=0)
-
+    by_side = jnp.where(core == 0, saved, saved[:, ::-1])
+    by_side = jnp.transpose(by_side, (1, 0, 2, 3)).reshape(2 * blocks * rows, LANES)
+    by_side = jnp.broadcast_to(by_side[None], (replicas,) + by_side.shape)
+
+    def not_own(block):
+        twice = jnp.concatenate([block, block[:-1]], axis=0)
+        return lax.dynamic_slice_in_dim(twice, index + 1, replicas - 1, 0)
+
+    held_back = {}
+
+    def between(step, up, down):
+        if step == 1:
+            side, tokens_in, up, down = lax.optimization_barrier((by_side, from_replicas, up, down))
+            rest = not_own(tokens_in).reshape((replicas - 1) * tokens, part + LANES)
+            held_back["rest"] = lax.all_gather(rest, "ey", axis=0)
+            held_back["saved"] = lax.all_to_all(side, "edata", 0, 0, tiled=True)
+        if step == 3:
+            held_back["saved"], up, down = lax.optimization_barrier((held_back["saved"], up, down))
+        return up, down
+
+    mine, theirs = gathered(jnp.concatenate([grad_out, meta], axis=1), between)
+    rest, saved_rest = held_back["rest"], not_own(held_back["saved"])
     weight = down_weight.reshape(held * LANES, width)
+    every = 2 * blocks * tokens
     grad_hidden, gate_part, grad = pl.pallas_call(
-        functools.partial(own_kernel, tokens, rows, width, part),
+        functools.partial(own_kernel, tokens, rows, width),
         out_shape=(
             jax.ShapeDtypeStruct((blocks, 2, rows, LANES), BF16),
             jax.ShapeDtypeStruct((blocks, LANES), F32),
             jax.ShapeDtypeStruct((part, held * LANES), F32),
         ),
+        scratch_shapes=[pltpu.VMEM((every, width + LANES), BF16)],
         compiler_params=PARAMS,
-        cost_estimate=cost(2 * blocks * tokens, (width + part) * held * LANES, 8 << 20),
+        cost_estimate=cost(every, (width + part) * held * LANES, 8 << 20),
         name="own_tokens",
-    )(own, own_other, weight, saved)
-
-    planes = lax.axis_size("tensor")
-    gate_all = lax.all_to_all(
-        jnp.broadcast_to(gate_part[None], (planes,) + gate_part.shape), "tensor", 0, 0, tiled=True
-    )
-    gate_sum = jnp.sum(gate_all, axis=0)
-    rest, grad, gate_sum = lax.optimization_barrier((rest, grad, gate_sum))
-    rest_other = lax.ppermute(rest, "core", swap)
-    gate_sum = gate_sum.reshape(2 * blocks, 1, held * tokens)
-    gate_home = lax.all_to_all(gate_sum, ("ey", "core"), 0, 0, tiled=True)
-    by_token = gate_home.reshape(2 * blocks * held, tokens)
-    experts = lax.broadcasted_iota(jnp.int32, (2 * blocks * held, tokens, choices), 0)
-    grad_gates = jnp.sum(
-        jnp.where(experts == expert_ids[None], by_token[:, :, None], 0.0), axis=0
-    )
-
+    )(*mine, *theirs, weight, saved)
+
+    rest, grad, gate_part = lax.optimization_barrier((rest, grad, gate_part))
+    rest_other = lax.ppermute(rest, "core", [(0, 1), (1, 0)])
+    gate_send = jnp.broadcast_to(
+        gate_part.reshape(2 * blocks, 1, held * tokens), (2 * blocks, planes, held * tokens)
+    ).reshape(2 * blocks * planes, 1, held * tokens)
+    gate_home = lax.all_to_all(gate_send, ("ey", "core", "tensor"), 0, 0, tiled=True)
     flat = (part * held, LANES)
     new_weight, new_one, new_two = pl.pallas_call(
         functools.partial(adam_kernel, tokens, rows, part),
@@ -220,13 +249,18 @@
         ),
         scratch_shapes=[pltpu.VMEM(flat, F32), pltpu.VMEM(flat, F32)],
         compiler_params=PARAMS,
-        cost_estimate=cost(
-            2 * blocks * tokens * (replicas - 1), part * held * LANES, 12 << 20
-        ),
+        cost_estimate=cost(every * (replicas - 1), part * held * LANES, 12 << 20),
         name="adam",
     )(
         rest, rest_other, grad, saved_rest, weight,
         moment_one.reshape(flat), moment_two.reshape(flat),
+    )
+    gate_home, new_one = lax.optimization_barrier((gate_home, new_one))
+    by_token = jnp.sum(gate_home.reshape(2 * blocks, planes, held * tokens), axis=1)
+    by_token = by_token.reshape(2 * blocks * held, tokens)
+    experts = lax.broadcasted_iota(jnp.int32, (2 * blocks * held, tokens, choices), 0)
+    grad_gates = jnp.sum(
+        jnp.where(experts == expert_ids[None], by_token[:, :, None], 0.0), axis=0
     )
     grad_hidden = jnp.transpose(
         grad_hidden.reshape(1, 2 * blocks, capacity, held, LANES), (0, 1, 3, 2, 4)

time: 146 us -> 145 us (level)
  starting transfers between devices: 20.8 us -> 76.8 us
  waiting for transfers between devices: 53.5 us -> 20.7 us
  blocking collectives: 30.6 us -> 0 us
  other arithmetic: 3.02 us -> 7.05 us
  Pallas kernels: 11.1 us -> 12.6 us
    ppermute x2 -> x14, starting transfers between devices: 12.5 us -> 52.8 us  [the longest x6 21 us: gathered(): up, down = (lax.ppermute(up, 'ey', ahead), lax.ppermute(down, 'ey', back))]
    all_gather x2 -> x1, waiting for transfers between devices: 37.2 us -> 0.01 us  [between(): held_back['rest'] = lax.all_gather(rest, 'ey', axis=0)]
    all_to_all x2 -> x0, blocking collectives: 30.6 us -> none  [the longest x1 19.4 us: shards(): lax.all_to_all(jnp.broadcast_to(gate_part[None], (planes,) + gate_part.sh...]
    all_to_all x1 -> x2, starting transfers between devices: 3.46 us -> 19.9 us  [the longest x1 15.8 us: shards(): lax.all_to_all(gate_send, ('ey', 'core', 'tensor'), 0, 0, tiled=True)]
    ppermute x2 -> x14, waiting for transfers between devices: 4.07 us -> 10.8 us  [the longest x6 5.29 us: gathered(): up, down = (lax.ppermute(up, 'ey', ahead), lax.ppermute(down, 'ey', back))]
    concatenate x2 -> x6, other arithmetic: 0.91 us -> 4.71 us  [the longest x4 2.78 us: gathered(): jnp.concatenate([up, down], axis=0)]
    unnamed x20 -> x18, local copies, waits for them, and re-layouts: 7.86 us -> 5.21 us
    all_to_all x1 -> x2, waiting for transfers between devices: 6.53 us -> 4.21 us  [the longest x1 4.21 us: shards(): lax.all_to_all(gate_send, ('ey', 'core', 'tensor'), 0, 0, tiled=True)]
  transfers between devices with their start and end apart: 6 -> 18, of which waited for: 5 -> 6; matrix products, arithmetic and copies ran while one was open for 4% -> 6% of each run, Pallas kernels for 3% -> 9%
where the time goes in v2:
time: 145 us; the launch traced here: 144 us
  starting transfers between devices  76.8 us (53%)
  waiting for transfers between devices  20.7 us (14%)
  between operations  14.3 us (10%)
  Pallas kernels  12.6 us (9%)
  local copies, waits for them, and re-layouts  12.3 us (8%)
  other arithmetic  7.05 us (5%)
    ppermute x6, starting transfers between devices, gathered(): up, down = (lax.ppermute(up, 'ey', ahead), lax.ppermute(down, 'ey', back))  21 us
    all_to_all x1, starting transfers between devices, shards(): lax.all_to_all(gate_send, ('ey', 'core', 'tensor'), 0, 0, tiled=True)  15.8 us
    ppermute x1, starting transfers between devices, gathered(): mine, theirs = ([own], [lax.ppermute(own, 'core', swap)])  12.2 us
    ppermute x4, starting transfers between devices, gathered(): lax.ppermute(jnp.concatenate([up, down], axis=0), 'core', swap)  11 us
    pallas_call x1, Pallas kernels, shards(): pl.pallas_call(functools.partial(adam_kernel, tokens, rows, part), out_sh...  7.26 us
    all_to_all x1, waiting for transfers between devices, shards(): from_replicas = lax.all_to_all(to_replicas, 'edata', 0, 0, tiled=True)  5.65 us
    pallas_call x1, Pallas kernels, shards(): pl.pallas_call(functools.partial(own_kernel, tokens, rows, width), out_sh...  5.32 us
    ppermute x6, waiting for transfers between devices, gathered(): up, down = (lax.ppermute(up, 'ey', ahead), lax.ppermute(down, 'ey', back))  5.29 us
  transfers between devices with their start and end apart: 18, of which 6 were waited for; matrix products, arithmetic and copies ran while one was open for 6% of the time, Pallas kernels for 9%

profile of v2, /device:TPU:1, one launch (start us, length us, event | category | flops | bytes accessed | tf_op | source)
XLA Modules:
  0.0 143.7 jit_solution(18290633314697119901)
XLA Ops:
  7.2 0.8 copy.36
  7.9 0.8 copy.37
  8.7 1.0 concatenate.39.refs_0_
  9.8 4.2 %collective-permute-start = (bf16[32,4224]{1,0:T(8,128)(2,1)S(1)}, bf16[32,4224]{1,0:T(8,128)(2,1)S(1)}, u32[]{:S(2)}, u32[]{:S(2)}) collective-permute-start(bf16[32,4224]{1,0:T(8,128)(2,1)S(1)} %concatenate.39.refs_0_), channel_id=1, source_target_pairs={{0,24},{24,48},{48,72},{72,96},{96,120},{120,144},{144,168},{168,0... | collective-permute-start | bytes 811016 | tf_op jit(solution)/shard_map/ppermute | solution.py:169
  13.9 3.8 %collective-permute-start.1 = (bf16[32,4224]{1,0:T(8,128)(2,1)S(1)}, bf16[32,4224]{1,0:T(8,128)(2,1)S(1)}, u32[]{:S(2)}, u32[]{:S(2)}) collective-permute-start(bf16[32,4224]{1,0:T(8,128)(2,1)S(1)} %concatenate.39.refs_0_), channel_id=1, source_target_pairs={{0,168},{24,0},{48,24},{72,48},{96,72},{120,96},{144,120},{168,144... | collective-permute-start | bytes 811016 | tf_op jit(solution)/shard_map/ppermute | solution.py:169
  17.8 1.0 fusion.3
  18.7 0.1 concatenate.43
  18.8 0.1 concatenate.40
  18.9 0.1 concatenate.41
  19.0 0.1 concatenate.42
  19.1 0.8 pad_maximum_fusion.3
  19.9 4.0 %all-to-all-start = ((bf16[4,32,1152]{2,1,0:T(8,128)(2,1)}), bf16[4,32,1152]{2,1,0:T(8,128)(2,1)S(1)}, u32[]{:S(2)}, u32[]{:S(2)}) async-start(bf16[4,32,1152]{2,1,0:T(8,128)(2,1)} %pad_maximum_fusion.3), calls=%async_computation | async-start | bytes 589824 | tf_op jit(solution)/shard_map/all_to_all | solution.py:197
  23.9 0.0 all-gather.2.cloned.1.call-start
  23.9 5.6 %all-to-all-done = bf16[4,32,1152]{2,1,0:T(8,128)(2,1)S(1)} async-done(((bf16[4,32,1152]{2,1,0:T(8,128)(2,1)}), bf16[4,32,1152]{2,1,0:T(8,128)(2,1)S(1)}, u32[]{:S(2)}, u32[]{:S(2)}) %all-to-all-start) | async-done | bytes 294944 | tf_op jit(solution)/shard_map/all_to_all | solution.py:197
  29.6 0.0 collective-permute-done.refs_1_
  29.6 0.0 collective-permute-done.1.refs_2_
  29.6 0.8 broadcast_in_dim.34
  30.4 0.8 fusion.1
  31.2 0.0 all-gather.2.cloned.1.call-update
  31.2 12.2 %collective-permute-start.8 = (bf16[32,4224]{1,0:T(8,128)(2,1)S(1)}, bf16[32,4224]{1,0:T(8,128)(2,1)}, u32[]{:S(2)}, u32[]{:S(2)}) collective-permute-start(bf16[32,4224]{1,0:T(8,128)(2,1)S(1)} %concatenate.39.refs_0_), channel_id=1, source_target_pairs={{0,12},{12,0},{1,13},{13,1},{2,14},{14,2},{3,15},{15,3},{4,16},{16... | collective-permute-start | bytes 811016 | tf_op jit(solution)/shard_map/ppermute | solution.py:166
  43.4 1.9 %collective-permute-start.2 = (bf16[32,4224]{1,0:T(8,128)(2,1)S(1)}, bf16[32,4224]{1,0:T(8,128)(2,1)}, u32[]{:S(2)}, u32[]{:S(2)}) collective-permute-start(bf16[32,4224]{1,0:T(8,128)(2,1)S(1)} %collective-permute-done.refs_1_), channel_id=1, source_target_pairs={{0,24},{24,48},{48,72},{72,96},{96,120},{120,144},{144,168},{168,0... | collective-permute-start | bytes 811016 | tf_op jit(solution)/shard_map/ppermute | solution.py:169
  45.4 4.6 %collective-permute-start.3 = (bf16[32,4224]{1,0:T(8,128)(2,1)S(1)}, bf16[32,4224]{1,0:T(8,128)(2,1)}, u32[]{:S(2)}, u32[]{:S(2)}) collective-permute-start(bf16[32,4224]{1,0:T(8,128)(2,1)S(1)} %collective-permute-done.1.refs_2_), channel_id=1, source_target_pairs={{0,168},{24,0},{48,24},{72,48},{96,72},{120,96},{144,120},{168,144... | collective-permute-start | bytes 811016 | tf_op jit(solution)/shard_map/ppermute | solution.py:169
  49.9 0.8 pad_maximum_fusion
  50.8 4.1 %all-to-all-start.1 = ((bf16[4,384,128]{2,1,0:T(8,128)(2,1)}), bf16[4,384,128]{2,1,0:T(8,128)(2,1)}, u32[]{:S(2)}, u32[]{:S(2)}) async-start(bf16[4,384,128]{2,1,0:T(8,128)(2,1)} %broadcast_in_dim.34), calls=%async_computation.1 | async-start | bytes 786432 | tf_op jit(solution)/shard_map/all_to_all | solution.py:214
  54.9 2.5 %collective-permute-start.9 = (bf16[64,4224]{1,0:T(8,128)(2,1)}, bf16[64,4224]{1,0:T(8,128)(2,1)}, u32[]{:S(2)}, u32[]{:S(2)}) collective-permute-start(bf16[64,4224]{1,0:T(8,128)(2,1)} %pad_maximum_fusion), channel_id=1, source_target_pairs={{0,12},{12,0},{1,13},{13,1},{2,14},{14,2},{3,15},{15,3},{4,16},{16... | collective-permute-start | bytes 1622024 | tf_op jit(solution)/shard_map/ppermute | solution.py:172
  57.4 0.0 collective-permute-done.2.refs_3_
  57.4 1.9 %collective-permute-start.4 = (bf16[32,4224]{1,0:T(8,128)(2,1)}, bf16[32,4224]{1,0:T(8,128)(2,1)S(1)}, u32[]{:S(2)}, u32[]{:S(2)}) collective-permute-start(bf16[32,4224]{1,0:T(8,128)(2,1)} %collective-permute-done.2.refs_3_), channel_id=1, source_target_pairs={{0,24},{24,48},{48,72},{72,96},{96,120},{120,144},{144,168},{168,0... | collective-permute-start | bytes 811016 | tf_op jit(solution)/shard_map/ppermute | solution.py:169
  59.3 0.0 collective-permute-done.3.refs_4_
  59.3 4.6 %collective-permute-start.5 = (bf16[32,4224]{1,0:T(8,128)(2,1)}, bf16[32,4224]{1,0:T(8,128)(2,1)S(1)}, u32[]{:S(2)}, u32[]{:S(2)}) collective-permute-start(bf16[32,4224]{1,0:T(8,128)(2,1)} %collective-permute-done.3.refs_4_), channel_id=1, source_target_pairs={{0,168},{24,0},{48,24},{72,48},{96,72},{120,96},{144,120},{168,144... | collective-permute-start | bytes 811016 | tf_op jit(solution)/shard_map/ppermute | solution.py:169
  63.9 1.9 %pad_maximum_fusion.1 = bf16[64,4224]{1,0:T(8,128)(2,1)} fusion(bf16[32,4224]{1,0:T(8,128)(2,1)} %collective-permute-done.3.refs_4_, bf16[32,4224]{1,0:T(8,128)(2,1)} %collective-permute-done.2.refs_3_), kind=kLoop, calls=%fused_computation.3 | loop fusion | flops 1081344 | bytes 1081344 | tf_op jit(solution)/shard_map/concatenate | solution.py:172
  65.8 2.6 %collective-permute-start.10 = (bf16[64,4224]{1,0:T(8,128)(2,1)}, bf16[64,4224]{1,0:T(8,128)(2,1)}, u32[]{:S(2)}, u32[]{:S(2)}) collective-permute-start(bf16[64,4224]{1,0:T(8,128)(2,1)} %pad_maximum_fusion.1), channel_id=1, source_target_pairs={{0,12},{12,0},{1,13},{13,1},{2,14},{14,2},{3,15},{15,3},{4,16},{16... | collective-permute-start | bytes 1622024 | tf_op jit(solution)/shard_map/ppermute | solution.py:172
  68.4 0.0 all-to-all-done.1
  68.4 4.9 %collective-permute-done.4.refs_5_ = bf16[32,4224]{1,0:T(8,128)(2,1)S(1)} collective-permute-done((bf16[32,4224]{1,0:T(8,128)(2,1)}, bf16[32,4224]{1,0:T(8,128)(2,1)S(1)}, u32[]{:S(2)}, u32[]{:S(2)}) %collective-permute-start.4) | collective-permute-done | bytes 270368 | tf_op jit(solution)/shard_map/ppermute | solution.py:169
  73.3 0.4 collective-permute-done.5.refs_6_
  73.7 1.9 %collective-permute-start.6 = (bf16[16,4224]{1,0:T(8,128)(2,1)S(1)}, bf16[16,4224]{1,0:T(8,128)(2,1)S(1)}, u32[]{:S(2)}, u32[]{:S(2)}) collective-permute-start(bf16[16,4224]{1,0:T(8,128)(2,1)S(1)} %slice.28), channel_id=1, source_target_pairs={{0,24},{24,48},{48,72},{72,96},{96,120},{120,144},{144,168},{168,0... | collective-permute-start | bytes 405512 | tf_op jit(solution)/shard_map/ppermute | solution.py:173
  75.7 4.6 %collective-permute-start.7 = (bf16[16,4224]{1,0:T(8,128)(2,1)S(1)}, bf16[16,4224]{1,0:T(8,128)(2,1)S(1)}, u32[]{:S(2)}, u32[]{:S(2)}) collective-permute-start(bf16[16,4224]{1,0:T(8,128)(2,1)S(1)} %slice.29), channel_id=1, source_target_pairs={{0,168},{24,0},{48,24},{72,48},{96,72},{120,96},{144,120},{168,144... | collective-permute-start | bytes 405512 | tf_op jit(solution)/shard_map/ppermute | solution.py:173
  80.3 4.0 %collective-permute-done.6.refs_7_ = bf16[16,4224]{1,0:T(8,128)(2,1)S(1)} collective-permute-done((bf16[16,4224]{1,0:T(8,128)(2,1)S(1)}, bf16[16,4224]{1,0:T(8,128)(2,1)S(1)}, u32[]{:S(2)}, u32[]{:S(2)}) %collective-permute-start.6) | collective-permute-done | bytes 135200 | tf_op jit(solution)/shard_map/ppermute | solution.py:173
  84.3 4.0 %collective-permute-start.11 = (bf16[64,4224]{1,0:T(8,128)(2,1)S(1)}, bf16[64,4224]{1,0:T(8,128)(2,1)S(1)}, u32[]{:S(2)}, u32[]{:S(2)}) collective-permute-start(bf16[64,4224]{1,0:T(8,128)(2,1)S(1)} %pad_maximum_fusion.2), channel_id=1, source_target_pairs={{0,12},{12,0},{1,13},{13,1},{2,14},{14,2},{3,15},{15,3},{4,16},{16... | collective-permute-start | bytes 1622024 | tf_op jit(solution)/shard_map/ppermute | solution.py:172
  88.3 0.0 collective-permute-done.7.refs_8_
  88.4 1.9 %collective-permute-start.12 = (bf16[32,4224]{1,0:T(8,128)(2,1)S(1)}, bf16[32,4224]{1,0:T(8,128)(2,1)S(1)}, u32[]{:S(2)}, u32[]{:S(2)}) collective-permute-start(bf16[32,4224]{1,0:T(8,128)(2,1)S(1)} %pad_maximum_fusion.4), channel_id=1, source_target_pairs={{0,12},{12,0},{1,13},{13,1},{2,14},{14,2},{3,15},{15,3},{4,16},{16... | collective-permute-start | bytes 811016 | tf_op jit(solution)/shard_map/ppermute | solution.py:175
  90.3 0.0 collective-permute-done.8.refs_9_
  90.3 0.0 collective-permute-done.9.refs_10_
  90.3 0.0 collective-permute-done.10.refs_11_
  90.3 1.5 %collective-permute-done.12.refs_13_ = bf16[32,4224]{1,0:T(8,128)(2,1)S(1)} collective-permute-done((bf16[32,4224]{1,0:T(8,128)(2,1)S(1)}, bf16[32,4224]{1,0:T(8,128)(2,1)S(1)}, u32[]{:S(2)}, u32[]{:S(2)}) %collective-permute-start.12) | collective-permute-done | bytes 270368 | tf_op jit(solution)/shard_map/ppermute | solution.py:175
  91.8 0.0 collective-permute-done.11.refs_12_
  91.8 5.3 %own_tokens.1 = (bf16[8,2,24,128]{3,2,1,0:T(8,128)(2,1)}, f32[8,128]{1,0:T(8,128)S(1)}, f32[1024,256]{1,0:T(8,128)S(1)}) custom-call(bf16[32,4224]{1,0:T(8,128)(2,1)S(1)} %concatenate.39.refs_0_, bf16[32,4224]{1,0:T(8,128)(2,1)S(1)} %collective-permute-done.refs_1_, bf16[32,4224]{1,0:T(8,128)(2,1)S(1)} %collective-permute-done.1.refs_2_, ...), custom_call_target="tpu_custom_call" | custom-call | flops 1342177280 | bytes 8388608 | tf_op jit(solution)/shard_map/own_tokens/pallas_call | solution.py:223
  97.1 1.0 copy-done.3
  98.1 2.2 %collective-permute-start.13 = (bf16[8,96,1152]{2,1,0:T(8,128)(2,1)}, bf16[8,96,1152]{2,1,0:T(8,128)(2,1)}, u32[]{:S(2)}, u32[]{:S(2)}) collective-permute-start(bf16[8,96,1152]{2,1,0:T(8,128)(2,1)} %all-gather.2.cloned.1.call-done.mine), channel_id=1, source_target_pairs={{0,12},{12,0},{1,13},{13,1},{2,14},{14,2},{3,15},{15,3},{4,16},{16... | collective-permute-start | bytes 5308424 | tf_op jit(solution)/shard_map/ppermute | solution.py:237
  100.3 1.0 slice.31
  101.3 0.1 broadcast_in_dim.35
  101.3 0.7 broadcast_in_dim.36
  102.0 1.5 %reshape.48 = f32[192,1,64]{2,0,1:T(8,128)} reshape(f32[16,12,64]{2,1,0:T(8,128)} %broadcast_in_dim.36) | data formatting | bytes 98304 | tf_op jit(solution)/shard_map/reshape | solution.py:240
  103.5 15.8 %all-to-all-start.2 = ((f32[192,1,64]{2,1,0:T(1,128)}), f32[192,1,64]{2,1,0:T(1,128)S(1)}, u32[]{:S(2)}, u32[]{:S(2)}) async-start(f32[192,1,64]{2,1,0:T(1,128)} %bitcast.31), calls=%async_computation.2 | async-start | bytes 196608 | tf_op jit(solution)/shard_map/all_to_all | solution.py:241
  119.4 0.0 copy-start.5
  119.4 1.1 fusion.hid
  120.5 0.0 collective-permute-done.13.theirs
  120.6 1.5 %copy-done.1 = bf16[8,96,1152]{2,1,0:T(8,128)(2,1)S(1)} copy-done((bf16[8,96,1152]{2,1,0:T(8,128)(2,1)S(1)}, bf16[8,96,1152]{2,1,0:T(8,128)(2,1)}, u32[]{:S(2)}) %copy-start.1) | copy-done | bytes 1769496
  122.0 1.2 copy-done.4
  123.3 7.3 %adam.1 = (bf16[2048,128]{1,0:T(8,128)(2,1)}, bf16[2048,128]{1,0:T(8,128)(2,1)}, f32[2048,128]{1,0:T(8,128)}) custom-call(bf16[8,96,1152]{2,1,0:T(8,128)(2,1)S(1)} %copy-done.1, bf16[8,96,1152]{2,1,0:T(8,128)(2,1)} %collective-permute-done.13.theirs, f32[1024,256]{1,0:T(8,128)S(1)} %copy-done.4, bf16[3,384,128]{2,1,0:T(8,128)(2,1)S(1)} %fusion.hid, ...), custom_call_target="tpu_custom_call" | custom-call | flops 805306368 | bytes 12582912 | tf_op jit(solution)/shard_map/adam/pallas_call | solution.py:243
  130.5 4.2 %all-to-all-done.2 = f32[192,1,64]{2,1,0:T(1,128)S(1)} async-done(((f32[192,1,64]{2,1,0:T(1,128)}), f32[192,1,64]{2,1,0:T(1,128)S(1)}, u32[]{:S(2)}, u32[]{:S(2)}) %all-to-all-start.2) | async-done | bytes 49184 | tf_op jit(solution)/shard_map/all_to_all | solution.py:241
  134.7 0.5 broadcast.4
  135.2 0.9 reduce.3
  136.2 0.1 broadcast_in_dim.37
  136.2 0.6 select_reduce_fusion
  (24 shorter events, 0.2 us)
Async XLA Ops:
  9.8 14.1 %copy-start.6 = (bf16[1,16,2,12,128]{4,2,3,1,0:T(2,128)(2,1)S(1)}, bf16[1,16,2,12,128]{4,2,3,1,0:T(2,128)(2,1)}, u32[]{:S(2)}) copy-start(bf16[1,16,2,12,128]{4,2,3,1,0:T(2,128)(2,1)} %param.10) | copy-start | bytes 294916
  9.8 19.8 %collective-permute-start = (bf16[32,4224]{1,0:T(8,128)(2,1)S(1)}, bf16[32,4224]{1,0:T(8,128)(2,1)S(1)}, u32[]{:S(2)}, u32[]{:S(2)}) collective-permute-start(bf16[32,4224]{1,0:T(8,128)(2,1)S(1)} %concatenate.39.refs_0_), channel_id=1, source_target_pairs={{0,24},{24,48},{48,72},{72,96},{96,120},{120,144},{144,168},{168,0... | collective-permute-start | bytes 811016 | tf_op jit(solution)/shard_map/ppermute | solution.py:169
  13.9 15.7 %collective-permute-start.1 = (bf16[32,4224]{1,0:T(8,128)(2,1)S(1)}, bf16[32,4224]{1,0:T(8,128)(2,1)S(1)}, u32[]{:S(2)}, u32[]{:S(2)}) collective-permute-start(bf16[32,4224]{1,0:T(8,128)(2,1)S(1)} %concatenate.39.refs_0_), channel_id=1, source_target_pairs={{0,168},{24,0},{48,24},{72,48},{96,72},{120,96},{144,120},{168,144... | collective-permute-start | bytes 811016 | tf_op jit(solution)/shard_map/ppermute | solution.py:169
  19.9 9.7 %all-to-all-start = ((bf16[4,32,1152]{2,1,0:T(8,128)(2,1)}), bf16[4,32,1152]{2,1,0:T(8,128)(2,1)S(1)}, u32[]{:S(2)}, u32[]{:S(2)}) async-start(bf16[4,32,1152]{2,1,0:T(8,128)(2,1)} %pad_maximum_fusion.3), calls=%async_computation | async-start | bytes 589824 | tf_op jit(solution)/shard_map/all_to_all | solution.py:197
  23.9 74.2 %all-gather.2.cloned.1.call-start = ((), (), s32[]{:S(2)}) async-start(), calls=%async_computation.3 | async-start | bytes 1990656 | tf_op jit(solution)/shard_map/all_gather | solution.py:213
  31.2 59.1 %collective-permute-start.8 = (bf16[32,4224]{1,0:T(8,128)(2,1)S(1)}, bf16[32,4224]{1,0:T(8,128)(2,1)}, u32[]{:S(2)}, u32[]{:S(2)}) collective-permute-start(bf16[32,4224]{1,0:T(8,128)(2,1)S(1)} %concatenate.39.refs_0_), channel_id=1, source_target_pairs={{0,12},{12,0},{1,13},{13,1},{2,14},{14,2},{3,15},{15,3},{4,16},{16... | collective-permute-start | bytes 811016 | tf_op jit(solution)/shard_map/ppermute | solution.py:166
  43.4 14.0 %collective-permute-start.2 = (bf16[32,4224]{1,0:T(8,128)(2,1)S(1)}, bf16[32,4224]{1,0:T(8,128)(2,1)}, u32[]{:S(2)}, u32[]{:S(2)}) collective-permute-start(bf16[32,4224]{1,0:T(8,128)(2,1)S(1)} %collective-permute-done.refs_1_), channel_id=1, source_target_pairs={{0,24},{24,48},{48,72},{72,96},{96,120},{120,144},{144,168},{168,0... | collective-permute-start | bytes 811016 | tf_op jit(solution)/shard_map/ppermute | solution.py:169
  45.4 14.0 %collective-permute-start.3 = (bf16[32,4224]{1,0:T(8,128)(2,1)S(1)}, bf16[32,4224]{1,0:T(8,128)(2,1)}, u32[]{:S(2)}, u32[]{:S(2)}) collective-permute-start(bf16[32,4224]{1,0:T(8,128)(2,1)S(1)} %collective-permute-done.1.refs_2_), channel_id=1, source_target_pairs={{0,168},{24,0},{48,24},{72,48},{96,72},{120,96},{144,120},{168,144... | collective-permute-start | bytes 811016 | tf_op jit(solution)/shard_map/ppermute | solution.py:169
  50.8 17.6 %all-to-all-start.1 = ((bf16[4,384,128]{2,1,0:T(8,128)(2,1)}), bf16[4,384,128]{2,1,0:T(8,128)(2,1)}, u32[]{:S(2)}, u32[]{:S(2)}) async-start(bf16[4,384,128]{2,1,0:T(8,128)(2,1)} %broadcast_in_dim.34), calls=%async_computation.1 | async-start | bytes 786432 | tf_op jit(solution)/shard_map/all_to_all | solution.py:214
  54.9 35.4 %collective-permute-start.9 = (bf16[64,4224]{1,0:T(8,128)(2,1)}, bf16[64,4224]{1,0:T(8,128)(2,1)}, u32[]{:S(2)}, u32[]{:S(2)}) collective-permute-start(bf16[64,4224]{1,0:T(8,128)(2,1)} %pad_maximum_fusion), channel_id=1, source_target_pairs={{0,12},{12,0},{1,13},{13,1},{2,14},{14,2},{3,15},{15,3},{4,16},{16... | collective-permute-start | bytes 1622024 | tf_op jit(solution)/shard_map/ppermute | solution.py:172
  57.4 15.9 %collective-permute-start.4 = (bf16[32,4224]{1,0:T(8,128)(2,1)}, bf16[32,4224]{1,0:T(8,128)(2,1)S(1)}, u32[]{:S(2)}, u32[]{:S(2)}) collective-permute-start(bf16[32,4224]{1,0:T(8,128)(2,1)} %collective-permute-done.2.refs_3_), channel_id=1, source_target_pairs={{0,24},{24,48},{48,72},{72,96},{96,120},{120,144},{144,168},{168,0... | collective-permute-start | bytes 811016 | tf_op jit(solution)/shard_map/ppermute | solution.py:169
  59.3 14.4 %collective-permute-start.5 = (bf16[32,4224]{1,0:T(8,128)(2,1)}, bf16[32,4224]{1,0:T(8,128)(2,1)S(1)}, u32[]{:S(2)}, u32[]{:S(2)}) collective-permute-start(bf16[32,4224]{1,0:T(8,128)(2,1)} %collective-permute-done.3.refs_4_), channel_id=1, source_target_pairs={{0,168},{24,0},{48,24},{72,48},{96,72},{120,96},{144,120},{168,144... | collective-permute-start | bytes 811016 | tf_op jit(solution)/shard_map/ppermute | solution.py:169
  65.8 26.0 %copy-start = (bf16[2,128,4096]{2,1,0:T(8,128)(2,1)S(1)}, bf16[2,128,4096]{2,1,0:T(8,128)(2,1)}, u32[]{:S(2)}) copy-start(bf16[2,128,4096]{2,1,0:T(8,128)(2,1)} %param.11) | copy-start | bytes 6291460
  65.8 24.5 %collective-permute-start.10 = (bf16[64,4224]{1,0:T(8,128)(2,1)}, bf16[64,4224]{1,0:T(8,128)(2,1)}, u32[]{:S(2)}, u32[]{:S(2)}) collective-permute-start(bf16[64,4224]{1,0:T(8,128)(2,1)} %pad_maximum_fusion.1), channel_id=1, source_target_pairs={{0,12},{12,0},{1,13},{13,1},{2,14},{14,2},{3,15},{15,3},{4,16},{16... | collective-permute-start | bytes 1622024 | tf_op jit(solution)/shard_map/ppermute | solution.py:172
  73.7 10.6 %collective-permute-start.6 = (bf16[16,4224]{1,0:T(8,128)(2,1)S(1)}, bf16[16,4224]{1,0:T(8,128)(2,1)S(1)}, u32[]{:S(2)}, u32[]{:S(2)}) collective-permute-start(bf16[16,4224]{1,0:T(8,128)(2,1)S(1)} %slice.28), channel_id=1, source_target_pairs={{0,24},{24,48},{48,72},{72,96},{96,120},{120,144},{144,168},{168,0... | collective-permute-start | bytes 405512 | tf_op jit(solution)/shard_map/ppermute | solution.py:173
  75.7 12.7 %collective-permute-start.7 = (bf16[16,4224]{1,0:T(8,128)(2,1)S(1)}, bf16[16,4224]{1,0:T(8,128)(2,1)S(1)}, u32[]{:S(2)}, u32[]{:S(2)}) collective-permute-start(bf16[16,4224]{1,0:T(8,128)(2,1)S(1)} %slice.29), channel_id=1, source_target_pairs={{0,168},{24,0},{48,24},{72,48},{96,72},{120,96},{144,120},{168,144... | collective-permute-start | bytes 405512 | tf_op jit(solution)/shard_map/ppermute | solution.py:173
  84.3 7.5 %collective-permute-start.11 = (bf16[64,4224]{1,0:T(8,128)(2,1)S(1)}, bf16[64,4224]{1,0:T(8,128)(2,1)S(1)}, u32[]{:S(2)}, u32[]{:S(2)}) collective-permute-start(bf16[64,4224]{1,0:T(8,128)(2,1)S(1)} %pad_maximum_fusion.2), channel_id=1, source_target_pairs={{0,12},{12,0},{1,13},{13,1},{2,14},{14,2},{3,15},{15,3},{4,16},{16... | collective-permute-start | bytes 1622024 | tf_op jit(solution)/shard_map/ppermute | solution.py:172
  88.4 3.4 %collective-permute-start.12 = (bf16[32,4224]{1,0:T(8,128)(2,1)S(1)}, bf16[32,4224]{1,0:T(8,128)(2,1)S(1)}, u32[]{:S(2)}, u32[]{:S(2)}) collective-permute-start(bf16[32,4224]{1,0:T(8,128)(2,1)S(1)} %pad_maximum_fusion.4), channel_id=1, source_target_pairs={{0,12},{12,0},{1,13},{13,1},{2,14},{14,2},{3,15},{15,3},{4,16},{16... | collective-permute-start | bytes 811016 | tf_op jit(solution)/shard_map/ppermute | solution.py:175
  97.1 1.0 copy-start.3
  98.1 22.4 %copy-start.2 = (f32[1024,2,128]{2,1,0:T(2,128)S(1)}, f32[1024,2,128]{2,1,0:T(2,128)}, u32[]{:S(2)}) copy-start(f32[1024,2,128]{2,1,0:T(2,128)} %param.13) | copy-start | bytes 3145732
  98.1 22.4 %collective-permute-start.13 = (bf16[8,96,1152]{2,1,0:T(8,128)(2,1)}, bf16[8,96,1152]{2,1,0:T(8,128)(2,1)}, u32[]{:S(2)}, u32[]{:S(2)}) collective-permute-start(bf16[8,96,1152]{2,1,0:T(8,128)(2,1)} %all-gather.2.cloned.1.call-done.mine), channel_id=1, source_target_pairs={{0,12},{12,0},{1,13},{13,1},{2,14},{14,2},{3,15},{15,3},{4,16},{16... | collective-permute-start | bytes 5308424 | tf_op jit(solution)/shard_map/ppermute | solution.py:237
  103.5 31.2 %all-to-all-start.2 = ((f32[192,1,64]{2,1,0:T(1,128)}), f32[192,1,64]{2,1,0:T(1,128)S(1)}, u32[]{:S(2)}, u32[]{:S(2)}) async-start(f32[192,1,64]{2,1,0:T(1,128)} %bitcast.31), calls=%async_computation.2 | async-start | bytes 196608 | tf_op jit(solution)/shard_map/all_to_all | solution.py:241
  119.4 1.2 copy-start.5
  120.5 1.5 %copy-start.1 = (bf16[8,96,1152]{2,1,0:T(8,128)(2,1)S(1)}, bf16[8,96,1152]{2,1,0:T(8,128)(2,1)}, u32[]{:S(2)}) copy-start(bf16[8,96,1152]{2,1,0:T(8,128)(2,1)} %all-gather.2.cloned.1.call-done.mine) | copy-start | bytes 5308420
  122.0 1.2 copy-start.4
  123.2 13.0 %copy-start.7 = (s32[32,8]{0,1:T(8,128)S(1)}, s32[32,8]{0,1:T(8,128)}, u32[]{:S(2)}) copy-start(s32[32,8]{0,1:T(8,128)} %param.9) | copy-start | bytes 3076
Sparse Core Ops, SparseCore 0:
  31.4 54.3 all-gather.1

commit v3 on v1

v3 whole, which is shorter than its diff:
```python
import functools

import jax
import jax.numpy as jnp
from jax import lax
from jax.experimental import pallas as pl
from jax.experimental.pallas import tpu as pltpu
from jax.sharding import Mesh, PartitionSpec as P

beta_one = 0.9
beta_two = 0.999
adam_eps = 1e-08
learn_rate = 0.01
corr_two = 0.6323045752

F32 = jnp.float32
BF16 = jnp.bfloat16
LANES = 128
PARAMS = pltpu.CompilerParams(vmem_limit_bytes=40 * 1024 * 1024)


def dot(a, b, over, precision=None):
    return lax.dot_general(
        a, b, (((over[0],), (over[1],)), ((), ())), precision=precision, preferred_element_type=F32
    )


def expert_base():
    return ((lax.axis_index("ey") * 2 + lax.axis_index("core")) * 2).astype(F32)


def routed(meta, base, tokens, rows):
    count = meta.shape[0]
    meta = meta.astype(F32)
    ids, gates = meta[:, :8], meta[:, 8:16]
    hits = [ids == base + e for e in range(2)]
    named = [jnp.sum(jnp.where(h, 1.0, 0.0), axis=1, keepdims=True) for h in hits]
    gate = [jnp.sum(jnp.where(h, gates, 0.0), axis=1, keepdims=True) for h in hits]
    lane = lax.broadcasted_iota(jnp.int32, (count, LANES), 1)
    marks = jnp.where(lane == 0, named[0], jnp.where(lane == 1, named[1], 0.0)).astype(BF16)
    row_i = lax.broadcasted_iota(jnp.int32, (count, count), 0)
    col_i = lax.broadcasted_iota(jnp.int32, (count, count), 1)
    earlier = ((row_i // tokens == col_i // tokens) & (col_i < row_i)).astype(F32).astype(BF16)
    rank = dot(earlier, marks, (1, 0))
    block = (lax.broadcasted_iota(jnp.int32, (count, 1), 0) // tokens).astype(F32)
    slot_rows = (count // tokens) * rows
    slot_lane = lax.broadcasted_iota(jnp.int32, (count, slot_rows), 1).astype(F32)
    keys = [
        jnp.where(named[e] > 0.5, block * rows + 2.0 * rank[:, e : e + 1] + e, -1.0)
        for e in range(2)
    ]
    onehot = ((slot_lane == keys[0]) | (slot_lane == keys[1])).astype(F32).astype(BF16)
    return onehot, gate


def by_expert(hid):
    odd = lax.broadcasted_iota(jnp.int32, hid.shape, 0) % 2
    hid = hid.astype(F32)
    return jnp.concatenate(
        [jnp.where(odd == 0, hid, 0.0), jnp.where(odd == 1, hid, 0.0)], axis=1
    ).astype(BF16)


def gate_lanes(gate):
    return jnp.concatenate([jnp.broadcast_to(g, (g.shape[0], LANES)) for g in gate], axis=1)


def own_kernel(
    tokens, rows, planes, toks, meta, weight, hid, grad_hidden, gate_part, grad, up, saved, scaled
):
    step = pl.program_id(0)
    groups = hid.shape[0] // rows
    halves = 2
    count = groups // halves * tokens
    slots = groups // halves * rows
    base = expert_base()

    def matrix(half):
        here = slice(half * count, (half + 1) * count)
        return here, *routed(meta[here, :], base, tokens, rows)

    @pl.when(step == 0)
    def _():
        for half in range(halves):
            here, onehot, gate = matrix(half)
            slot_rows = hid[half * slots : (half + 1) * slots, :]
            mine = dot(onehot, by_expert(slot_rows), (1, 0))
            saved[here, :] = mine
            scaled[here, :] = (gate_lanes(gate) * mine).astype(BF16)
        up[...] = jnp.zeros_like(up)

    up[...] += dot(toks[...], weight[...], (1, 1))
    grad[...] = dot(toks[...], scaled[...], (0, 0)).astype(BF16)

    @pl.when(step == pl.num_programs(0) - 1)
    def _():
        rows_out = None
        for half in range(halves):
            here, onehot, gate = matrix(half)
            upstream = up[here, :]
            picked = dot(onehot, (gate_lanes(gate) * upstream).astype(BF16), (0, 0))
            even = lax.broadcasted_iota(jnp.int32, (slots, LANES), 0) % 2 == 0
            picked = jnp.where(even, picked[:, :LANES], picked[:, LANES:])
            grad_hidden[half * slots : (half + 1) * slots, :] = picked.astype(BF16)
            prod = saved[here, :] * upstream
            lane = lax.broadcasted_iota(jnp.int32, (count, LANES), 1)
            tok = lax.broadcasted_iota(jnp.int32, (count, LANES), 0) % tokens
            spread = jnp.zeros((count, LANES), F32)
            for e in range(2):
                total = jnp.sum(prod[:, e * LANES : (e + 1) * LANES], axis=1, keepdims=True)
                spread = jnp.where(lane == e * tokens + tok, total, spread)
            block_of = lax.broadcasted_iota(jnp.int32, (groups, count), 1) // tokens
            row = lax.broadcasted_iota(jnp.int32, (groups, count), 0)
            pick = (block_of + half * (groups // halves) == row).astype(F32)
            piece = dot(pick, spread, (1, 0), lax.Precision.HIGHEST)
            rows_out = piece if rows_out is None else rows_out + piece
        for group in range(groups):
            line = rows_out[group : group + 1, : 2 * tokens]
            for plane in range(planes):
                gate_part[group * planes + plane] = line


def home_kernel(tokens, planes, arrived, ids, out):
    groups = arrived.shape[0] // planes
    total = jnp.zeros(ids.shape, F32)
    named = ids[...]
    for group in range(groups):
        line = arrived[group * planes]
        for plane in range(1, planes):
            line = line + arrived[group * planes + plane]
        for e in range(2):
            value = line[:, e * tokens : (e + 1) * tokens]
            total = jnp.where(named == group * 2 + e, value, total)
    out[...] = total


def adam_kernel(part, grad, weight, one, two, new_weight, new_one, new_two, grad_rows, weight_rows):
    total = grad[...].astype(F32)
    column = pl.multiple_of(lax.axis_index("edata") * part, LANES)
    for e in range(2):
        grad_rows[pl.ds(e, part, 2), :] = total[:, e * LANES : (e + 1) * LANES]
        piece = weight[e * LANES : (e + 1) * LANES, pl.ds(column, part)].astype(F32)
        weight_rows[pl.ds(e, part, 2), :] = piece.T
    g = grad_rows[...]
    first = beta_one * one[...].astype(F32) + (1.0 - beta_one) * g
    second = beta_two * two[...] + (1.0 - beta_two) * g * g
    update = first / (jnp.sqrt(second / corr_two) + adam_eps)
    new_weight[...] = (weight_rows[...] - learn_rate * update).astype(BF16)
    new_one[...] = first.astype(BF16)
    new_two[...] = second


def cost(tokens, terms, moved):
    return pl.CostEstimate(flops=2 * tokens * terms, bytes_accessed=moved, transcendentals=0)


def shards(grad_out, gates, expert_ids, hidden, down_weight, moment_one, moment_two):
    tokens, width = grad_out.shape
    choices = gates.shape[1]
    replicas, planes = lax.axis_size("edata"), lax.axis_size("tensor")
    groups = lax.axis_size("ey") * 2
    held, capacity = hidden.shape[2], hidden.shape[3]
    rows = held * capacity
    part = width // replicas
    every = groups * tokens

    meta = jnp.concatenate(
        [expert_ids.astype(BF16), gates, jnp.zeros((tokens, LANES - 2 * choices), BF16)], axis=1
    )
    toks = lax.all_gather(
        jnp.concatenate([grad_out, meta], axis=1), ("ey", "core"), axis=0, tiled=True
    )
    saved = jnp.transpose(hidden[0], (0, 2, 1, 3)).reshape(groups * rows, LANES)
    weight = down_weight.reshape(held * LANES, width)
    whole = pl.BlockSpec((groups * rows, LANES), lambda d: (0, 0))
    grad_hidden, gate_part, grad = pl.pallas_call(
        functools.partial(own_kernel, tokens, rows, planes),
        grid=(replicas,),
        in_specs=[
            pl.BlockSpec((every, part), lambda d: (0, d)),
            pl.BlockSpec((every, LANES), lambda d: (0, width // LANES)),
            pl.BlockSpec((held * LANES, part), lambda d: (0, d)),
            whole,
        ],
        out_specs=(
            whole,
            pl.BlockSpec((groups * planes, 1, held * tokens), lambda d: (0, 0, 0)),
            pl.BlockSpec((part, held * LANES), lambda d: (d, 0)),
        ),
        out_shape=(
            jax.ShapeDtypeStruct((groups * rows, LANES), BF16),
            jax.ShapeDtypeStruct((groups * planes, 1, held * tokens), F32),
            jax.ShapeDtypeStruct((width, held * LANES), BF16),
        ),
        scratch_shapes=[
            pltpu.VMEM((every, held * LANES), F32),
            pltpu.VMEM((every, held * LANES), F32),
            pltpu.VMEM((every, held * LANES), BF16),
        ],
        compiler_params=PARAMS,
        cost_estimate=cost(every, 2 * width * held * LANES, 8 << 20),
        name="own_tokens",
    )(toks, toks, weight, saved)

    grad = lax.psum_scatter(grad, "edata", scatter_dimension=0, tiled=True)
    gate_home = lax.all_to_all(gate_part, ("ey", "core", "tensor"), 0, 0, tiled=True)
    grad_gates = pl.pallas_call(
        functools.partial(home_kernel, tokens, planes),
        out_shape=jax.ShapeDtypeStruct((choices, tokens), F32),
        compiler_params=PARAMS,
        name="gates_home",
    )(gate_home, expert_ids.T).T

    flat = (part * held, LANES)
    new_weight, new_one, new_two = pl.pallas_call(
        functools.partial(adam_kernel, part),
        out_shape=(
            jax.ShapeDtypeStruct(flat, BF16),
            jax.ShapeDtypeStruct(flat, BF16),
            jax.ShapeDtypeStruct(flat, F32),
        ),
        scratch_shapes=[pltpu.VMEM(flat, F32), pltpu.VMEM(flat, F32)],
        compiler_params=PARAMS,
        cost_estimate=cost(part, held * LANES, 8 << 20),
        name="adam",
    )(grad, weight, moment_one.reshape(flat), moment_two.reshape(flat))
    grad_hidden = jnp.transpose(
        grad_hidden.reshape(1, groups, capacity, held, LANES), (0, 1, 3, 2, 4)
    )
    shape = moment_one.shape
    return (
        grad_hidden, grad_gates, new_weight.reshape(shape), new_one.reshape(shape),
        new_two.reshape(shape),
    )


def solution(mesh):
    replicas, groups, planes = mesh.devices.shape
    fine = Mesh(
        mesh.devices.reshape(replicas, groups // 2, 2, planes), ("edata", "ey", "core", "tensor")
    )
    expert = ("ey", "core")
    block = P(("edata", "ey", "core"), None)
    state = P("edata", expert, "tensor")
    saved = P("edata", None, expert, None, "tensor")
    return jax.shard_map(
        shards,
        mesh=fine,
        in_specs=(block, block, block, saved, P(expert, "tensor", None), state, state),
        out_specs=(saved, block, state, state, state),
        check_vma=False,
    )
```

time: 146 us -> 128 us (0.88)
  starting transfers between devices: 20.8 us -> 0.08 us
  waiting for transfers between devices: 53.5 us -> 61.1 us
  other arithmetic: 3.02 us -> 0.69 us
  local copies, waits for them, and re-layouts: 12.5 us -> 10.7 us
    all_gather x2 -> x1, waiting for transfers between devices: 37.2 us -> 55.7 us  [shards(): lax.all_gather(jnp.concatenate([grad_out, meta], axis=1), ('ey', 'core'),...]
    ppermute x2 -> x0, starting transfers between devices: 12.5 us -> none  [the longest x1 6.25 us: shards(): rest_other = lax.ppermute(rest, 'core', swap)]
    all_to_all x2 -> x0, waiting for transfers between devices: 12.2 us -> none  [the longest x1 6.53 us: shards(): lax.all_to_all(jnp.broadcast_to(saved[None], (replicas,) + saved.shape),...]
    all_to_all x2 -> x0, starting transfers between devices: 8.3 us -> none  [the longest x1 4.84 us: shards(): from_replicas = lax.all_to_all(to_replicas, 'edata', 0, 0, tiled=True)]
    reduce_scatter x0 -> x1, waiting for transfers between devices: none -> 5.39 us  [shards(): grad = lax.psum_scatter(grad, 'edata', scatter_dimension=0, tiled=True)]
    ppermute x2 -> x0, waiting for transfers between devices: 4.07 us -> none  [the longest x1 4.07 us: shards(): own_other = lax.ppermute(own, 'core', swap)]
    pallas_call x2 -> x3, Pallas kernels: 11.1 us -> 9.92 us  [the longest x1 6.89 us: shards(): pl.pallas_call(functools.partial(own_kernel, tokens, rows, planes), grid=...]
    unnamed x20 -> x19, local copies, waits for them, and re-layouts: 7.86 us -> 8.91 us
  transfers between devices with their start and end apart: 6 -> 2, of which waited for: 5 -> 2; matrix products, arithmetic and copies ran while one was open for 4% -> 0% of each run, Pallas kernels for 3% -> 1%
where the time goes in v3:
time: 128 us; the launch traced here: 127 us
  waiting for transfers between devices  61.1 us (48%)
  blocking collectives  30.6 us (24%)
  between operations  14.1 us (11%)
  local copies, waits for them, and re-layouts  10.7 us (8%)
  Pallas kernels  9.92 us (8%)
    all_gather x1, waiting for transfers between devices, shards(): lax.all_gather(jnp.concatenate([grad_out, meta], axis=1), ('ey', 'core'),...  55.7 us
    all_to_all x1, blocking collectives, shards(): lax.all_to_all(gate_part, ('ey', 'core', 'tensor'), 0, 0, tiled=True)  30.6 us
    unnamed x19, local copies, waits for them, and re-layouts  8.91 us
    pallas_call x1, Pallas kernels, shards(): pl.pallas_call(functools.partial(own_kernel, tokens, rows, planes), grid=...  6.89 us
    reduce_scatter x1, waiting for transfers between devices, shards(): grad = lax.psum_scatter(grad, 'edata', scatter_dimension=0, tiled=True)  5.39 us
  transfers between devices with their start and end apart: 2, of which 2 were waited for; matrix products, arithmetic and copies ran while one was open for 0% of the time, Pallas kernels for 1%

profile of v3, /device:TPU:1, one launch (start us, length us, event | category | flops | bytes accessed | tf_op | source)
XLA Modules:
  0.0 127.2 jit_solution(4955043602523685200)
XLA Ops:
  7.2 0.0 all-gather.2.cloned.1.call-start
  7.2 0.7 convert_element_type.3
  7.9 0.1 copy.14
  8.0 0.8 copy.15
  8.8 1.7 %concatenate.3 = bf16[32,4224]{1,0:T(8,128)(2,1)} concatenate(bf16[32,4096]{1,0:T(8,128)(2,1)} %param.7, bf16[32,8]{1,0:T(8,128)(2,1)S(1)} %copy.14, bf16[32,8]{1,0:T(8,128)(2,1)S(1)} %copy.15, bf16[32,112]{1,0:T(8,128)(2,1)S(1)} %broadcast_in_dim.3), dimensions={1} | concatenate | bytes 540672 | tf_op jit(solution)/shard_map/concatenate | solution.py:171
  10.5 0.0 all-gather.2.cloned.1.call-update
  10.5 0.0 reduce-scatter.2.cloned.1.call-start
  10.6 55.7 %all-gather.2.cloned.1.call-done.toks.meta = bf16[512,4224]{1,0:T(8,128)(2,1)} async-done(((bf16[32,4224]{1,0:T(8,128)(2,1)}), bf16[512,4224]{1,0:T(8,128)(2,1)}) %all-gather.2.cloned.1.call-update) | async-done | bytes 4325392 | tf_op jit(solution)/shard_map/all_gather | solution.py:170
  66.3 0.0 copy-start
  66.3 2.2 %copy-done = bf16[512,4224]{1,0:T(8,128)(2,1)S(1)} copy-done((bf16[512,4224]{1,0:T(8,128)(2,1)S(1)}, bf16[512,4224]{1,0:T(8,128)(2,1)}, u32[]{:S(2)}) %copy-start) | copy-done | bytes 4325400
  68.5 0.0 copy-start.1
  68.5 1.6 %copy-done.1 = bf16[2,128,4096]{2,1,0:T(8,128)(2,1)S(1)} copy-done((bf16[2,128,4096]{2,1,0:T(8,128)(2,1)S(1)}, bf16[2,128,4096]{2,1,0:T(8,128)(2,1)}, u32[]{:S(2)}) %copy-start.1) | copy-done | bytes 2097176
  70.1 0.0 copy-start.7
  70.1 0.9 copy-done.7
  71.0 0.0 copy-start.4
  71.0 6.9 %own_tokens.1 = (bf16[384,128]{1,0:T(8,128)(2,1)}, f32[192,1,64]{2,1,0:T(1,128)S(1)}, bf16[4096,256]{1,0:T(8,128)(2,1)S(1)}) custom-call(bf16[512,4224]{1,0:T(8,128)(2,1)S(1)} %copy-done, bf16[512,4224]{1,0:T(8,128)(2,1)S(1)} %copy-done, bf16[256,4096]{1,0:T(8,128)(2,1)S(1)} %bitcast.16, bf16[384,128]{1,0:T(8,128)(2,1)S(1)} %bitcast.20), custom_call_target="tpu_custom_call" | custom-call | flops 2147483648 | bytes 8388608 | tf_op jit(solution)/shard_map/own_tokens/pallas_call | solution.py:176
  77.9 0.0 copy-start.3
  77.9 1.3 %copy-done.3 = bf16[4096,256]{1,0:T(8,128)(2,1)} copy-done((bf16[4096,256]{1,0:T(8,128)(2,1)}, bf16[4096,256]{1,0:T(8,128)(2,1)S(1)}, u32[]{:S(2)}) %copy-start.3) | copy-done | bytes 2097176
  79.2 0.0 copy-start.8
  79.2 0.0 copy-start.2
  79.2 0.0 reduce-scatter.2.cloned.1.call-update
  79.2 30.6 %all_to_all.5.arrived = f32[192,1,64]{2,1,0:T(1,128)S(1)} all-to-all(f32[192,1,64]{2,1,0:T(1,128)S(1)} %get-tuple-element.12), channel_id=1, replica_groups=mesh['edata'=4,'ey'=8,'core'=2,'tensor'=12] {'ey','core','tensor'}, dimensions={0} | all-to-all | bytes 98304 | tf_op jit(solution)/shard_map/all_to_all | solution.py:206
  109.9 0.0 copy-done.8
  109.9 0.7 gates_home.1
  110.6 5.4 %reduce-scatter.2.cloned.1.call-done.grad = bf16[1024,256]{1,0:T(8,128)(2,1)} async-done(((bf16[4096,256]{1,0:T(8,128)(2,1)}), bf16[1024,256]{1,0:T(8,128)(2,1)}) %reduce-scatter.2.cloned.1.call-update) | async-done | bytes 524304 | tf_op jit(solution)/shard_map/reduce_scatter | solution.py:205
  115.9 0.0 copy-done.4
  115.9 0.0 copy-done.2
  116.0 0.0 copy-start.5
  116.0 1.0 copy-done.5
  117.0 0.0 copy-start.6
  117.0 1.0 copy-done.6
  118.0 2.3 %adam.1 = (bf16[2048,128]{1,0:T(8,128)(2,1)}, bf16[2048,128]{1,0:T(8,128)(2,1)}, f32[2048,128]{1,0:T(8,128)}) custom-call(bf16[1024,256]{1,0:T(8,128)(2,1)S(1)} %copy-done.6, bf16[256,4096]{1,0:T(8,128)(2,1)S(1)} %bitcast.17, bf16[2048,128]{1,0:T(8,128)(2,1)S(1)} %bitcast.19, f32[2048,128]{1,0:T(8,128)S(1)} %bitcast.18), custom_call_target="tpu_custom_call" | custom-call | flops 524288 | bytes 8388608 | tf_op jit(solution)/shard_map/adam/pallas_call | solution.py:215
  (1 shorter events, 0.0 us)
Async XLA Ops:
  7.2 59.1 %all-gather.2.cloned.1.call-start = ((), (), s32[]{:S(2)}) async-start(), calls=%async_computation.2 | async-start | bytes 4595712 | tf_op jit(solution)/shard_map/all_gather | solution.py:170
  10.5 105.4 %reduce-scatter.2.cloned.1.call-start = ((), (), s32[]{:S(2)}) async-start(), calls=%async_computation.3 | async-start | bytes 2621440 | tf_op jit(solution)/shard_map/reduce_scatter | solution.py:205
  66.3 2.2 %copy-start = (bf16[512,4224]{1,0:T(8,128)(2,1)S(1)}, bf16[512,4224]{1,0:T(8,128)(2,1)}, u32[]{:S(2)}) copy-start(bf16[512,4224]{1,0:T(8,128)(2,1)} %all-gather.2.cloned.1.call-done.toks.meta) | copy-start | bytes 12976132
  68.5 1.6 %copy-start.1 = (bf16[2,128,4096]{2,1,0:T(8,128)(2,1)S(1)}, bf16[2,128,4096]{2,1,0:T(8,128)(2,1)}, u32[]{:S(2)}) copy-start(bf16[2,128,4096]{2,1,0:T(8,128)(2,1)} %param.11) | copy-start | bytes 6291460
  70.1 0.9 copy-start.7
  71.0 45.0 %copy-start.4 = (f32[1024,2,128]{2,1,0:T(2,128)S(1)}, f32[1024,2,128]{2,1,0:T(2,128)}, u32[]{:S(2)}) copy-start(f32[1024,2,128]{2,1,0:T(2,128)} %param.13) | copy-start | bytes 3145732
  77.9 1.3 %copy-start.3 = (bf16[4096,256]{1,0:T(8,128)(2,1)}, bf16[4096,256]{1,0:T(8,128)(2,1)S(1)}, u32[]{:S(2)}) copy-start(bf16[4096,256]{1,0:T(8,128)(2,1)S(1)} %get-tuple-element.13) | copy-start | bytes 6291460
  79.2 30.6 %copy-start.8 = (s32[32,8]{0,1:T(8,128)S(1)}, s32[32,8]{0,1:T(8,128)}, u32[]{:S(2)}) copy-start(s32[32,8]{0,1:T(8,128)} %param.9) | copy-start | bytes 3076
  79.2 36.7 %copy-start.2 = (bf16[2,128,4096]{2,1,0:T(8,128)(2,1)S(1)}, bf16[2,128,4096]{2,1,0:T(8,128)(2,1)}, u32[]{:S(2)}) copy-start(bf16[2,128,4096]{2,1,0:T(8,128)(2,1)} %param.11) | copy-start | bytes 6291460
  116.0 1.0 copy-start.5
  117.0 1.0 copy-start.6
Sparse Core Ops, SparseCore 0:
  11.0 55.2 all-gather.1
  79.4 36.5 reduce-scatter.1

commit v4 on v2

v4 whole, which is shorter than its diff:
```python
import functools

import jax
import jax.numpy as jnp
from jax import lax
from jax.experimental import pallas as pl
from jax.experimental.pallas import tpu as pltpu
from jax.sharding import Mesh, PartitionSpec as P

beta_one = 0.9
beta_two = 0.999
adam_eps = 1e-08
learn_rate = 0.01
corr_two = 0.6323045752

F32 = jnp.float32
BF16 = jnp.bfloat16
LANES = 128
PARAMS = pltpu.CompilerParams(vmem_limit_bytes=40 * 1024 * 1024)


def dot(a, b, over, precision=None):
    return lax.dot_general(
        a, b, (((over[0],), (over[1],)), ((), ())), precision=precision, preferred_element_type=F32
    )


def expert_base():
    return ((lax.axis_index("ey") * 2 + lax.axis_index("core")) * 2).astype(F32)


def routed(meta, base, tokens, rows):
    count = meta.shape[0]
    meta = meta.astype(F32)
    ids, gates = meta[:, :8], meta[:, 8:16]
    hits = [ids == base + e for e in range(2)]
    named = [jnp.sum(jnp.where(h, 1.0, 0.0), axis=1, keepdims=True) for h in hits]
    gate = [jnp.sum(jnp.where(h, gates, 0.0), axis=1, keepdims=True) for h in hits]
    lane = lax.broadcasted_iota(jnp.int32, (count, LANES), 1)
    marks = jnp.where(lane == 0, named[0], jnp.where(lane == 1, named[1], 0.0)).astype(BF16)
    row_i = lax.broadcasted_iota(jnp.int32, (count, count), 0)
    col_i = lax.broadcasted_iota(jnp.int32, (count, count), 1)
    earlier = ((row_i // tokens == col_i // tokens) & (col_i < row_i)).astype(F32).astype(BF16)
    rank = dot(earlier, marks, (1, 0))
    block = (lax.broadcasted_iota(jnp.int32, (count, 1), 0) // tokens).astype(F32)
    slot_rows = (count // tokens) * rows
    slot_lane = lax.broadcasted_iota(jnp.int32, (count, slot_rows), 1).astype(F32)
    keys = [
        jnp.where(named[e] > 0.5, block * rows + 2.0 * rank[:, e : e + 1] + e, -1.0)
        for e in range(2)
    ]
    onehot = ((slot_lane == keys[0]) | (slot_lane == keys[1])).astype(F32).astype(BF16)
    return onehot, gate


def by_expert(hid):
    odd = lax.broadcasted_iota(jnp.int32, hid.shape, 0) % 2
    hid = hid.astype(F32)
    return jnp.concatenate(
        [jnp.where(odd == 0, hid, 0.0), jnp.where(odd == 1, hid, 0.0)], axis=1
    ).astype(BF16)


def gate_lanes(gate):
    return jnp.concatenate([jnp.broadcast_to(g, (g.shape[0], LANES)) for g in gate], axis=1)


def own_kernel(tokens, rows, width, planes, pieces, *refs):
    weight, hid, grad_hidden, gate_part = refs[pieces : pieces + 4]
    grads, toks = refs[pieces + 4 : -1], refs[-1]
    core, line = lax.axis_index("core"), lax.axis_index("ey")
    base = expert_base()
    blocks = grad_hidden.shape[0]
    count = blocks * tokens
    at = 0
    for ref in refs[:pieces]:
        toks[at : at + ref.shape[0], :] = ref[...]
        at += ref.shape[0]
    where = [(line + step) % blocks for step in arrival(blocks)]
    gates_out = None
    scaled = []
    for rel in range(2):
        side = core if rel == 0 else 1 - core
        here = slice(rel * count, (rel + 1) * count)
        onehot, gate = routed(toks[here, width : width + LANES], base, tokens, rows)
        slots = jnp.concatenate([hid[block, side].astype(F32) for block in where], axis=0)
        saved = dot(onehot, by_expert(slots), (1, 0))
        up = dot(toks[here, :width], weight[...], (1, 1))
        scale = gate_lanes(gate)
        scaled.append((scale * saved).astype(BF16))
        picked = dot(onehot, (scale * up).astype(BF16), (0, 0))
        even = lax.broadcasted_iota(jnp.int32, (blocks * rows, LANES), 0) % 2 == 0
        picked = jnp.where(even, picked[:, :LANES], picked[:, LANES:])
        for order, block in enumerate(where):
            grad_hidden[block, side] = picked[order * rows : (order + 1) * rows].astype(BF16)
        prod = saved * up
        lane = lax.broadcasted_iota(jnp.int32, (count, LANES), 1)
        tok = lax.broadcasted_iota(jnp.int32, (count, LANES), 0) % tokens
        spread = jnp.zeros((count, LANES), F32)
        for e in range(2):
            total = jnp.sum(prod[:, e * LANES : (e + 1) * LANES], axis=1, keepdims=True)
            spread = jnp.where(lane == e * tokens + tok, total, spread)
        order = lax.broadcasted_iota(jnp.int32, (2 * blocks, count), 1) // tokens
        away = jnp.where(order % 2 == 1, -((order + 1) // 2), order // 2)
        row = lax.broadcasted_iota(jnp.int32, (2 * blocks, count), 0)
        pick = ((line + away + blocks) % blocks * 2 + side == row).astype(F32)
        piece = dot(pick, spread, (1, 0), lax.Precision.HIGHEST)
        gates_out = piece if gates_out is None else gates_out + piece
    for group in range(2 * blocks):
        values = gates_out[group : group + 1, : 2 * tokens]
        for plane in range(planes):
            gate_part[group * planes + plane] = values
    scaled = jnp.concatenate(scaled, axis=0)
    part = grads[0].shape[0]
    replicas = len(grads)
    for step, grad in enumerate(grads):
        owner = (lax.axis_index("edata") + step) % replicas
        columns = toks[:, pl.ds(pl.multiple_of(owner * part, LANES), part)]
        grad[...] = dot(columns, scaled, (0, 0)).astype(BF16)


def arrival(blocks):
    steps = [0]
    for away in range(1, blocks // 2):
        steps += [blocks - away, away]
    return steps + [blocks // 2]


def home_kernel(tokens, planes, arrived, ids, out):
    groups = arrived.shape[0] // planes
    total = jnp.zeros(ids.shape, F32)
    named = ids[...]
    for group in range(groups):
        line = arrived[group * planes]
        for plane in range(1, planes):
            line = line + arrived[group * planes + plane]
        for e in range(2):
            value = line[:, e * tokens : (e + 1) * tokens]
            total = jnp.where(named == group * 2 + e, value, total)
    out[...] = total


def adam_kernel(part, replicas, *refs):
    weight, one, two, new_weight, new_one, new_two, grad_rows, weight_rows = refs[replicas:]
    total = sum(ref[...].astype(F32) for ref in refs[1:replicas]) + refs[0][...].astype(F32)
    column = pl.multiple_of(lax.axis_index("edata") * part, LANES)
    for e in range(2):
        grad_rows[pl.ds(e, part, 2), :] = total[:, e * LANES : (e + 1) * LANES]
        piece = weight[e * LANES : (e + 1) * LANES, pl.ds(column, part)].astype(F32)
        weight_rows[pl.ds(e, part, 2), :] = piece.T
    g = grad_rows[...]
    first = beta_one * one[...].astype(F32) + (1.0 - beta_one) * g
    second = beta_two * two[...] + (1.0 - beta_two) * g * g
    update = first / (jnp.sqrt(second / corr_two) + adam_eps)
    new_weight[...] = (weight_rows[...] - learn_rate * update).astype(BF16)
    new_one[...] = first.astype(BF16)
    new_two[...] = second


def cost(tokens, terms, moved):
    return pl.CostEstimate(flops=2 * tokens * terms, bytes_accessed=moved, transcendentals=0)


def gathered(own):
    size, half = lax.axis_size("ey"), own.shape[0] // 2
    ahead = [(i, (i + 1) % size) for i in range(size)]
    back = [(i, (i - 1) % size) for i in range(size)]
    swap = [(0, 1), (1, 0)]
    mine = [own]
    up = down = own
    for _ in range(1, size // 2):
        up, down = lax.ppermute(up, "ey", ahead), lax.ppermute(down, "ey", back)
        mine += [up, down]
    last = [lax.ppermute(up[:half], "ey", ahead), lax.ppermute(down[half:], "ey", back)]
    theirs = [lax.ppermute(jnp.concatenate(g, axis=0), "core", swap) for g in (mine, last)]
    return mine + last + theirs


def shards(grad_out, gates, expert_ids, hidden, down_weight, moment_one, moment_two):
    tokens, width = grad_out.shape
    choices = gates.shape[1]
    replicas, planes = lax.axis_size("edata"), lax.axis_size("tensor")
    groups = lax.axis_size("ey") * 2
    held, capacity = hidden.shape[2], hidden.shape[3]
    rows = held * capacity
    part = width // replicas
    every = groups * tokens

    meta = jnp.concatenate(
        [expert_ids.astype(BF16), gates, jnp.zeros((tokens, LANES - 2 * choices), BF16)], axis=1
    )
    toks = gathered(jnp.concatenate([grad_out, meta], axis=1))
    saved = jnp.transpose(hidden[0], (0, 2, 1, 3)).reshape(groups // 2, 2, rows, LANES)
    weight = down_weight.reshape(held * LANES, width)
    grad_hidden, gate_part, *grads = pl.pallas_call(
        functools.partial(own_kernel, tokens, rows, width, planes, len(toks)),
        out_shape=(
            jax.ShapeDtypeStruct(saved.shape, BF16),
            jax.ShapeDtypeStruct((groups * planes, 1, held * tokens), F32),
        )
        + (jax.ShapeDtypeStruct((part, held * LANES), BF16),) * replicas,
        scratch_shapes=[pltpu.VMEM((every, width + LANES), BF16)],
        compiler_params=PARAMS,
        cost_estimate=cost(every, 2 * width * held * LANES, 8 << 20),
        name="own_tokens",
    )(*toks, weight, saved)

    for step in range(1, replicas):
        to_owner = [(i, (i + step) % replicas) for i in range(replicas)]
        grads[step] = lax.ppermute(grads[step], "edata", to_owner)
    gate_home = lax.all_to_all(gate_part, ("ey", "core", "tensor"), 0, 0, tiled=True)
    grad_gates = pl.pallas_call(
        functools.partial(home_kernel, tokens, planes),
        out_shape=jax.ShapeDtypeStruct((choices, tokens), F32),
        compiler_params=PARAMS,
        name="gates_home",
    )(gate_home, expert_ids.T).T

    flat = (part * held, LANES)
    new_weight, new_one, new_two = pl.pallas_call(
        functools.partial(adam_kernel, part, replicas),
        out_shape=(
            jax.ShapeDtypeStruct(flat, BF16),
            jax.ShapeDtypeStruct(flat, BF16),
            jax.ShapeDtypeStruct(flat, F32),
        ),
        scratch_shapes=[pltpu.VMEM(flat, F32), pltpu.VMEM(flat, F32)],
        compiler_params=PARAMS,
        cost_estimate=cost(part, held * LANES, 8 << 20),
        name="adam",
    )(*grads, weight, moment_one.reshape(flat), moment_two.reshape(flat))
    grad_hidden = jnp.transpose(
        grad_hidden.reshape(1, groups, capacity, held, LANES), (0, 1, 3, 2, 4)
    )
    shape = moment_one.shape
    return (
        grad_hidden, grad_gates, new_weight.reshape(shape), new_one.reshape(shape),
        new_two.reshape(shape),
    )


def solution(mesh):
    replicas, groups, planes = mesh.devices.shape
    fine = Mesh(
        mesh.devices.reshape(replicas, groups // 2, 2, planes), ("edata", "ey", "core", "tensor")
    )
    expert = ("ey", "core")
    block = P(("edata", "ey", "core"), None)
    state = P("edata", expert, "tensor")
    saved = P("edata", None, expert, None, "tensor")
    return jax.shard_map(
        shards,
        mesh=fine,
        in_specs=(block, block, block, saved, P(expert, "tensor", None), state, state),
        out_specs=(saved, block, state, state, state),
        check_vma=False,
    )
```

time: 145 us -> 113 us (0.78)
  blocking collectives: 0 us -> 31.1 us
  starting transfers between devices: 76.8 us -> 49.9 us
  between operations: 14.3 us -> 0.86 us
  local copies, waits for them, and re-layouts: 12.3 us -> 2.14 us
  other arithmetic: 7.05 us -> 0.71 us
  Pallas kernels: 12.6 us -> 7.77 us
    all_to_all x0 -> x1, blocking collectives: none -> 31.1 us  [shards(): lax.all_to_all(gate_part, ('ey', 'core', 'tensor'), 0, 0, tiled=True)]
    all_to_all x3 -> x0, starting transfers between devices: 23.9 us -> none  [the longest x1 15.8 us: shards(): lax.all_to_all(gate_send, ('ey', 'core', 'tensor'), 0, 0, tiled=True)]
    all_to_all x3 -> x0, waiting for transfers between devices: 9.86 us -> none  [the longest x1 5.65 us: shards(): from_replicas = lax.all_to_all(to_replicas, 'edata', 0, 0, tiled=True)]
    ppermute x6, waiting for transfers between devices: 5.29 us -> 13.3 us  [gathered(): up, down = (lax.ppermute(up, 'ey', ahead), lax.ppermute(down, 'ey', back))]
    pallas_call x2 -> x3, Pallas kernels: 12.6 us -> 7.77 us  [the longest x1 4.56 us: shards(): pl.pallas_call(functools.partial(own_kernel, tokens, rows, width, planes,...]
    concatenate x6 -> x1, other arithmetic: 4.71 us -> 0.02 us  [gathered(): jnp.concatenate(g, axis=0)]
    unnamed x18 -> x17, local copies, waits for them, and re-layouts: 5.21 us -> 0.95 us
    ppermute x1, starting transfers between devices: 4.57 us -> 1.92 us  [gathered(): lax.ppermute(down[half:], 'ey', back)]
  transfers between devices with their start and end apart: 18 -> 13, of which waited for: 6 -> 7; matrix products, arithmetic and copies ran while one was open for 6% -> 0% of each run, Pallas kernels for 9% -> 1%
where the time goes in v4:
time: 113 us; the launch traced here: 112 us
  starting transfers between devices  49.9 us (44%)
  blocking collectives  31.1 us (28%)
  waiting for transfers between devices  19.4 us (17%)
  Pallas kernels  7.77 us (7%)
  local copies, waits for them, and re-layouts  2.14 us (2%)
    all_to_all x1, blocking collectives, shards(): lax.all_to_all(gate_part, ('ey', 'core', 'tensor'), 0, 0, tiled=True)  31.1 us
    ppermute x6, starting transfers between devices, gathered(): up, down = (lax.ppermute(up, 'ey', ahead), lax.ppermute(down, 'ey', back))  21.6 us
    ppermute x2, starting transfers between devices, gathered(): lax.ppermute(jnp.concatenate(g, axis=0), 'core', swap)  14.6 us
    ppermute x6, waiting for transfers between devices, gathered(): up, down = (lax.ppermute(up, 'ey', ahead), lax.ppermute(down, 'ey', back))  13.3 us
    ppermute x3, starting transfers between devices, shards(): grads[step] = lax.ppermute(grads[step], 'edata', to_owner)  8.41 us
    pallas_call x1, Pallas kernels, shards(): pl.pallas_call(functools.partial(own_kernel, tokens, rows, width, planes,...  4.56 us
    ppermute x1, starting transfers between devices, gathered(): lax.ppermute(up[:half], 'ey', ahead)  3.36 us
    ppermute x1, waiting for transfers between devices, gathered(): lax.ppermute(up[:half], 'ey', ahead)  3.16 us
  transfers between devices with their start and end apart: 13, of which 7 were waited for; matrix products, arithmetic and copies ran while one was open for 0% of the time, Pallas kernels for 1%

profile of v4, /device:TPU:1, one launch (start us, length us, event | category | flops | bytes accessed | tf_op | source)
XLA Modules:
  0.0 111.9 jit_solution(2019061184048378815)
XLA Ops:
  0.6 0.7 convert_element_type.3
  1.3 0.1 copy.14
  1.4 0.8 copy.15
  2.2 1.0 concatenate.9.refs_0_
  3.2 5.9 %collective-permute-start.1 = (bf16[32,4224]{1,0:T(8,128)(2,1)S(1)}, bf16[32,4224]{1,0:T(8,128)(2,1)S(1)}, u32[]{:S(2)}, u32[]{:S(2)}) collective-permute-start(bf16[32,4224]{1,0:T(8,128)(2,1)S(1)} %concatenate.9.refs_0_), channel_id=1, source_target_pairs={{0,168},{24,0},{48,24},{72,48},{96,72},{120,96},{144,120},{168,144... | collective-permute-start | bytes 811016 | tf_op jit(solution)/shard_map/ppermute | solution.py:172
  9.2 1.9 %collective-permute-start = (bf16[32,4224]{1,0:T(8,128)(2,1)S(1)}, bf16[32,4224]{1,0:T(8,128)(2,1)S(1)}, u32[]{:S(2)}, u32[]{:S(2)}) collective-permute-start(bf16[32,4224]{1,0:T(8,128)(2,1)S(1)} %concatenate.9.refs_0_), channel_id=1, source_target_pairs={{0,24},{24,48},{48,72},{72,96},{96,120},{120,144},{144,168},{168,0... | collective-permute-start | bytes 811016 | tf_op jit(solution)/shard_map/ppermute | solution.py:172
  11.1 1.4 %collective-permute-done.1.refs_2_ = bf16[32,4224]{1,0:T(8,128)(2,1)S(1)} collective-permute-done((bf16[32,4224]{1,0:T(8,128)(2,1)S(1)}, bf16[32,4224]{1,0:T(8,128)(2,1)S(1)}, u32[]{:S(2)}, u32[]{:S(2)}) %collective-permute-start.1) | collective-permute-done | bytes 270368 | tf_op jit(solution)/shard_map/ppermute | solution.py:172
  12.5 5.0 %collective-permute-start.3 = (bf16[32,4224]{1,0:T(8,128)(2,1)S(1)}, bf16[32,4224]{1,0:T(8,128)(2,1)S(1)}, u32[]{:S(2)}, u32[]{:S(2)}) collective-permute-start(bf16[32,4224]{1,0:T(8,128)(2,1)S(1)} %collective-permute-done.1.refs_2_), channel_id=1, source_target_pairs={{0,168},{24,0},{48,24},{72,48},{96,72},{120,96},{144,120},{168,144... | collective-permute-start | bytes 811016 | tf_op jit(solution)/shard_map/ppermute | solution.py:172
  17.6 0.0 collective-permute-done.refs_1_
  17.6 1.9 %collective-permute-start.2 = (bf16[32,4224]{1,0:T(8,128)(2,1)S(1)}, bf16[32,4224]{1,0:T(8,128)(2,1)S(1)}, u32[]{:S(2)}, u32[]{:S(2)}) collective-permute-start(bf16[32,4224]{1,0:T(8,128)(2,1)S(1)} %collective-permute-done.refs_1_), channel_id=1, source_target_pairs={{0,24},{24,48},{48,72},{72,96},{96,120},{120,144},{144,168},{168,0... | collective-permute-start | bytes 811016 | tf_op jit(solution)/shard_map/ppermute | solution.py:172
  19.5 0.0 copy-start
  19.5 0.0 copy-start.4
  19.6 2.9 %collective-permute-done.3.refs_4_ = bf16[32,4224]{1,0:T(8,128)(2,1)S(1)} collective-permute-done((bf16[32,4224]{1,0:T(8,128)(2,1)S(1)}, bf16[32,4224]{1,0:T(8,128)(2,1)S(1)}, u32[]{:S(2)}, u32[]{:S(2)}) %collective-permute-start.3) | collective-permute-done | bytes 270368 | tf_op jit(solution)/shard_map/ppermute | solution.py:172
  22.4 4.7 %collective-permute-start.5 = (bf16[32,4224]{1,0:T(8,128)(2,1)S(1)}, bf16[32,4224]{1,0:T(8,128)(2,1)S(1)}, u32[]{:S(2)}, u32[]{:S(2)}) collective-permute-start(bf16[32,4224]{1,0:T(8,128)(2,1)S(1)} %collective-permute-done.3.refs_4_), channel_id=1, source_target_pairs={{0,168},{24,0},{48,24},{72,48},{96,72},{120,96},{144,120},{168,144... | collective-permute-start | bytes 811016 | tf_op jit(solution)/shard_map/ppermute | solution.py:172
  27.2 0.3 collective-permute-done.2.refs_3_
  27.4 2.2 %collective-permute-start.4 = (bf16[32,4224]{1,0:T(8,128)(2,1)S(1)}, bf16[32,4224]{1,0:T(8,128)(2,1)S(1)}, u32[]{:S(2)}, u32[]{:S(2)}) collective-permute-start(bf16[32,4224]{1,0:T(8,128)(2,1)S(1)} %collective-permute-done.2.refs_3_), channel_id=1, source_target_pairs={{0,24},{24,48},{48,72},{72,96},{96,120},{120,144},{144,168},{168,0... | collective-permute-start | bytes 811016 | tf_op jit(solution)/shard_map/ppermute | solution.py:172
  29.7 8.7 %collective-permute-done.4.refs_5_ = bf16[32,4224]{1,0:T(8,128)(2,1)S(1)} collective-permute-done((bf16[32,4224]{1,0:T(8,128)(2,1)S(1)}, bf16[32,4224]{1,0:T(8,128)(2,1)S(1)}, u32[]{:S(2)}, u32[]{:S(2)}) %collective-permute-start.4) | collective-permute-done | bytes 270368 | tf_op jit(solution)/shard_map/ppermute | solution.py:172
  38.4 0.0 collective-permute-done.5.refs_6_
  38.5 11.9 %collective-permute-start.8 = (bf16[224,4224]{1,0:T(8,128)(2,1)S(1)}, bf16[224,4224]{1,0:T(8,128)(2,1)S(1)}, u32[]{:S(2)}, u32[]{:S(2)}) collective-permute-start(bf16[224,4224]{1,0:T(8,128)(2,1)S(1)} %constant_dynamic-update-slice_fusion), channel_id=1, source_target_pairs={{0,12},{12,0},{1,13},{13,1},{2,14},{14,2},{3,15},{15,3},{4,16},{16... | collective-permute-start | bytes 5677064 | tf_op jit(solution)/shard_map/ppermute | solution.py:175
  50.4 1.9 %collective-permute-start.7 = (bf16[16,4224]{1,0:T(8,128)(2,1)S(1)}, bf16[16,4224]{1,0:T(8,128)(2,1)S(1)}, u32[]{:S(2)}, u32[]{:S(2)}) collective-permute-start(bf16[16,4224]{1,0:T(8,128)(2,1)S(1)} %slice.9), channel_id=1, source_target_pairs={{0,168},{24,0},{48,24},{72,48},{96,72},{120,96},{144,120},{168,144... | collective-permute-start | bytes 405512 | tf_op jit(solution)/shard_map/ppermute | solution.py:174
  52.3 3.4 %collective-permute-start.6 = (bf16[16,4224]{1,0:T(8,128)(2,1)S(1)}, bf16[16,4224]{1,0:T(8,128)(2,1)S(1)}, u32[]{:S(2)}, u32[]{:S(2)}) collective-permute-start(bf16[16,4224]{1,0:T(8,128)(2,1)S(1)} %slice.8), channel_id=1, source_target_pairs={{0,24},{24,48},{48,72},{72,96},{96,120},{120,144},{144,168},{168,0... | collective-permute-start | bytes 405512 | tf_op jit(solution)/shard_map/ppermute | solution.py:174
  55.7 1.8 %collective-permute-done.7.refs_8_ = bf16[16,4224]{1,0:T(8,128)(2,1)S(1)} collective-permute-done((bf16[16,4224]{1,0:T(8,128)(2,1)S(1)}, bf16[16,4224]{1,0:T(8,128)(2,1)S(1)}, u32[]{:S(2)}, u32[]{:S(2)}) %collective-permute-start.7) | collective-permute-done | bytes 135200 | tf_op jit(solution)/shard_map/ppermute | solution.py:174
  57.5 3.2 %collective-permute-done.6.refs_7_ = bf16[16,4224]{1,0:T(8,128)(2,1)S(1)} collective-permute-done((bf16[16,4224]{1,0:T(8,128)(2,1)S(1)}, bf16[16,4224]{1,0:T(8,128)(2,1)S(1)}, u32[]{:S(2)}, u32[]{:S(2)}) %collective-permute-start.6) | collective-permute-done | bytes 135200 | tf_op jit(solution)/shard_map/ppermute | solution.py:174
  60.6 2.7 %collective-permute-start.9 = (bf16[32,4224]{1,0:T(8,128)(2,1)S(1)}, bf16[32,4224]{1,0:T(8,128)(2,1)S(1)}, u32[]{:S(2)}, u32[]{:S(2)}) collective-permute-start(bf16[32,4224]{1,0:T(8,128)(2,1)S(1)} %pad_maximum_fusion), channel_id=1, source_target_pairs={{0,12},{12,0},{1,13},{13,1},{2,14},{14,2},{3,15},{15,3},{4,16},{16... | collective-permute-start | bytes 811016 | tf_op jit(solution)/shard_map/ppermute | solution.py:175
  63.4 1.2 %collective-permute-done.9.refs_10_ = bf16[32,4224]{1,0:T(8,128)(2,1)S(1)} collective-permute-done((bf16[32,4224]{1,0:T(8,128)(2,1)S(1)}, bf16[32,4224]{1,0:T(8,128)(2,1)S(1)}, u32[]{:S(2)}, u32[]{:S(2)}) %collective-permute-start.9) | collective-permute-done | bytes 270368 | tf_op jit(solution)/shard_map/ppermute | solution.py:175
  64.5 0.0 collective-permute-done.8.refs_9_
  64.5 0.0 copy-done
  64.5 0.0 copy-done.4
  64.5 0.0 copy-start.3
  64.5 0.0 copy-start.1
  64.5 0.0 copy-start.2
  64.5 4.6 %own_tokens.1 = (bf16[8,2,24,128]{3,2,1,0:T(8,128)(2,1)}, f32[192,1,64]{2,1,0:T(1,128)S(1)}, bf16[1024,256]{1,0:T(8,128)(2,1)S(1)}, bf16[1024,256]{1,0:T(8,128)(...) custom-call(bf16[32,4224]{1,0:T(8,128)(2,1)S(1)} %concatenate.9.refs_0_, ...), custom_call_target="tpu_custom_call" | custom-call | flops 2147483648 | bytes 8388608 | tf_op jit(solution)/shard_map/own_tokens/pallas_call | solution.py:195
  69.1 1.9 %collective-permute-start.10 = (bf16[1024,256]{1,0:T(8,128)(2,1)S(1)}, bf16[1024,256]{1,0:T(8,128)(2,1)S(1)}, u32[]{:S(2)}, u32[]{:S(2)}) collective-permute-start(bf16[1024,256]{1,0:T(8,128)(2,1)S(1)} %get-tuple-element.17), channel_id=1, source_target_pairs={{0,192},{192,384},{384,576},{576,0},{1,193},{193,385},{385,577},{5... | collective-permute-start | bytes 1572872 | tf_op jit(solution)/shard_map/ppermute | solution.py:210
  71.0 1.9 %collective-permute-start.11 = (bf16[1024,256]{1,0:T(8,128)(2,1)S(1)}, bf16[1024,256]{1,0:T(8,128)(2,1)S(1)}, u32[]{:S(2)}, u32[]{:S(2)}) collective-permute-start(bf16[1024,256]{1,0:T(8,128)(2,1)S(1)} %get-tuple-element.18), channel_id=1, source_target_pairs={{0,384},{192,576},{384,0},{576,192},{1,385},{193,577},{385,1},{577... | collective-permute-start | bytes 1572872 | tf_op jit(solution)/shard_map/ppermute | solution.py:210
  73.0 4.6 %collective-permute-start.12 = (bf16[1024,256]{1,0:T(8,128)(2,1)S(1)}, bf16[1024,256]{1,0:T(8,128)(2,1)S(1)}, u32[]{:S(2)}, u32[]{:S(2)}) collective-permute-start(bf16[1024,256]{1,0:T(8,128)(2,1)S(1)} %get-tuple-element.19), channel_id=1, source_target_pairs={{0,576},{192,0},{384,192},{576,384},{1,577},{193,1},{385,193},{577... | collective-permute-start | bytes 1572872 | tf_op jit(solution)/shard_map/ppermute | solution.py:210
  77.5 31.1 %all_to_all.5.arrived = f32[192,1,64]{2,1,0:T(1,128)S(1)} all-to-all(f32[192,1,64]{2,1,0:T(1,128)S(1)} %get-tuple-element.15), channel_id=1, replica_groups=mesh['edata'=4,'ey'=8,'core'=2,'tensor'=12] {'ey','core','tensor'}, dimensions={0} | all-to-all | bytes 98304 | tf_op jit(solution)/shard_map/all_to_all | solution.py:211
  108.7 0.0 copy-done.3
  108.7 0.7 gates_home.1
  109.4 0.0 collective-permute-done.10.refs_1_
  109.4 0.0 collective-permute-done.11.refs_2_
  109.4 0.0 collective-permute-done.12.refs_3_
  109.4 0.0 copy-done.1
  109.4 0.0 copy-done.2
  109.4 2.5 %adam.1 = (bf16[2048,128]{1,0:T(8,128)(2,1)}, bf16[2048,128]{1,0:T(8,128)(2,1)}, f32[2048,128]{1,0:T(8,128)}) custom-call(bf16[1024,256]{1,0:T(8,128)(2,1)S(1)} %get-tuple-element.16.refs_0_, bf16[1024,256]{1,0:T(8,128)(2,1)S(1)} %collective-permute-done.10.refs_1_, bf16[1024,256]{1,0:T(8,128)(2,1)S(1)} %collective-permute-done.11.refs_2_, ...), custom_call_target="tpu_custom_call" | custom-call | flops 524288 | bytes 8388608 | tf_op jit(solution)/shard_map/adam/pallas_call | solution.py:220
  (11 shorter events, 0.2 us)
Async XLA Ops:
  3.2 9.3 %collective-permute-start.1 = (bf16[32,4224]{1,0:T(8,128)(2,1)S(1)}, bf16[32,4224]{1,0:T(8,128)(2,1)S(1)}, u32[]{:S(2)}, u32[]{:S(2)}) collective-permute-start(bf16[32,4224]{1,0:T(8,128)(2,1)S(1)} %concatenate.9.refs_0_), channel_id=1, source_target_pairs={{0,168},{24,0},{48,24},{72,48},{96,72},{120,96},{144,120},{168,144... | collective-permute-start | bytes 811016 | tf_op jit(solution)/shard_map/ppermute | solution.py:172
  9.2 8.4 %collective-permute-start = (bf16[32,4224]{1,0:T(8,128)(2,1)S(1)}, bf16[32,4224]{1,0:T(8,128)(2,1)S(1)}, u32[]{:S(2)}, u32[]{:S(2)}) collective-permute-start(bf16[32,4224]{1,0:T(8,128)(2,1)S(1)} %concatenate.9.refs_0_), channel_id=1, source_target_pairs={{0,24},{24,48},{48,72},{72,96},{96,120},{120,144},{144,168},{168,0... | collective-permute-start | bytes 811016 | tf_op jit(solution)/shard_map/ppermute | solution.py:172
  12.5 9.9 %collective-permute-start.3 = (bf16[32,4224]{1,0:T(8,128)(2,1)S(1)}, bf16[32,4224]{1,0:T(8,128)(2,1)S(1)}, u32[]{:S(2)}, u32[]{:S(2)}) collective-permute-start(bf16[32,4224]{1,0:T(8,128)(2,1)S(1)} %collective-permute-done.1.refs_2_), channel_id=1, source_target_pairs={{0,168},{24,0},{48,24},{72,48},{96,72},{120,96},{144,120},{168,144... | collective-permute-start | bytes 811016 | tf_op jit(solution)/shard_map/ppermute | solution.py:172
  17.6 9.9 %collective-permute-start.2 = (bf16[32,4224]{1,0:T(8,128)(2,1)S(1)}, bf16[32,4224]{1,0:T(8,128)(2,1)S(1)}, u32[]{:S(2)}, u32[]{:S(2)}) collective-permute-start(bf16[32,4224]{1,0:T(8,128)(2,1)S(1)} %collective-permute-done.refs_1_), channel_id=1, source_target_pairs={{0,24},{24,48},{48,72},{72,96},{96,120},{120,144},{144,168},{168,0... | collective-permute-start | bytes 811016 | tf_op jit(solution)/shard_map/ppermute | solution.py:172
  19.5 45.0 %copy-start = (bf16[2,128,4096]{2,1,0:T(8,128)(2,1)S(1)}, bf16[2,128,4096]{2,1,0:T(8,128)(2,1)}, u32[]{:S(2)}) copy-start(bf16[2,128,4096]{2,1,0:T(8,128)(2,1)} %param.11) | copy-start | bytes 6291460
  19.5 45.0 %copy-start.4 = (bf16[1,16,2,12,128]{4,2,3,1,0:T(2,128)(2,1)S(1)}, bf16[1,16,2,12,128]{4,2,3,1,0:T(2,128)(2,1)}, u32[]{:S(2)}) copy-start(bf16[1,16,2,12,128]{4,2,3,1,0:T(2,128)(2,1)} %param.10) | copy-start | bytes 294916
  22.4 16.0 %collective-permute-start.5 = (bf16[32,4224]{1,0:T(8,128)(2,1)S(1)}, bf16[32,4224]{1,0:T(8,128)(2,1)S(1)}, u32[]{:S(2)}, u32[]{:S(2)}) collective-permute-start(bf16[32,4224]{1,0:T(8,128)(2,1)S(1)} %collective-permute-done.3.refs_4_), channel_id=1, source_target_pairs={{0,168},{24,0},{48,24},{72,48},{96,72},{120,96},{144,120},{168,144... | collective-permute-start | bytes 811016 | tf_op jit(solution)/shard_map/ppermute | solution.py:172
  27.4 11.0 %collective-permute-start.4 = (bf16[32,4224]{1,0:T(8,128)(2,1)S(1)}, bf16[32,4224]{1,0:T(8,128)(2,1)S(1)}, u32[]{:S(2)}, u32[]{:S(2)}) collective-permute-start(bf16[32,4224]{1,0:T(8,128)(2,1)S(1)} %collective-permute-done.2.refs_3_), channel_id=1, source_target_pairs={{0,24},{24,48},{48,72},{72,96},{96,120},{120,144},{144,168},{168,0... | collective-permute-start | bytes 811016 | tf_op jit(solution)/shard_map/ppermute | solution.py:172
  38.5 26.0 %collective-permute-start.8 = (bf16[224,4224]{1,0:T(8,128)(2,1)S(1)}, bf16[224,4224]{1,0:T(8,128)(2,1)S(1)}, u32[]{:S(2)}, u32[]{:S(2)}) collective-permute-start(bf16[224,4224]{1,0:T(8,128)(2,1)S(1)} %constant_dynamic-update-slice_fusion), channel_id=1, source_target_pairs={{0,12},{12,0},{1,13},{13,1},{2,14},{14,2},{3,15},{15,3},{4,16},{16... | collective-permute-start | bytes 5677064 | tf_op jit(solution)/shard_map/ppermute | solution.py:175
  50.4 7.1 %collective-permute-start.7 = (bf16[16,4224]{1,0:T(8,128)(2,1)S(1)}, bf16[16,4224]{1,0:T(8,128)(2,1)S(1)}, u32[]{:S(2)}, u32[]{:S(2)}) collective-permute-start(bf16[16,4224]{1,0:T(8,128)(2,1)S(1)} %slice.9), channel_id=1, source_target_pairs={{0,168},{24,0},{48,24},{72,48},{96,72},{120,96},{144,120},{168,144... | collective-permute-start | bytes 405512 | tf_op jit(solution)/shard_map/ppermute | solution.py:174
  52.3 8.3 %collective-permute-start.6 = (bf16[16,4224]{1,0:T(8,128)(2,1)S(1)}, bf16[16,4224]{1,0:T(8,128)(2,1)S(1)}, u32[]{:S(2)}, u32[]{:S(2)}) collective-permute-start(bf16[16,4224]{1,0:T(8,128)(2,1)S(1)} %slice.8), channel_id=1, source_target_pairs={{0,24},{24,48},{48,72},{72,96},{96,120},{120,144},{144,168},{168,0... | collective-permute-start | bytes 405512 | tf_op jit(solution)/shard_map/ppermute | solution.py:174
  60.6 3.9 %collective-permute-start.9 = (bf16[32,4224]{1,0:T(8,128)(2,1)S(1)}, bf16[32,4224]{1,0:T(8,128)(2,1)S(1)}, u32[]{:S(2)}, u32[]{:S(2)}) collective-permute-start(bf16[32,4224]{1,0:T(8,128)(2,1)S(1)} %pad_maximum_fusion), channel_id=1, source_target_pairs={{0,12},{12,0},{1,13},{13,1},{2,14},{14,2},{3,15},{15,3},{4,16},{16... | collective-permute-start | bytes 811016 | tf_op jit(solution)/shard_map/ppermute | solution.py:175
  64.5 44.2 %copy-start.3 = (s32[32,8]{0,1:T(8,128)S(1)}, s32[32,8]{0,1:T(8,128)}, u32[]{:S(2)}) copy-start(s32[32,8]{0,1:T(8,128)} %param.9) | copy-start | bytes 3076
  64.5 44.9 %copy-start.1 = (f32[1024,2,128]{2,1,0:T(2,128)S(1)}, f32[1024,2,128]{2,1,0:T(2,128)}, u32[]{:S(2)}) copy-start(f32[1024,2,128]{2,1,0:T(2,128)} %param.13) | copy-start | bytes 3145732
  64.5 44.9 %copy-start.2 = (bf16[1024,2,128]{2,1,0:T(2,128)(2,1)S(1)}, bf16[1024,2,128]{2,1,0:T(2,128)(2,1)}, u32[]{:S(2)}) copy-start(bf16[1024,2,128]{2,1,0:T(2,128)(2,1)} %param.12) | copy-start | bytes 1572868
  69.1 40.3 %collective-permute-start.10 = (bf16[1024,256]{1,0:T(8,128)(2,1)S(1)}, bf16[1024,256]{1,0:T(8,128)(2,1)S(1)}, u32[]{:S(2)}, u32[]{:S(2)}) collective-permute-start(bf16[1024,256]{1,0:T(8,128)(2,1)S(1)} %get-tuple-element.17), channel_id=1, source_target_pairs={{0,192},{192,384},{384,576},{576,0},{1,193},{193,385},{385,577},{5... | collective-permute-start | bytes 1572872 | tf_op jit(solution)/shard_map/ppermute | solution.py:210
  71.0 38.3 %collective-permute-start.11 = (bf16[1024,256]{1,0:T(8,128)(2,1)S(1)}, bf16[1024,256]{1,0:T(8,128)(2,1)S(1)}, u32[]{:S(2)}, u32[]{:S(2)}) collective-permute-start(bf16[1024,256]{1,0:T(8,128)(2,1)S(1)} %get-tuple-element.18), channel_id=1, source_target_pairs={{0,384},{192,576},{384,0},{576,192},{1,385},{193,577},{385,1},{577... | collective-permute-start | bytes 1572872 | tf_op jit(solution)/shard_map/ppermute | solution.py:210
  73.0 36.4 %collective-permute-start.12 = (bf16[1024,256]{1,0:T(8,128)(2,1)S(1)}, bf16[1024,256]{1,0:T(8,128)(2,1)S(1)}, u32[]{:S(2)}, u32[]{:S(2)}) collective-permute-start(bf16[1024,256]{1,0:T(8,128)(2,1)S(1)} %get-tuple-element.19), channel_id=1, source_target_pairs={{0,576},{192,0},{384,192},{576,384},{1,577},{193,1},{385,193},{577... | collective-permute-start | bytes 1572872 | tf_op jit(solution)/shard_map/ppermute | solution.py:210

commit v5 on v4

--- a/solution.py
+++ b/solution.py
@@ -101,9 +101,11 @@
             total = jnp.sum(prod[:, e * LANES : (e + 1) * LANES], axis=1, keepdims=True)
             spread = jnp.where(lane == e * tokens + tok, total, spread)
         order = lax.broadcasted_iota(jnp.int32, (2 * blocks, count), 1) // tokens
-        away = jnp.where(order % 2 == 1, -((order + 1) // 2), order // 2)
+        away = jnp.zeros_like(order)
+        for place, step in enumerate(arrival(blocks)):
+            away = jnp.where(order == place, step, away)
         row = lax.broadcasted_iota(jnp.int32, (2 * blocks, count), 0)
-        pick = ((line + away + blocks) % blocks * 2 + side == row).astype(F32)
+        pick = ((line + away) % blocks * 2 + side == row).astype(F32)
         piece = dot(pick, spread, (1, 0), lax.Precision.HIGHEST)
         gates_out = piece if gates_out is None else gates_out + piece
     for group in range(2 * blocks):
@@ -123,7 +125,7 @@
     steps = [0]
     for away in range(1, blocks // 2):
         steps += [blocks - away, away]
-    return steps + [blocks // 2]
+    return steps[:-2] + [blocks // 2] + steps[-2:]
 
 
 def home_kernel(tokens, planes, arrived, ids, out):
@@ -162,16 +164,19 @@
 
 
 def gathered(own):
-    size, half = lax.axis_size("ey"), own.shape[0] // 2
-    ahead = [(i, (i + 1) % size) for i in range(size)]
-    back = [(i, (i - 1) % size) for i in range(size)]
+    size = lax.axis_size("ey")
+
+    def turn(block, by):
+        return lax.ppermute(block, "ey", [(i, (i + by) % size) for i in range(size)])
+
+    up, down = turn(own, 1), turn(own, -1)
+    far = turn(own, size // 2)
+    mine = [own, up, down]
+    for _ in range(2, size // 2 - 1):
+        up, down = turn(up, 1), turn(down, -1)
+        mine += [up, down]
+    last = [far, turn(up, 1), turn(down, -1)]
     swap = [(0, 1), (1, 0)]
-    mine = [own]
-    up = down = own
-    for _ in range(1, size // 2):
-        up, down = lax.ppermute(up, "ey", ahead), lax.ppermute(down, "ey", back)
-        mine += [up, down]
-    last = [lax.ppermute(up[:half], "ey", ahead), lax.ppermute(down[half:], "ey", back)]
     theirs = [lax.ppermute(jnp.concatenate(g, axis=0), "core", swap) for g in (mine, last)]
     return mine + last + theirs
 

time: 113 us -> 114 us (level)
  starting transfers between devices: 49.9 us -> 46.2 us
  blocking collectives: 31.1 us -> 34.1 us
  waiting for transfers between devices: 19.4 us -> 22.1 us
    ppermute x2, starting transfers between devices: 14.6 us -> 7.98 us  [gathered(): lax.ppermute(jnp.concatenate(g, axis=0), 'core', swap)]
    all_to_all x1, blocking collectives: 31.1 us -> 34.1 us  [shards(): lax.all_to_all(gate_part, ('ey', 'core', 'tensor'), 0, 0, tiled=True)]
    ppermute x3, starting transfers between devices: 8.41 us -> 10.5 us  [shards(): grads[step] = lax.ppermute(grads[step], 'edata', to_owner)]
    ppermute x8 -> x7, waiting for transfers between devices: 18.3 us -> 20.1 us  [turn(): lax.ppermute(block, 'ey', [(i, (i + by) % size) for i in range(size)])]
    ppermute x8 -> x7, starting transfers between devices: 26.9 us -> 27.7 us  [turn(): lax.ppermute(block, 'ey', [(i, (i + by) % size) for i in range(size)])]
  transfers between devices with their start and end apart: 13 -> 12, of which waited for: 7 -> 4; matrix products, arithmetic and copies ran while one was open for 0% -> 0% of each run, Pallas kernels for 1% -> 1%
where the time goes in v5:
time: 114 us
  starting transfers between devices  46.2 us (41%)
  blocking collectives  34.1 us (30%)
  waiting for transfers between devices  22.1 us (19%)
  Pallas kernels  7.77 us (7%)
  local copies, waits for them, and re-layouts  2.06 us (2%)
    all_to_all x1, blocking collectives, shards(): lax.all_to_all(gate_part, ('ey', 'core', 'tensor'), 0, 0, tiled=True)  34.1 us
    ppermute x7, starting transfers between devices, turn(): lax.ppermute(block, 'ey', [(i, (i + by) % size) for i in range(size)])  27.7 us
    ppermute x7, waiting for transfers between devices, turn(): lax.ppermute(block, 'ey', [(i, (i + by) % size) for i in range(size)])  20.1 us
    ppermute x3, starting transfers between devices, shards(): grads[step] = lax.ppermute(grads[step], 'edata', to_owner)  10.5 us
    ppermute x2, starting transfers between devices, gathered(): lax.ppermute(jnp.concatenate(g, axis=0), 'core', swap)  7.98 us
    pallas_call x1, Pallas kernels, shards(): pl.pallas_call(functools.partial(own_kernel, tokens, rows, width, planes,...  4.56 us
    pallas_call x1, Pallas kernels, shards(): pl.pallas_call(functools.partial(adam_kernel, part, replicas), out_shape=...  2.51 us
  transfers between devices with their start and end apart: 12, of which 4 were waited for; matrix products, arithmetic and copies ran while one was open for 0% of the time, Pallas kernels for 1%

profile of v5, /device:TPU:1, one launch (start us, length us, event | category | flops | bytes accessed | tf_op | source)
XLA Modules:
  0.0 113.8 jit_solution(7255125039270257467)
XLA Ops:
  0.6 0.7 convert_element_type.3
  1.3 0.1 copy.14
  1.4 0.8 copy.15
  2.2 1.0 concatenate.9.refs_0_
  3.2 8.3 %collective-permute-start.4 = (bf16[32,4224]{1,0:T(8,128)(2,1)S(1)}, bf16[32,4224]{1,0:T(8,128)(2,1)S(1)}, u32[]{:S(2)}, u32[]{:S(2)}) collective-permute-start(bf16[32,4224]{1,0:T(8,128)(2,1)S(1)} %concatenate.9.refs_0_), channel_id=1, source_target_pairs={{0,96},{24,120},{48,144},{72,168},{96,0},{120,24},{144,48},{168,72... | collective-permute-start | bytes 811016 | tf_op jit(solution)/shard_map/ppermute | solution.py:170
  11.5 2.1 %collective-permute-start.1 = (bf16[32,4224]{1,0:T(8,128)(2,1)S(1)}, bf16[32,4224]{1,0:T(8,128)(2,1)S(1)}, u32[]{:S(2)}, u32[]{:S(2)}) collective-permute-start(bf16[32,4224]{1,0:T(8,128)(2,1)S(1)} %concatenate.9.refs_0_), channel_id=1, source_target_pairs={{0,168},{24,0},{48,24},{72,48},{96,72},{120,96},{144,120},{168,144... | collective-permute-start | bytes 811016 | tf_op jit(solution)/shard_map/ppermute | solution.py:170
  13.6 3.2 %collective-permute-start = (bf16[32,4224]{1,0:T(8,128)(2,1)S(1)}, bf16[32,4224]{1,0:T(8,128)(2,1)S(1)}, u32[]{:S(2)}, u32[]{:S(2)}) collective-permute-start(bf16[32,4224]{1,0:T(8,128)(2,1)S(1)} %concatenate.9.refs_0_), channel_id=1, source_target_pairs={{0,24},{24,48},{48,72},{72,96},{96,120},{120,144},{144,168},{168,0... | collective-permute-start | bytes 811016 | tf_op jit(solution)/shard_map/ppermute | solution.py:170
  16.8 12.9 %collective-permute-done.1.refs_2_ = bf16[32,4224]{1,0:T(8,128)(2,1)S(1)} collective-permute-done((bf16[32,4224]{1,0:T(8,128)(2,1)S(1)}, bf16[32,4224]{1,0:T(8,128)(2,1)S(1)}, u32[]{:S(2)}, u32[]{:S(2)}) %collective-permute-start.1) | collective-permute-done | bytes 270368 | tf_op jit(solution)/shard_map/ppermute | solution.py:170
  29.7 5.0 %collective-permute-start.3 = (bf16[32,4224]{1,0:T(8,128)(2,1)S(1)}, bf16[32,4224]{1,0:T(8,128)(2,1)S(1)}, u32[]{:S(2)}, u32[]{:S(2)}) collective-permute-start(bf16[32,4224]{1,0:T(8,128)(2,1)S(1)} %collective-permute-done.1.refs_2_), channel_id=1, source_target_pairs={{0,168},{24,0},{48,24},{72,48},{96,72},{120,96},{144,120},{168,144... | collective-permute-start | bytes 811016 | tf_op jit(solution)/shard_map/ppermute | solution.py:170
  34.7 0.0 collective-permute-done.refs_1_
  34.7 1.9 %collective-permute-start.2 = (bf16[32,4224]{1,0:T(8,128)(2,1)S(1)}, bf16[32,4224]{1,0:T(8,128)(2,1)S(1)}, u32[]{:S(2)}, u32[]{:S(2)}) collective-permute-start(bf16[32,4224]{1,0:T(8,128)(2,1)S(1)} %collective-permute-done.refs_1_), channel_id=1, source_target_pairs={{0,24},{24,48},{48,72},{72,96},{96,120},{120,144},{144,168},{168,0... | collective-permute-start | bytes 811016 | tf_op jit(solution)/shard_map/ppermute | solution.py:170
  36.7 0.0 copy-start
  36.7 0.0 copy-start.4
  36.7 3.3 %collective-permute-done.3.refs_4_ = bf16[32,4224]{1,0:T(8,128)(2,1)S(1)} collective-permute-done((bf16[32,4224]{1,0:T(8,128)(2,1)S(1)}, bf16[32,4224]{1,0:T(8,128)(2,1)S(1)}, u32[]{:S(2)}, u32[]{:S(2)}) %collective-permute-start.3) | collective-permute-done | bytes 270368 | tf_op jit(solution)/shard_map/ppermute | solution.py:170
  40.0 5.3 %collective-permute-start.6 = (bf16[32,4224]{1,0:T(8,128)(2,1)S(1)}, bf16[32,4224]{1,0:T(8,128)(2,1)S(1)}, u32[]{:S(2)}, u32[]{:S(2)}) collective-permute-start(bf16[32,4224]{1,0:T(8,128)(2,1)S(1)} %collective-permute-done.3.refs_4_), channel_id=1, source_target_pairs={{0,168},{24,0},{48,24},{72,48},{96,72},{120,96},{144,120},{168,144... | collective-permute-start | bytes 811016 | tf_op jit(solution)/shard_map/ppermute | solution.py:170
  45.4 0.0 collective-permute-done.2.refs_3_
  45.4 1.9 %collective-permute-start.5 = (bf16[32,4224]{1,0:T(8,128)(2,1)S(1)}, bf16[32,4224]{1,0:T(8,128)(2,1)S(1)}, u32[]{:S(2)}, u32[]{:S(2)}) collective-permute-start(bf16[32,4224]{1,0:T(8,128)(2,1)S(1)} %collective-permute-done.2.refs_3_), channel_id=1, source_target_pairs={{0,24},{24,48},{48,72},{72,96},{96,120},{120,144},{144,168},{168,0... | collective-permute-start | bytes 811016 | tf_op jit(solution)/shard_map/ppermute | solution.py:170
  47.4 3.5 %collective-permute-start.7 = (bf16[160,4224]{1,0:T(8,128)(2,1)S(1)}, bf16[160,4224]{1,0:T(8,128)(2,1)S(1)}, u32[]{:S(2)}, u32[]{:S(2)}) collective-permute-start(bf16[160,4224]{1,0:T(8,128)(2,1)S(1)} %constant_dynamic-update-slice_fusion), channel_id=1, source_target_pairs={{0,12},{12,0},{1,13},{13,1},{2,14},{14,2},{3,15},{15,3},{4,16},{16... | collective-permute-start | bytes 4055048 | tf_op jit(solution)/shard_map/ppermute | solution.py:180
  50.9 0.0 collective-permute-done.4.refs_5_
  50.9 0.0 collective-permute-done.6.refs_7_
  50.9 3.9 %collective-permute-done.5.refs_6_ = bf16[32,4224]{1,0:T(8,128)(2,1)S(1)} collective-permute-done((bf16[32,4224]{1,0:T(8,128)(2,1)S(1)}, bf16[32,4224]{1,0:T(8,128)(2,1)S(1)}, u32[]{:S(2)}, u32[]{:S(2)}) %collective-permute-start.5) | collective-permute-done | bytes 270368 | tf_op jit(solution)/shard_map/ppermute | solution.py:170
  54.8 0.1 pad_maximum_fusion
  54.9 4.4 %collective-permute-start.8 = (bf16[96,4224]{1,0:T(8,128)(2,1)S(1)}, bf16[96,4224]{1,0:T(8,128)(2,1)S(1)}, u32[]{:S(2)}, u32[]{:S(2)}) collective-permute-start(bf16[96,4224]{1,0:T(8,128)(2,1)S(1)} %pad_maximum_fusion), channel_id=1, source_target_pairs={{0,12},{12,0},{1,13},{13,1},{2,14},{14,2},{3,15},{15,3},{4,16},{16... | collective-permute-start | bytes 2433032 | tf_op jit(solution)/shard_map/ppermute | solution.py:180
  59.4 1.9 %collective-permute-done.8.refs_9_ = bf16[96,4224]{1,0:T(8,128)(2,1)S(1)} collective-permute-done((bf16[96,4224]{1,0:T(8,128)(2,1)S(1)}, bf16[96,4224]{1,0:T(8,128)(2,1)S(1)}, u32[]{:S(2)}, u32[]{:S(2)}) %collective-permute-start.8) | collective-permute-done | bytes 811040 | tf_op jit(solution)/shard_map/ppermute | solution.py:180
  61.3 0.0 collective-permute-done.7.refs_8_
  61.3 0.0 copy-done
  61.3 0.0 copy-done.4
  61.3 0.0 copy-start.3
  61.3 0.0 copy-start.1
  61.3 0.0 copy-start.2
  61.3 4.6 %own_tokens.1 = (bf16[8,2,24,128]{3,2,1,0:T(8,128)(2,1)}, f32[192,1,64]{2,1,0:T(1,128)S(1)}, bf16[1024,256]{1,0:T(8,128)(2,1)S(1)}, bf16[1024,256]{1,0:T(8,128)(...) custom-call(bf16[32,4224]{1,0:T(8,128)(2,1)S(1)} %concatenate.9.refs_0_, ...), custom_call_target="tpu_custom_call" | custom-call | flops 2147483648 | bytes 8388608 | tf_op jit(solution)/shard_map/own_tokens/pallas_call | solution.py:200
  65.9 3.1 %collective-permute-start.9 = (bf16[1024,256]{1,0:T(8,128)(2,1)S(1)}, bf16[1024,256]{1,0:T(8,128)(2,1)S(1)}, u32[]{:S(2)}, u32[]{:S(2)}) collective-permute-start(bf16[1024,256]{1,0:T(8,128)(2,1)S(1)} %get-tuple-element.17), channel_id=1, source_target_pairs={{0,192},{192,384},{384,576},{576,0},{1,193},{193,385},{385,577},{5... | collective-permute-start | bytes 1572872 | tf_op jit(solution)/shard_map/ppermute | solution.py:215
  69.0 4.4 %collective-permute-start.10 = (bf16[1024,256]{1,0:T(8,128)(2,1)S(1)}, bf16[1024,256]{1,0:T(8,128)(2,1)S(1)}, u32[]{:S(2)}, u32[]{:S(2)}) collective-permute-start(bf16[1024,256]{1,0:T(8,128)(2,1)S(1)} %get-tuple-element.18), channel_id=1, source_target_pairs={{0,384},{192,576},{384,0},{576,192},{1,385},{193,577},{385,1},{577... | collective-permute-start | bytes 1572872 | tf_op jit(solution)/shard_map/ppermute | solution.py:215
  73.4 3.1 %collective-permute-start.11 = (bf16[1024,256]{1,0:T(8,128)(2,1)S(1)}, bf16[1024,256]{1,0:T(8,128)(2,1)S(1)}, u32[]{:S(2)}, u32[]{:S(2)}) collective-permute-start(bf16[1024,256]{1,0:T(8,128)(2,1)S(1)} %get-tuple-element.19), channel_id=1, source_target_pairs={{0,576},{192,0},{384,192},{576,384},{1,577},{193,1},{385,193},{577... | collective-permute-start | bytes 1572872 | tf_op jit(solution)/shard_map/ppermute | solution.py:215
  76.4 34.1 %all_to_all.5.arrived = f32[192,1,64]{2,1,0:T(1,128)S(1)} all-to-all(f32[192,1,64]{2,1,0:T(1,128)S(1)} %get-tuple-element.15), channel_id=1, replica_groups=mesh['edata'=4,'ey'=8,'core'=2,'tensor'=12] {'ey','core','tensor'}, dimensions={0} | all-to-all | bytes 98304 | tf_op jit(solution)/shard_map/all_to_all | solution.py:216
  110.6 0.0 copy-done.3
  110.6 0.7 gates_home.1
  111.3 0.0 collective-permute-done.9.refs_1_
  111.3 0.0 collective-permute-done.10.refs_2_
  111.3 0.0 collective-permute-done.11.refs_3_
  111.3 0.0 copy-done.1
  111.3 0.0 copy-done.2
  111.3 2.5 %adam.1 = (bf16[2048,128]{1,0:T(8,128)(2,1)}, bf16[2048,128]{1,0:T(8,128)(2,1)}, f32[2048,128]{1,0:T(8,128)}) custom-call(bf16[1024,256]{1,0:T(8,128)(2,1)S(1)} %get-tuple-element.16.refs_0_, bf16[1024,256]{1,0:T(8,128)(2,1)S(1)} %collective-permute-done.9.refs_1_, bf16[1024,256]{1,0:T(8,128)(2,1)S(1)} %collective-permute-done.10.refs_2_, ...), custom_call_target="tpu_custom_call" | custom-call | flops 524288 | bytes 8388608 | tf_op jit(solution)/shard_map/adam/pallas_call | solution.py:225
  (6 shorter events, 0.1 us)
Async XLA Ops:
  3.2 47.7 %collective-permute-start.4 = (bf16[32,4224]{1,0:T(8,128)(2,1)S(1)}, bf16[32,4224]{1,0:T(8,128)(2,1)S(1)}, u32[]{:S(2)}, u32[]{:S(2)}) collective-permute-start(bf16[32,4224]{1,0:T(8,128)(2,1)S(1)} %concatenate.9.refs_0_), channel_id=1, source_target_pairs={{0,96},{24,120},{48,144},{72,168},{96,0},{120,24},{144,48},{168,72... | collective-permute-start | bytes 811016 | tf_op jit(solution)/shard_map/ppermute | solution.py:170
  11.5 18.2 %collective-permute-start.1 = (bf16[32,4224]{1,0:T(8,128)(2,1)S(1)}, bf16[32,4224]{1,0:T(8,128)(2,1)S(1)}, u32[]{:S(2)}, u32[]{:S(2)}) collective-permute-start(bf16[32,4224]{1,0:T(8,128)(2,1)S(1)} %concatenate.9.refs_0_), channel_id=1, source_target_pairs={{0,168},{24,0},{48,24},{72,48},{96,72},{120,96},{144,120},{168,144... | collective-permute-start | bytes 811016 | tf_op jit(solution)/shard_map/ppermute | solution.py:170
  13.6 21.1 %collective-permute-start = (bf16[32,4224]{1,0:T(8,128)(2,1)S(1)}, bf16[32,4224]{1,0:T(8,128)(2,1)S(1)}, u32[]{:S(2)}, u32[]{:S(2)}) collective-permute-start(bf16[32,4224]{1,0:T(8,128)(2,1)S(1)} %concatenate.9.refs_0_), channel_id=1, source_target_pairs={{0,24},{24,48},{48,72},{72,96},{96,120},{120,144},{144,168},{168,0... | collective-permute-start | bytes 811016 | tf_op jit(solution)/shard_map/ppermute | solution.py:170
  29.7 10.3 %collective-permute-start.3 = (bf16[32,4224]{1,0:T(8,128)(2,1)S(1)}, bf16[32,4224]{1,0:T(8,128)(2,1)S(1)}, u32[]{:S(2)}, u32[]{:S(2)}) collective-permute-start(bf16[32,4224]{1,0:T(8,128)(2,1)S(1)} %collective-permute-done.1.refs_2_), channel_id=1, source_target_pairs={{0,168},{24,0},{48,24},{72,48},{96,72},{120,96},{144,120},{168,144... | collective-permute-start | bytes 811016 | tf_op jit(solution)/shard_map/ppermute | solution.py:170
  34.7 10.6 %collective-permute-start.2 = (bf16[32,4224]{1,0:T(8,128)(2,1)S(1)}, bf16[32,4224]{1,0:T(8,128)(2,1)S(1)}, u32[]{:S(2)}, u32[]{:S(2)}) collective-permute-start(bf16[32,4224]{1,0:T(8,128)(2,1)S(1)} %collective-permute-done.refs_1_), channel_id=1, source_target_pairs={{0,24},{24,48},{48,72},{72,96},{96,120},{120,144},{144,168},{168,0... | collective-permute-start | bytes 811016 | tf_op jit(solution)/shard_map/ppermute | solution.py:170
  36.7 24.6 %copy-start = (bf16[2,128,4096]{2,1,0:T(8,128)(2,1)S(1)}, bf16[2,128,4096]{2,1,0:T(8,128)(2,1)}, u32[]{:S(2)}) copy-start(bf16[2,128,4096]{2,1,0:T(8,128)(2,1)} %param.11) | copy-start | bytes 6291460
  36.7 24.6 %copy-start.4 = (bf16[1,16,2,12,128]{4,2,3,1,0:T(2,128)(2,1)S(1)}, bf16[1,16,2,12,128]{4,2,3,1,0:T(2,128)(2,1)}, u32[]{:S(2)}) copy-start(bf16[1,16,2,12,128]{4,2,3,1,0:T(2,128)(2,1)} %param.10) | copy-start | bytes 294916
  40.0 10.9 %collective-permute-start.6 = (bf16[32,4224]{1,0:T(8,128)(2,1)S(1)}, bf16[32,4224]{1,0:T(8,128)(2,1)S(1)}, u32[]{:S(2)}, u32[]{:S(2)}) collective-permute-start(bf16[32,4224]{1,0:T(8,128)(2,1)S(1)} %collective-permute-done.3.refs_4_), channel_id=1, source_target_pairs={{0,168},{24,0},{48,24},{72,48},{96,72},{120,96},{144,120},{168,144... | collective-permute-start | bytes 811016 | tf_op jit(solution)/shard_map/ppermute | solution.py:170
  45.4 9.5 %collective-permute-start.5 = (bf16[32,4224]{1,0:T(8,128)(2,1)S(1)}, bf16[32,4224]{1,0:T(8,128)(2,1)S(1)}, u32[]{:S(2)}, u32[]{:S(2)}) collective-permute-start(bf16[32,4224]{1,0:T(8,128)(2,1)S(1)} %collective-permute-done.2.refs_3_), channel_id=1, source_target_pairs={{0,24},{24,48},{48,72},{72,96},{96,120},{120,144},{144,168},{168,0... | collective-permute-start | bytes 811016 | tf_op jit(solution)/shard_map/ppermute | solution.py:170
  47.4 13.9 %collective-permute-start.7 = (bf16[160,4224]{1,0:T(8,128)(2,1)S(1)}, bf16[160,4224]{1,0:T(8,128)(2,1)S(1)}, u32[]{:S(2)}, u32[]{:S(2)}) collective-permute-start(bf16[160,4224]{1,0:T(8,128)(2,1)S(1)} %constant_dynamic-update-slice_fusion), channel_id=1, source_target_pairs={{0,12},{12,0},{1,13},{13,1},{2,14},{14,2},{3,15},{15,3},{4,16},{16... | collective-permute-start | bytes 4055048 | tf_op jit(solution)/shard_map/ppermute | solution.py:180
  54.9 6.4 %collective-permute-start.8 = (bf16[96,4224]{1,0:T(8,128)(2,1)S(1)}, bf16[96,4224]{1,0:T(8,128)(2,1)S(1)}, u32[]{:S(2)}, u32[]{:S(2)}) collective-permute-start(bf16[96,4224]{1,0:T(8,128)(2,1)S(1)} %pad_maximum_fusion), channel_id=1, source_target_pairs={{0,12},{12,0},{1,13},{13,1},{2,14},{14,2},{3,15},{15,3},{4,16},{16... | collective-permute-start | bytes 2433032 | tf_op jit(solution)/shard_map/ppermute | solution.py:180
  61.3 49.3 %copy-start.3 = (s32[32,8]{0,1:T(8,128)S(1)}, s32[32,8]{0,1:T(8,128)}, u32[]{:S(2)}) copy-start(s32[32,8]{0,1:T(8,128)} %param.9) | copy-start | bytes 3076
  61.3 50.0 %copy-start.1 = (f32[1024,2,128]{2,1,0:T(2,128)S(1)}, f32[1024,2,128]{2,1,0:T(2,128)}, u32[]{:S(2)}) copy-start(f32[1024,2,128]{2,1,0:T(2,128)} %param.13) | copy-start | bytes 3145732
  61.3 50.0 %copy-start.2 = (bf16[1024,2,128]{2,1,0:T(2,128)(2,1)S(1)}, bf16[1024,2,128]{2,1,0:T(2,128)(2,1)}, u32[]{:S(2)}) copy-start(bf16[1024,2,128]{2,1,0:T(2,128)(2,1)} %param.12) | copy-start | bytes 1572868
  65.9 45.4 %collective-permute-start.9 = (bf16[1024,256]{1,0:T(8,128)(2,1)S(1)}, bf16[1024,256]{1,0:T(8,128)(2,1)S(1)}, u32[]{:S(2)}, u32[]{:S(2)}) collective-permute-start(bf16[1024,256]{1,0:T(8,128)(2,1)S(1)} %get-tuple-element.17), channel_id=1, source_target_pairs={{0,192},{192,384},{384,576},{576,0},{1,193},{193,385},{385,577},{5... | collective-permute-start | bytes 1572872 | tf_op jit(solution)/shard_map/ppermute | solution.py:215
  69.0 42.3 %collective-permute-start.10 = (bf16[1024,256]{1,0:T(8,128)(2,1)S(1)}, bf16[1024,256]{1,0:T(8,128)(2,1)S(1)}, u32[]{:S(2)}, u32[]{:S(2)}) collective-permute-start(bf16[1024,256]{1,0:T(8,128)(2,1)S(1)} %get-tuple-element.18), channel_id=1, source_target_pairs={{0,384},{192,576},{384,0},{576,192},{1,385},{193,577},{385,1},{577... | collective-permute-start | bytes 1572872 | tf_op jit(solution)/shard_map/ppermute | solution.py:215
  73.4 37.9 %collective-permute-start.11 = (bf16[1024,256]{1,0:T(8,128)(2,1)S(1)}, bf16[1024,256]{1,0:T(8,128)(2,1)S(1)}, u32[]{:S(2)}, u32[]{:S(2)}) collective-permute-start(bf16[1024,256]{1,0:T(8,128)(2,1)S(1)} %get-tuple-element.19), channel_id=1, source_target_pairs={{0,576},{192,0},{384,192},{576,384},{1,577},{193,1},{385,193},{577... | collective-permute-start | bytes 1572872 | tf_op jit(solution)/shard_map/ppermute | solution.py:215

commit v6 on v5

--- a/solution.py
+++ b/solution.py
@@ -16,7 +16,7 @@
 F32 = jnp.float32
 BF16 = jnp.bfloat16
 LANES = 128
-PARAMS = pltpu.CompilerParams(vmem_limit_bytes=40 * 1024 * 1024)
+PARAMS = pltpu.CompilerParams(vmem_limit_bytes=24 * 1024 * 1024)
 
 
 def dot(a, b, over, precision=None):
@@ -65,6 +65,21 @@
     return jnp.concatenate([jnp.broadcast_to(g, (g.shape[0], LANES)) for g in gate], axis=1)
 
 
+def pack_kernel(rows_in, ids, gates, out):
+    width, tokens = rows_in.shape[1], rows_in.shape[0]
+    out[:, :width] = rows_in[...]
+    turned = jnp.concatenate([ids[...].astype(F32), gates[...].astype(F32)], axis=0)
+    turned = jnp.concatenate([turned, jnp.zeros((turned.shape[0], LANES - tokens), F32)], axis=1)
+    turned = jnp.concatenate([turned, jnp.zeros((tokens - turned.shape[0], LANES), F32)], axis=0)
+    out[:, width:] = turned.astype(BF16)
+
+
+def by_token(meta, tokens):
+    meta = meta.astype(F32)
+    blocks = [meta[at : at + tokens, :].T for at in range(0, meta.shape[0], tokens)]
+    return jnp.concatenate([block[:tokens, :] for block in blocks], axis=0)
+
+
 def own_kernel(tokens, rows, width, planes, pieces, *refs):
     weight, hid, grad_hidden, gate_part = refs[pieces : pieces + 4]
     grads, toks = refs[pieces + 4 : -1], refs[-1]
@@ -82,7 +97,7 @@
     for rel in range(2):
         side = core if rel == 0 else 1 - core
         here = slice(rel * count, (rel + 1) * count)
-        onehot, gate = routed(toks[here, width : width + LANES], base, tokens, rows)
+        onehot, gate = routed(by_token(toks[here, width : width + LANES], tokens), base, tokens, rows)
         slots = jnp.concatenate([hid[block, side].astype(F32) for block in where], axis=0)
         saved = dot(onehot, by_expert(slots), (1, 0))
         up = dot(toks[here, :width], weight[...], (1, 1))
@@ -170,11 +185,13 @@
         return lax.ppermute(block, "ey", [(i, (i + by) % size) for i in range(size)])
 
     up, down = turn(own, 1), turn(own, -1)
-    far = turn(own, size // 2)
     mine = [own, up, down]
     for _ in range(2, size // 2 - 1):
         up, down = turn(up, 1), turn(down, -1)
         mine += [up, down]
+    again, up, down = lax.optimization_barrier((own, up, down))
+    far = turn(again, size // 2)
+    mine[-2:] = [up, down]
     last = [far, turn(up, 1), turn(down, -1)]
     swap = [(0, 1), (1, 0)]
     theirs = [lax.ppermute(jnp.concatenate(g, axis=0), "core", swap) for g in (mine, last)]
@@ -191,10 +208,14 @@
     part = width // replicas
     every = groups * tokens
 
-    meta = jnp.concatenate(
-        [expert_ids.astype(BF16), gates, jnp.zeros((tokens, LANES - 2 * choices), BF16)], axis=1
-    )
-    toks = gathered(jnp.concatenate([grad_out, meta], axis=1))
+    toks = gathered(
+        pl.pallas_call(
+            pack_kernel,
+            out_shape=jax.ShapeDtypeStruct((tokens, width + LANES), BF16),
+            compiler_params=PARAMS,
+            name="pack",
+        )(grad_out, expert_ids.T, gates.T)
+    )
     saved = jnp.transpose(hidden[0], (0, 2, 1, 3)).reshape(groups // 2, 2, rows, LANES)
     weight = down_weight.reshape(held * LANES, width)
     grad_hidden, gate_part, *grads = pl.pallas_call(
@@ -214,13 +235,6 @@
         to_owner = [(i, (i + step) % replicas) for i in range(replicas)]
         grads[step] = lax.ppermute(grads[step], "edata", to_owner)
     gate_home = lax.all_to_all(gate_part, ("ey", "core", "tensor"), 0, 0, tiled=True)
-    grad_gates = pl.pallas_call(
-        functools.partial(home_kernel, tokens, planes),
-        out_shape=jax.ShapeDtypeStruct((choices, tokens), F32),
-        compiler_params=PARAMS,
-        name="gates_home",
-    )(gate_home, expert_ids.T).T
-
     flat = (part * held, LANES)
     new_weight, new_one, new_two = pl.pallas_call(
         functools.partial(adam_kernel, part, replicas),
@@ -234,6 +248,13 @@
         cost_estimate=cost(part, held * LANES, 8 << 20),
         name="adam",
     )(*grads, weight, moment_one.reshape(flat), moment_two.reshape(flat))
+    gate_home, new_one = lax.optimization_barrier((gate_home, new_one))
+    grad_gates = pl.pallas_call(
+        functools.partial(home_kernel, tokens, planes),
+        out_shape=jax.ShapeDtypeStruct((choices, tokens), F32),
+        compiler_params=PARAMS,
+        name="gates_home",
+    )(gate_home, expert_ids.T).T
     grad_hidden = jnp.transpose(
         grad_hidden.reshape(1, groups, capacity, held, LANES), (0, 1, 3, 2, 4)
     )

time: 114 us -> 111 us (0.974)
  blocking collectives: 34.1 us -> 0 us
  starting transfers between devices: 46.2 us -> 73.6 us
  local copies, waits for them, and re-layouts: 2.06 us -> 5.34 us
  Pallas kernels: 7.77 us -> 10.2 us
  waiting for transfers between devices: 22.1 us -> 20.7 us
    all_to_all x1 -> x0, blocking collectives: 34.1 us -> none  [shards(): lax.all_to_all(gate_part, ('ey', 'core', 'tensor'), 0, 0, tiled=True)]
    all_to_all x0 -> x1, starting transfers between devices: none -> 19 us  [shards(): lax.all_to_all(gate_part, ('ey', 'core', 'tensor'), 0, 0, tiled=True)]
    ppermute x2, starting transfers between devices: 7.98 us -> 19.1 us  [gathered(): lax.ppermute(jnp.concatenate(g, axis=0), 'core', swap)]
    ppermute x7, waiting for transfers between devices: 20.1 us -> 9.3 us  [turn(): lax.ppermute(block, 'ey', [(i, (i + by) % size) for i in range(size)])]
    all_to_all x0 -> x1, waiting for transfers between devices: none -> 6.92 us  [shards(): lax.all_to_all(gate_part, ('ey', 'core', 'tensor'), 0, 0, tiled=True)]
    unnamed x15 -> x24, local copies, waits for them, and re-layouts: 0.89 us -> 5.32 us
    ppermute x3, waiting for transfers between devices: 0.01 us -> 2.53 us  [shards(): grads[step] = lax.ppermute(grads[step], 'edata', to_owner)]
    ppermute x3, starting transfers between devices: 10.5 us -> 8.41 us  [shards(): grads[step] = lax.ppermute(grads[step], 'edata', to_owner)]
  transfers between devices with their start and end apart: 12 -> 13, of which waited for: 4 -> 7; matrix products, arithmetic and copies ran while one was open for 0% -> 0% of each run, Pallas kernels for 1% -> 3%
where the time goes in v6:
time: 111 us
  starting transfers between devices  73.6 us (66%)
  waiting for transfers between devices  20.7 us (19%)
  Pallas kernels  10.2 us (9%)
  local copies, waits for them, and re-layouts  5.34 us (5%)
    ppermute x7, starting transfers between devices, turn(): lax.ppermute(block, 'ey', [(i, (i + by) % size) for i in range(size)])  27.1 us
    ppermute x2, starting transfers between devices, gathered(): lax.ppermute(jnp.concatenate(g, axis=0), 'core', swap)  19.1 us
    all_to_all x1, starting transfers between devices, shards(): lax.all_to_all(gate_part, ('ey', 'core', 'tensor'), 0, 0, tiled=True)  19 us
    ppermute x7, waiting for transfers between devices, turn(): lax.ppermute(block, 'ey', [(i, (i + by) % size) for i in range(size)])  9.3 us
    ppermute x3, starting transfers between devices, shards(): grads[step] = lax.ppermute(grads[step], 'edata', to_owner)  8.41 us
    all_to_all x1, waiting for transfers between devices, shards(): lax.all_to_all(gate_part, ('ey', 'core', 'tensor'), 0, 0, tiled=True)  6.92 us
    pallas_call x1, Pallas kernels, shards(): pl.pallas_call(functools.partial(own_kernel, tokens, rows, width, planes,...  5.6 us
    unnamed x24, local copies, waits for them, and re-layouts  5.32 us
  transfers between devices with their start and end apart: 13, of which 7 were waited for; matrix products, arithmetic and copies ran while one was open for 0% of the time, Pallas kernels for 3%

profile of v6, /device:TPU:1, one launch (start us, length us, event | category | flops | bytes accessed | tf_op | source)
XLA Modules:
  0.0 110.7 jit_solution(10899059180806407114)
XLA Ops:
  0.6 0.0 copy-start.5
  0.6 0.9 copy-done.5
  1.6 0.0 copy-start.6
  1.6 0.7 copy-done.6
  2.3 0.0 copy-start.8
  2.3 0.7 copy-done.8
  3.0 5.9 %collective-permute-start.1 = (bf16[32,4224]{1,0:T(8,128)(2,1)S(1)}, bf16[32,4224]{1,0:T(8,128)(2,1)S(1)}, u32[]{:S(2)}, u32[]{:S(2)}) collective-permute-start(bf16[32,4224]{1,0:T(8,128)(2,1)S(1)} %pack.1.refs_0_), channel_id=1, source_target_pairs={{0,168},{24,0},{48,24},{72,48},{96,72},{120,96},{144,120},{168,144... | collective-permute-start | bytes 811016 | tf_op jit(solution)/shard_map/ppermute | solution.py:185
  8.9 1.9 %collective-permute-start = (bf16[32,4224]{1,0:T(8,128)(2,1)S(1)}, bf16[32,4224]{1,0:T(8,128)(2,1)S(1)}, u32[]{:S(2)}, u32[]{:S(2)}) collective-permute-start(bf16[32,4224]{1,0:T(8,128)(2,1)S(1)} %pack.1.refs_0_), channel_id=1, source_target_pairs={{0,24},{24,48},{48,72},{72,96},{96,120},{120,144},{144,168},{168,0... | collective-permute-start | bytes 811016 | tf_op jit(solution)/shard_map/ppermute | solution.py:185
  10.9 1.4 %collective-permute-done.1.refs_2_ = bf16[32,4224]{1,0:T(8,128)(2,1)S(1)} collective-permute-done((bf16[32,4224]{1,0:T(8,128)(2,1)S(1)}, bf16[32,4224]{1,0:T(8,128)(2,1)S(1)}, u32[]{:S(2)}, u32[]{:S(2)}) %collective-permute-start.1) | collective-permute-done | bytes 270368 | tf_op jit(solution)/shard_map/ppermute | solution.py:185
  12.3 5.0 %collective-permute-start.3 = (bf16[32,4224]{1,0:T(8,128)(2,1)S(1)}, bf16[32,4224]{1,0:T(8,128)(2,1)S(1)}, u32[]{:S(2)}, u32[]{:S(2)}) collective-permute-start(bf16[32,4224]{1,0:T(8,128)(2,1)S(1)} %collective-permute-done.1.refs_2_), channel_id=1, source_target_pairs={{0,168},{24,0},{48,24},{72,48},{96,72},{120,96},{144,120},{168,144... | collective-permute-start | bytes 811016 | tf_op jit(solution)/shard_map/ppermute | solution.py:185
  17.3 0.0 collective-permute-done.refs_1_
  17.3 1.9 %collective-permute-start.2 = (bf16[32,4224]{1,0:T(8,128)(2,1)S(1)}, bf16[32,4224]{1,0:T(8,128)(2,1)S(1)}, u32[]{:S(2)}, u32[]{:S(2)}) collective-permute-start(bf16[32,4224]{1,0:T(8,128)(2,1)S(1)} %collective-permute-done.refs_1_), channel_id=1, source_target_pairs={{0,24},{24,48},{48,72},{72,96},{96,120},{120,144},{144,168},{168,0... | collective-permute-start | bytes 811016 | tf_op jit(solution)/shard_map/ppermute | solution.py:185
  19.3 0.0 copy-start
  19.3 0.0 copy-start.9
  19.3 2.9 %collective-permute-done.3.refs_4_ = bf16[32,4224]{1,0:T(8,128)(2,1)S(1)} collective-permute-done((bf16[32,4224]{1,0:T(8,128)(2,1)S(1)}, bf16[32,4224]{1,0:T(8,128)(2,1)S(1)}, u32[]{:S(2)}, u32[]{:S(2)}) %collective-permute-start.3) | collective-permute-done | bytes 270368 | tf_op jit(solution)/shard_map/ppermute | solution.py:185
  22.2 5.0 %collective-permute-done.2.refs_3_ = bf16[32,4224]{1,0:T(8,128)(2,1)S(1)} collective-permute-done((bf16[32,4224]{1,0:T(8,128)(2,1)S(1)}, bf16[32,4224]{1,0:T(8,128)(2,1)S(1)}, u32[]{:S(2)}, u32[]{:S(2)}) %collective-permute-start.2) | collective-permute-done | bytes 270368 | tf_op jit(solution)/shard_map/ppermute | solution.py:185
  27.2 5.8 %collective-permute-start.4 = (bf16[32,4224]{1,0:T(8,128)(2,1)S(1)}, bf16[32,4224]{1,0:T(8,128)(2,1)S(1)}, u32[]{:S(2)}, u32[]{:S(2)}) collective-permute-start(bf16[32,4224]{1,0:T(8,128)(2,1)S(1)} %pack.1.refs_0_), channel_id=1, source_target_pairs={{0,96},{24,120},{48,144},{72,168},{96,0},{120,24},{144,48},{168,72... | collective-permute-start | bytes 811016 | tf_op jit(solution)/shard_map/ppermute | solution.py:185
  33.0 1.9 %collective-permute-start.5 = (bf16[32,4224]{1,0:T(8,128)(2,1)S(1)}, bf16[32,4224]{1,0:T(8,128)(2,1)S(1)}, u32[]{:S(2)}, u32[]{:S(2)}) collective-permute-start(bf16[32,4224]{1,0:T(8,128)(2,1)S(1)} %collective-permute-done.2.refs_3_), channel_id=1, source_target_pairs={{0,24},{24,48},{48,72},{72,96},{96,120},{120,144},{144,168},{168,0... | collective-permute-start | bytes 811016 | tf_op jit(solution)/shard_map/ppermute | solution.py:185
  35.0 4.6 %collective-permute-start.6 = (bf16[32,4224]{1,0:T(8,128)(2,1)S(1)}, bf16[32,4224]{1,0:T(8,128)(2,1)S(1)}, u32[]{:S(2)}, u32[]{:S(2)}) collective-permute-start(bf16[32,4224]{1,0:T(8,128)(2,1)S(1)} %collective-permute-done.3.refs_4_), channel_id=1, source_target_pairs={{0,168},{24,0},{48,24},{72,48},{96,72},{120,96},{144,120},{168,144... | collective-permute-start | bytes 811016 | tf_op jit(solution)/shard_map/ppermute | solution.py:185
  39.6 13.8 %collective-permute-start.7 = (bf16[160,4224]{1,0:T(8,128)(2,1)S(1)}, bf16[160,4224]{1,0:T(8,128)(2,1)S(1)}, u32[]{:S(2)}, u32[]{:S(2)}) collective-permute-start(bf16[160,4224]{1,0:T(8,128)(2,1)S(1)} %constant_dynamic-update-slice_fusion), channel_id=1, source_target_pairs={{0,12},{12,0},{1,13},{13,1},{2,14},{14,2},{3,15},{15,3},{4,16},{16... | collective-permute-start | bytes 4055048 | tf_op jit(solution)/shard_map/ppermute | solution.py:197
  53.4 0.0 collective-permute-done.4.refs_5_
  53.4 0.0 collective-permute-done.5.refs_6_
  53.4 0.0 collective-permute-done.6.refs_7_
  53.5 0.1 pad_maximum_fusion
  53.5 5.3 %collective-permute-start.8 = (bf16[96,4224]{1,0:T(8,128)(2,1)S(1)}, bf16[96,4224]{1,0:T(8,128)(2,1)S(1)}, u32[]{:S(2)}, u32[]{:S(2)}) collective-permute-start(bf16[96,4224]{1,0:T(8,128)(2,1)S(1)} %pad_maximum_fusion), channel_id=1, source_target_pairs={{0,12},{12,0},{1,13},{13,1},{2,14},{14,2},{3,15},{15,3},{4,16},{16... | collective-permute-start | bytes 2433032 | tf_op jit(solution)/shard_map/ppermute | solution.py:197
  58.8 1.9 %collective-permute-done.8.refs_9_ = bf16[96,4224]{1,0:T(8,128)(2,1)S(1)} collective-permute-done((bf16[96,4224]{1,0:T(8,128)(2,1)S(1)}, bf16[96,4224]{1,0:T(8,128)(2,1)S(1)}, u32[]{:S(2)}, u32[]{:S(2)}) %collective-permute-start.8) | collective-permute-done | bytes 811040 | tf_op jit(solution)/shard_map/ppermute | solution.py:197
  60.7 0.0 collective-permute-done.7.refs_8_
  60.7 0.0 copy-done
  60.7 0.0 copy-done.9
  60.8 0.0 copy-start.1
  60.8 5.6 %own_tokens.1 = (bf16[8,2,24,128]{3,2,1,0:T(8,128)(2,1)}, f32[192,1,64]{2,1,0:T(1,128)}, bf16[1024,256]{1,0:T(8,128)(2,1)S(1)}, bf16[1024,256]{1,0:T(8,128)(2,1)...) custom-call(bf16[32,4224]{1,0:T(8,128)(2,1)S(1)} %pack.1.refs_0_, ...), custom_call_target="tpu_custom_call" | custom-call | flops 2147483648 | bytes 8388608 | tf_op jit(solution)/shard_map/own_tokens/pallas_call | solution.py:221
  66.4 0.0 copy-start.3
  66.4 0.8 copy-done.3
  67.2 1.9 %collective-permute-start.9 = (bf16[1024,256]{1,0:T(8,128)(2,1)}, bf16[1024,256]{1,0:T(8,128)(2,1)}, u32[]{:S(2)}, u32[]{:S(2)}) collective-permute-start(bf16[1024,256]{1,0:T(8,128)(2,1)} %get-tuple-element.25), channel_id=1, source_target_pairs={{0,192},{192,384},{384,576},{576,0},{1,193},{193,385},{385,577},{5... | collective-permute-start | bytes 1572872 | tf_op jit(solution)/shard_map/ppermute | solution.py:236
  69.1 1.9 %collective-permute-start.10 = (bf16[1024,256]{1,0:T(8,128)(2,1)}, bf16[1024,256]{1,0:T(8,128)(2,1)}, u32[]{:S(2)}, u32[]{:S(2)}) collective-permute-start(bf16[1024,256]{1,0:T(8,128)(2,1)} %get-tuple-element.26), channel_id=1, source_target_pairs={{0,384},{192,576},{384,0},{576,192},{1,385},{193,577},{385,1},{577... | collective-permute-start | bytes 1572872 | tf_op jit(solution)/shard_map/ppermute | solution.py:236
  71.0 4.6 %collective-permute-start.11 = (bf16[1024,256]{1,0:T(8,128)(2,1)}, bf16[1024,256]{1,0:T(8,128)(2,1)}, u32[]{:S(2)}, u32[]{:S(2)}) collective-permute-start(bf16[1024,256]{1,0:T(8,128)(2,1)} %get-tuple-element.27), channel_id=1, source_target_pairs={{0,576},{192,0},{384,192},{576,384},{1,577},{193,1},{385,193},{577... | collective-permute-start | bytes 1572872 | tf_op jit(solution)/shard_map/ppermute | solution.py:236
  75.6 19.0 %all-to-all-start = ((f32[192,1,64]{2,1,0:T(1,128)}), f32[192,1,64]{2,1,0:T(1,128)S(1)}, u32[]{:S(2)}, u32[]{:S(2)}) async-start(f32[192,1,64]{2,1,0:T(1,128)} %get-tuple-element.23), calls=%async_computation | async-start | bytes 196608 | tf_op jit(solution)/shard_map/all_to_all | solution.py:237
  94.6 0.3 collective-permute-done.9.refs_1_
  94.9 0.0 collective-permute-done.10.refs_2_
  94.9 2.2 %collective-permute-done.11.refs_3_ = bf16[1024,256]{1,0:T(8,128)(2,1)} collective-permute-done((bf16[1024,256]{1,0:T(8,128)(2,1)}, bf16[1024,256]{1,0:T(8,128)(2,1)}, u32[]{:S(2)}, u32[]{:S(2)}) %collective-permute-start.11) | collective-permute-done | bytes 524320 | tf_op jit(solution)/shard_map/ppermute | solution.py:236
  97.1 0.0 copy-done.1
  97.1 0.0 copy-start.2
  97.2 1.0 copy-done.2
  98.2 0.0 copy-start.4
  98.2 1.0 copy-done.4
  99.2 0.0 copy-start.7
  99.2 3.9 %adam.1 = (bf16[2048,128]{1,0:T(8,128)(2,1)}, bf16[2048,128]{1,0:T(8,128)(2,1)}, f32[2048,128]{1,0:T(8,128)}) custom-call(bf16[1024,256]{1,0:T(8,128)(2,1)S(1)} %copy-done.4, bf16[1024,256]{1,0:T(8,128)(2,1)} %collective-permute-done.9.refs_1_, bf16[1024,256]{1,0:T(8,128)(2,1)} %collective-permute-done.10.refs_2_, ...), custom_call_target="tpu_custom_call" | custom-call | flops 524288 | bytes 8388608 | tf_op jit(solution)/shard_map/adam/pallas_call | solution.py:239
  103.1 6.9 %all-to-all-done.arrived = f32[192,1,64]{2,1,0:T(1,128)S(1)} async-done(((f32[192,1,64]{2,1,0:T(1,128)}), f32[192,1,64]{2,1,0:T(1,128)S(1)}, u32[]{:S(2)}, u32[]{:S(2)}) %all-to-all-start) | async-done | bytes 49184 | tf_op jit(solution)/shard_map/all_to_all | solution.py:237
  110.0 0.0 copy-done.7
  110.0 0.7 gates_home.1
  (6 shorter events, 0.1 us)
Async XLA Ops:
  0.6 1.0 copy-start.5
  1.6 0.7 copy-start.6
  2.3 0.7 copy-start.8
  3.0 9.3 %collective-permute-start.1 = (bf16[32,4224]{1,0:T(8,128)(2,1)S(1)}, bf16[32,4224]{1,0:T(8,128)(2,1)S(1)}, u32[]{:S(2)}, u32[]{:S(2)}) collective-permute-start(bf16[32,4224]{1,0:T(8,128)(2,1)S(1)} %pack.1.refs_0_), channel_id=1, source_target_pairs={{0,168},{24,0},{48,24},{72,48},{96,72},{120,96},{144,120},{168,144... | collective-permute-start | bytes 811016 | tf_op jit(solution)/shard_map/ppermute | solution.py:185
  8.9 8.4 %collective-permute-start = (bf16[32,4224]{1,0:T(8,128)(2,1)S(1)}, bf16[32,4224]{1,0:T(8,128)(2,1)S(1)}, u32[]{:S(2)}, u32[]{:S(2)}) collective-permute-start(bf16[32,4224]{1,0:T(8,128)(2,1)S(1)} %pack.1.refs_0_), channel_id=1, source_target_pairs={{0,24},{24,48},{48,72},{72,96},{96,120},{120,144},{144,168},{168,0... | collective-permute-start | bytes 811016 | tf_op jit(solution)/shard_map/ppermute | solution.py:185
  12.3 9.9 %collective-permute-start.3 = (bf16[32,4224]{1,0:T(8,128)(2,1)S(1)}, bf16[32,4224]{1,0:T(8,128)(2,1)S(1)}, u32[]{:S(2)}, u32[]{:S(2)}) collective-permute-start(bf16[32,4224]{1,0:T(8,128)(2,1)S(1)} %collective-permute-done.1.refs_2_), channel_id=1, source_target_pairs={{0,168},{24,0},{48,24},{72,48},{96,72},{120,96},{144,120},{168,144... | collective-permute-start | bytes 811016 | tf_op jit(solution)/shard_map/ppermute | solution.py:185
  17.3 9.9 %collective-permute-start.2 = (bf16[32,4224]{1,0:T(8,128)(2,1)S(1)}, bf16[32,4224]{1,0:T(8,128)(2,1)S(1)}, u32[]{:S(2)}, u32[]{:S(2)}) collective-permute-start(bf16[32,4224]{1,0:T(8,128)(2,1)S(1)} %collective-permute-done.refs_1_), channel_id=1, source_target_pairs={{0,24},{24,48},{48,72},{72,96},{96,120},{120,144},{144,168},{168,0... | collective-permute-start | bytes 811016 | tf_op jit(solution)/shard_map/ppermute | solution.py:185
  19.3 41.4 %copy-start = (bf16[2,128,4096]{2,1,0:T(8,128)(2,1)S(1)}, bf16[2,128,4096]{2,1,0:T(8,128)(2,1)}, u32[]{:S(2)}) copy-start(bf16[2,128,4096]{2,1,0:T(8,128)(2,1)} %param.11) | copy-start | bytes 6291460
  19.3 41.4 %copy-start.9 = (bf16[1,16,2,12,128]{4,2,3,1,0:T(2,128)(2,1)S(1)}, bf16[1,16,2,12,128]{4,2,3,1,0:T(2,128)(2,1)}, u32[]{:S(2)}) copy-start(bf16[1,16,2,12,128]{4,2,3,1,0:T(2,128)(2,1)} %param.10) | copy-start | bytes 294916
  27.2 26.2 %collective-permute-start.4 = (bf16[32,4224]{1,0:T(8,128)(2,1)S(1)}, bf16[32,4224]{1,0:T(8,128)(2,1)S(1)}, u32[]{:S(2)}, u32[]{:S(2)}) collective-permute-start(bf16[32,4224]{1,0:T(8,128)(2,1)S(1)} %pack.1.refs_0_), channel_id=1, source_target_pairs={{0,96},{24,120},{48,144},{72,168},{96,0},{120,24},{144,48},{168,72... | collective-permute-start | bytes 811016 | tf_op jit(solution)/shard_map/ppermute | solution.py:185
  33.0 20.4 %collective-permute-start.5 = (bf16[32,4224]{1,0:T(8,128)(2,1)S(1)}, bf16[32,4224]{1,0:T(8,128)(2,1)S(1)}, u32[]{:S(2)}, u32[]{:S(2)}) collective-permute-start(bf16[32,4224]{1,0:T(8,128)(2,1)S(1)} %collective-permute-done.2.refs_3_), channel_id=1, source_target_pairs={{0,24},{24,48},{48,72},{72,96},{96,120},{120,144},{144,168},{168,0... | collective-permute-start | bytes 811016 | tf_op jit(solution)/shard_map/ppermute | solution.py:185
  35.0 18.5 %collective-permute-start.6 = (bf16[32,4224]{1,0:T(8,128)(2,1)S(1)}, bf16[32,4224]{1,0:T(8,128)(2,1)S(1)}, u32[]{:S(2)}, u32[]{:S(2)}) collective-permute-start(bf16[32,4224]{1,0:T(8,128)(2,1)S(1)} %collective-permute-done.3.refs_4_), channel_id=1, source_target_pairs={{0,168},{24,0},{48,24},{72,48},{96,72},{120,96},{144,120},{168,144... | collective-permute-start | bytes 811016 | tf_op jit(solution)/shard_map/ppermute | solution.py:185
  39.6 21.1 %collective-permute-start.7 = (bf16[160,4224]{1,0:T(8,128)(2,1)S(1)}, bf16[160,4224]{1,0:T(8,128)(2,1)S(1)}, u32[]{:S(2)}, u32[]{:S(2)}) collective-permute-start(bf16[160,4224]{1,0:T(8,128)(2,1)S(1)} %constant_dynamic-update-slice_fusion), channel_id=1, source_target_pairs={{0,12},{12,0},{1,13},{13,1},{2,14},{14,2},{3,15},{15,3},{4,16},{16... | collective-permute-start | bytes 4055048 | tf_op jit(solution)/shard_map/ppermute | solution.py:197
  53.5 7.2 %collective-permute-start.8 = (bf16[96,4224]{1,0:T(8,128)(2,1)S(1)}, bf16[96,4224]{1,0:T(8,128)(2,1)S(1)}, u32[]{:S(2)}, u32[]{:S(2)}) collective-permute-start(bf16[96,4224]{1,0:T(8,128)(2,1)S(1)} %pad_maximum_fusion), channel_id=1, source_target_pairs={{0,12},{12,0},{1,13},{13,1},{2,14},{14,2},{3,15},{15,3},{4,16},{16... | collective-permute-start | bytes 2433032 | tf_op jit(solution)/shard_map/ppermute | solution.py:197
  60.8 36.4 %copy-start.1 = (f32[1024,2,128]{2,1,0:T(2,128)S(1)}, f32[1024,2,128]{2,1,0:T(2,128)}, u32[]{:S(2)}) copy-start(f32[1024,2,128]{2,1,0:T(2,128)} %param.13) | copy-start | bytes 3145732
  66.4 0.8 copy-start.3
  67.2 27.8 %collective-permute-start.9 = (bf16[1024,256]{1,0:T(8,128)(2,1)}, bf16[1024,256]{1,0:T(8,128)(2,1)}, u32[]{:S(2)}, u32[]{:S(2)}) collective-permute-start(bf16[1024,256]{1,0:T(8,128)(2,1)} %get-tuple-element.25), channel_id=1, source_target_pairs={{0,192},{192,384},{384,576},{576,0},{1,193},{193,385},{385,577},{5... | collective-permute-start | bytes 1572872 | tf_op jit(solution)/shard_map/ppermute | solution.py:236
  69.1 25.9 %collective-permute-start.10 = (bf16[1024,256]{1,0:T(8,128)(2,1)}, bf16[1024,256]{1,0:T(8,128)(2,1)}, u32[]{:S(2)}, u32[]{:S(2)}) collective-permute-start(bf16[1024,256]{1,0:T(8,128)(2,1)} %get-tuple-element.26), channel_id=1, source_target_pairs={{0,384},{192,576},{384,0},{576,192},{1,385},{193,577},{385,1},{577... | collective-permute-start | bytes 1572872 | tf_op jit(solution)/shard_map/ppermute | solution.py:236
  71.0 26.1 %collective-permute-start.11 = (bf16[1024,256]{1,0:T(8,128)(2,1)}, bf16[1024,256]{1,0:T(8,128)(2,1)}, u32[]{:S(2)}, u32[]{:S(2)}) collective-permute-start(bf16[1024,256]{1,0:T(8,128)(2,1)} %get-tuple-element.27), channel_id=1, source_target_pairs={{0,576},{192,0},{384,192},{576,384},{1,577},{193,1},{385,193},{577... | collective-permute-start | bytes 1572872 | tf_op jit(solution)/shard_map/ppermute | solution.py:236
  75.6 34.4 %all-to-all-start = ((f32[192,1,64]{2,1,0:T(1,128)}), f32[192,1,64]{2,1,0:T(1,128)S(1)}, u32[]{:S(2)}, u32[]{:S(2)}) async-start(f32[192,1,64]{2,1,0:T(1,128)} %get-tuple-element.23), calls=%async_computation | async-start | bytes 196608 | tf_op jit(solution)/shard_map/all_to_all | solution.py:237
  97.1 1.0 copy-start.2
  98.2 1.0 copy-start.4
  99.2 10.8 %copy-start.7 = (s32[32,8]{0,1:T(8,128)S(1)}, s32[32,8]{0,1:T(8,128)}, u32[]{:S(2)}) copy-start(s32[32,8]{0,1:T(8,128)} %param.9) | copy-start | bytes 3076

commit v7 on v6

--- a/solution.py
+++ b/solution.py
@@ -65,19 +65,21 @@
     return jnp.concatenate([jnp.broadcast_to(g, (g.shape[0], LANES)) for g in gate], axis=1)
 
 
-def pack_kernel(rows_in, ids, gates, out):
-    width, tokens = rows_in.shape[1], rows_in.shape[0]
-    out[:, :width] = rows_in[...]
-    turned = jnp.concatenate([ids[...].astype(F32), gates[...].astype(F32)], axis=0)
-    turned = jnp.concatenate([turned, jnp.zeros((turned.shape[0], LANES - tokens), F32)], axis=1)
-    turned = jnp.concatenate([turned, jnp.zeros((tokens - turned.shape[0], LANES), F32)], axis=0)
-    out[:, width:] = turned.astype(BF16)
-
-
-def by_token(meta, tokens):
-    meta = meta.astype(F32)
-    blocks = [meta[at : at + tokens, :].T for at in range(0, meta.shape[0], tokens)]
-    return jnp.concatenate([block[:tokens, :] for block in blocks], axis=0)
+def pack_kernel(rows_in, ids_in, gates_in, out, ids, gates, sems):
+    tokens, width = rows_in.shape
+    rows_copy = pltpu.make_async_copy(rows_in, out.at[:, pl.ds(0, width)], sems.at[0])
+    ids_copy = pltpu.make_async_copy(ids_in, ids, sems.at[1])
+    gates_copy = pltpu.make_async_copy(gates_in, gates, sems.at[2])
+    rows_copy.start()
+    ids_copy.start()
+    gates_copy.start()
+    ids_copy.wait()
+    gates_copy.wait()
+    lying = jnp.concatenate([ids[...].astype(F32), gates[...].astype(F32)], axis=0)
+    lying = jnp.concatenate([lying, jnp.zeros((lying.shape[0], LANES - tokens), F32)], axis=1)
+    lying = jnp.concatenate([lying, jnp.zeros((LANES - lying.shape[0], LANES), F32)], axis=0)
+    out[:, width:] = lying.T[:tokens, :].astype(BF16)
+    rows_copy.wait()
 
 
 def own_kernel(tokens, rows, width, planes, pieces, *refs):
@@ -97,7 +99,7 @@
     for rel in range(2):
         side = core if rel == 0 else 1 - core
         here = slice(rel * count, (rel + 1) * count)
-        onehot, gate = routed(by_token(toks[here, width : width + LANES], tokens), base, tokens, rows)
+        onehot, gate = routed(toks[here, width : width + LANES], base, tokens, rows)
         slots = jnp.concatenate([hid[block, side].astype(F32) for block in where], axis=0)
         saved = dot(onehot, by_expert(slots), (1, 0))
         up = dot(toks[here, :width], weight[...], (1, 1))
@@ -211,8 +213,14 @@
     toks = gathered(
         pl.pallas_call(
             pack_kernel,
+            in_specs=[pl.BlockSpec(memory_space=pltpu.HBM)] * 3,
             out_shape=jax.ShapeDtypeStruct((tokens, width + LANES), BF16),
-            compiler_params=PARAMS,
+            scratch_shapes=[
+                pltpu.VMEM((choices, tokens), jnp.int32),
+                pltpu.VMEM((choices, tokens), BF16),
+                pltpu.SemaphoreType.DMA((3,)),
+            ],
+            compiler_params=pltpu.CompilerParams(vmem_limit_bytes=60 * 1024 * 1024),
             name="pack",
         )(grad_out, expert_ids.T, gates.T)
     )
@@ -248,7 +256,6 @@
         cost_estimate=cost(part, held * LANES, 8 << 20),
         name="adam",
     )(*grads, weight, moment_one.reshape(flat), moment_two.reshape(flat))
-    gate_home, new_one = lax.optimization_barrier((gate_home, new_one))
     grad_gates = pl.pallas_call(
         functools.partial(home_kernel, tokens, planes),
         out_shape=jax.ShapeDtypeStruct((choices, tokens), F32),

time: 111 us -> 112 us (level)
  blocking collectives: 0 us -> 34.2 us
  starting transfers between devices: 73.6 us -> 54.6 us
  waiting for transfers between devices: 20.7 us -> 10.6 us
  local copies, waits for them, and re-layouts: 5.34 us -> 1.13 us
    all_to_all x0 -> x1, blocking collectives: none -> 34.2 us  [shards(): lax.all_to_all(gate_part, ('ey', 'core', 'tensor'), 0, 0, tiled=True)]
    all_to_all x1 -> x0, starting transfers between devices: 19 us -> none  [shards(): lax.all_to_all(gate_part, ('ey', 'core', 'tensor'), 0, 0, tiled=True)]
    all_to_all x1 -> x0, waiting for transfers between devices: 6.92 us -> none  [shards(): lax.all_to_all(gate_part, ('ey', 'core', 'tensor'), 0, 0, tiled=True)]
    unnamed x24 -> x16, local copies, waits for them, and re-layouts: 5.32 us -> 1.1 us
    ppermute x3, waiting for transfers between devices: 2.53 us -> 0.01 us  [shards(): grads[step] = lax.ppermute(grads[step], 'edata', to_owner)]
    pallas_call x1, Pallas kernels: 0.02 us -> 1.68 us  [shards(): pl.pallas_call(pack_kernel, in_specs=[pl.BlockSpec(memory_space=pltpu.HBM...]
    pallas_call x1, Pallas kernels: 3.86 us -> 2.55 us  [shards(): pl.pallas_call(functools.partial(adam_kernel, part, replicas), out_shape=...]
  transfers between devices with their start and end apart: 13 -> 12, of which waited for: 7 -> 4; matrix products, arithmetic and copies ran while one was open for 0% -> 1% of each run, Pallas kernels for 3% -> 1%
where the time goes in v7:
time: 112 us; the launch traced here: 111 us
  starting transfers between devices  54.6 us (49%)
  blocking collectives  34.2 us (31%)
  waiting for transfers between devices  10.6 us (9%)
  Pallas kernels  9.5 us (8%)
  local copies, waits for them, and re-layouts  1.13 us (1%)
    all_to_all x1, blocking collectives, shards(): lax.all_to_all(gate_part, ('ey', 'core', 'tensor'), 0, 0, tiled=True)  34.2 us
    ppermute x7, starting transfers between devices, turn(): lax.ppermute(block, 'ey', [(i, (i + by) % size) for i in range(size)])  27.1 us
    ppermute x2, starting transfers between devices, gathered(): lax.ppermute(jnp.concatenate(g, axis=0), 'core', swap)  19.1 us
    ppermute x7, waiting for transfers between devices, turn(): lax.ppermute(block, 'ey', [(i, (i + by) % size) for i in range(size)])  8.65 us
    ppermute x3, starting transfers between devices, shards(): grads[step] = lax.ppermute(grads[step], 'edata', to_owner)  8.41 us
    pallas_call x1, Pallas kernels, shards(): pl.pallas_call(functools.partial(own_kernel, tokens, rows, width, planes,...  4.56 us
    pallas_call x1, Pallas kernels, shards(): pl.pallas_call(functools.partial(adam_kernel, part, replicas), out_shape=...  2.55 us
  transfers between devices with their start and end apart: 12, of which 4 were waited for; matrix products, arithmetic and copies ran while one was open for 1% of the time, Pallas kernels for 1%

profile of v7, /device:TPU:1, one launch (start us, length us, event | category | flops | bytes accessed | tf_op | source)
XLA Modules:
  0.0 111.0 jit_solution(10166946851730569286)
XLA Ops:
  0.6 1.7 %pack.1.refs_0_ = bf16[32,4224]{1,0:T(8,128)(2,1)} custom-call(bf16[32,4096]{1,0:T(8,128)(2,1)} %rows_in.1, s32[8,32]{1,0:T(8,128)} %bitcast.21, bf16[8,32]{1,0:T(8,128)(2,1)} %bitcast.25), custom_call_target="tpu_custom_call" | custom-call | tf_op jit(solution)/shard_map/pack/pallas_call | solution.py:214
  2.3 0.0 copy-start.1
  2.3 6.1 %collective-permute-start.1 = (bf16[32,4224]{1,0:T(8,128)(2,1)}, bf16[32,4224]{1,0:T(8,128)(2,1)S(1)}, u32[]{:S(2)}, u32[]{:S(2)}) collective-permute-start(bf16[32,4224]{1,0:T(8,128)(2,1)} %pack.1.refs_0_), channel_id=1, source_target_pairs={{0,168},{24,0},{48,24},{72,48},{96,72},{120,96},{144,120},{168,144... | collective-permute-start | bytes 811016 | tf_op jit(solution)/shard_map/ppermute | solution.py:187
  8.4 1.9 %collective-permute-start = (bf16[32,4224]{1,0:T(8,128)(2,1)}, bf16[32,4224]{1,0:T(8,128)(2,1)S(1)}, u32[]{:S(2)}, u32[]{:S(2)}) collective-permute-start(bf16[32,4224]{1,0:T(8,128)(2,1)} %pack.1.refs_0_), channel_id=1, source_target_pairs={{0,24},{24,48},{48,72},{72,96},{96,120},{120,144},{144,168},{168,0... | collective-permute-start | bytes 811016 | tf_op jit(solution)/shard_map/ppermute | solution.py:187
  10.3 1.0 constant_dynamic-update-slice_fusion.4
  11.3 0.8 collective-permute-done.1.refs_2_
  12.1 4.9 %collective-permute-start.3 = (bf16[32,4224]{1,0:T(8,128)(2,1)S(1)}, bf16[32,4224]{1,0:T(8,128)(2,1)S(1)}, u32[]{:S(2)}, u32[]{:S(2)}) collective-permute-start(bf16[32,4224]{1,0:T(8,128)(2,1)S(1)} %collective-permute-done.1.refs_2_), channel_id=1, source_target_pairs={{0,168},{24,0},{48,24},{72,48},{96,72},{120,96},{144,120},{168,144... | collective-permute-start | bytes 811016 | tf_op jit(solution)/shard_map/ppermute | solution.py:187
  17.0 0.0 collective-permute-done.refs_1_
  17.0 1.9 %collective-permute-start.2 = (bf16[32,4224]{1,0:T(8,128)(2,1)S(1)}, bf16[32,4224]{1,0:T(8,128)(2,1)S(1)}, u32[]{:S(2)}, u32[]{:S(2)}) collective-permute-start(bf16[32,4224]{1,0:T(8,128)(2,1)S(1)} %collective-permute-done.refs_1_), channel_id=1, source_target_pairs={{0,24},{24,48},{48,72},{72,96},{96,120},{120,144},{144,168},{168,0... | collective-permute-start | bytes 811016 | tf_op jit(solution)/shard_map/ppermute | solution.py:187
  19.0 0.0 copy-start
  19.0 0.0 copy-start.5
  19.0 2.9 %collective-permute-done.3.refs_4_ = bf16[32,4224]{1,0:T(8,128)(2,1)S(1)} collective-permute-done((bf16[32,4224]{1,0:T(8,128)(2,1)S(1)}, bf16[32,4224]{1,0:T(8,128)(2,1)S(1)}, u32[]{:S(2)}, u32[]{:S(2)}) %collective-permute-start.3) | collective-permute-done | bytes 270368 | tf_op jit(solution)/shard_map/ppermute | solution.py:187
  21.9 5.0 %collective-permute-done.2.refs_3_ = bf16[32,4224]{1,0:T(8,128)(2,1)S(1)} collective-permute-done((bf16[32,4224]{1,0:T(8,128)(2,1)S(1)}, bf16[32,4224]{1,0:T(8,128)(2,1)S(1)}, u32[]{:S(2)}, u32[]{:S(2)}) %collective-permute-start.2) | collective-permute-done | bytes 270368 | tf_op jit(solution)/shard_map/ppermute | solution.py:187
  26.9 0.0 copy-done.1
  26.9 5.8 %collective-permute-start.4 = (bf16[32,4224]{1,0:T(8,128)(2,1)S(1)}, bf16[32,4224]{1,0:T(8,128)(2,1)S(1)}, u32[]{:S(2)}, u32[]{:S(2)}) collective-permute-start(bf16[32,4224]{1,0:T(8,128)(2,1)S(1)} %copy-done.1), channel_id=1, source_target_pairs={{0,96},{24,120},{48,144},{72,168},{96,0},{120,24},{144,48},{168,72... | collective-permute-start | bytes 811016 | tf_op jit(solution)/shard_map/ppermute | solution.py:187
  32.7 1.9 %collective-permute-start.5 = (bf16[32,4224]{1,0:T(8,128)(2,1)S(1)}, bf16[32,4224]{1,0:T(8,128)(2,1)S(1)}, u32[]{:S(2)}, u32[]{:S(2)}) collective-permute-start(bf16[32,4224]{1,0:T(8,128)(2,1)S(1)} %collective-permute-done.2.refs_3_), channel_id=1, source_target_pairs={{0,24},{24,48},{48,72},{72,96},{96,120},{120,144},{144,168},{168,0... | collective-permute-start | bytes 811016 | tf_op jit(solution)/shard_map/ppermute | solution.py:187
  34.7 4.6 %collective-permute-start.6 = (bf16[32,4224]{1,0:T(8,128)(2,1)S(1)}, bf16[32,4224]{1,0:T(8,128)(2,1)S(1)}, u32[]{:S(2)}, u32[]{:S(2)}) collective-permute-start(bf16[32,4224]{1,0:T(8,128)(2,1)S(1)} %collective-permute-done.3.refs_4_), channel_id=1, source_target_pairs={{0,168},{24,0},{48,24},{72,48},{96,72},{120,96},{144,120},{168,144... | collective-permute-start | bytes 811016 | tf_op jit(solution)/shard_map/ppermute | solution.py:187
  39.3 13.8 %collective-permute-start.7 = (bf16[160,4224]{1,0:T(8,128)(2,1)S(1)}, bf16[160,4224]{1,0:T(8,128)(2,1)S(1)}, u32[]{:S(2)}, u32[]{:S(2)}) collective-permute-start(bf16[160,4224]{1,0:T(8,128)(2,1)S(1)} %constant_dynamic-update-slice_fusion), channel_id=1, source_target_pairs={{0,12},{12,0},{1,13},{13,1},{2,14},{14,2},{3,15},{15,3},{4,16},{16... | collective-permute-start | bytes 4055048 | tf_op jit(solution)/shard_map/ppermute | solution.py:199
  53.1 0.0 collective-permute-done.4.refs_5_
  53.1 0.0 collective-permute-done.5.refs_6_
  53.1 0.0 collective-permute-done.6.refs_7_
  53.1 0.1 pad_maximum_fusion
  53.2 5.3 %collective-permute-start.8 = (bf16[96,4224]{1,0:T(8,128)(2,1)S(1)}, bf16[96,4224]{1,0:T(8,128)(2,1)S(1)}, u32[]{:S(2)}, u32[]{:S(2)}) collective-permute-start(bf16[96,4224]{1,0:T(8,128)(2,1)S(1)} %pad_maximum_fusion), channel_id=1, source_target_pairs={{0,12},{12,0},{1,13},{13,1},{2,14},{14,2},{3,15},{15,3},{4,16},{16... | collective-permute-start | bytes 2433032 | tf_op jit(solution)/shard_map/ppermute | solution.py:199
  58.5 1.9 %collective-permute-done.8.refs_9_ = bf16[96,4224]{1,0:T(8,128)(2,1)S(1)} collective-permute-done((bf16[96,4224]{1,0:T(8,128)(2,1)S(1)}, bf16[96,4224]{1,0:T(8,128)(2,1)S(1)}, u32[]{:S(2)}, u32[]{:S(2)}) %collective-permute-start.8) | collective-permute-done | bytes 811040 | tf_op jit(solution)/shard_map/ppermute | solution.py:199
  60.4 0.0 collective-permute-done.7.refs_8_
  60.4 0.0 copy-done
  60.4 0.0 copy-done.5
  60.4 0.0 copy-start.4
  60.4 0.0 copy-start.2
  60.5 0.0 copy-start.3
  60.5 4.6 %own_tokens.1 = (bf16[8,2,24,128]{3,2,1,0:T(8,128)(2,1)}, f32[192,1,64]{2,1,0:T(1,128)S(1)}, bf16[1024,256]{1,0:T(8,128)(2,1)S(1)}, bf16[1024,256]{1,0:T(8,128)(...) custom-call(bf16[32,4224]{1,0:T(8,128)(2,1)S(1)} %copy-done.1, ...), custom_call_target="tpu_custom_call" | custom-call | flops 2147483648 | bytes 8388608 | tf_op jit(solution)/shard_map/own_tokens/pallas_call | solution.py:229
  65.0 1.9 %collective-permute-start.9 = (bf16[1024,256]{1,0:T(8,128)(2,1)S(1)}, bf16[1024,256]{1,0:T(8,128)(2,1)S(1)}, u32[]{:S(2)}, u32[]{:S(2)}) collective-permute-start(bf16[1024,256]{1,0:T(8,128)(2,1)S(1)} %get-tuple-element.23), channel_id=1, source_target_pairs={{0,192},{192,384},{384,576},{576,0},{1,193},{193,385},{385,577},{5... | collective-permute-start | bytes 1572872 | tf_op jit(solution)/shard_map/ppermute | solution.py:244
  67.0 1.9 %collective-permute-start.10 = (bf16[1024,256]{1,0:T(8,128)(2,1)S(1)}, bf16[1024,256]{1,0:T(8,128)(2,1)S(1)}, u32[]{:S(2)}, u32[]{:S(2)}) collective-permute-start(bf16[1024,256]{1,0:T(8,128)(2,1)S(1)} %get-tuple-element.24), channel_id=1, source_target_pairs={{0,384},{192,576},{384,0},{576,192},{1,385},{193,577},{385,1},{577... | collective-permute-start | bytes 1572872 | tf_op jit(solution)/shard_map/ppermute | solution.py:244
  68.9 4.6 %collective-permute-start.11 = (bf16[1024,256]{1,0:T(8,128)(2,1)S(1)}, bf16[1024,256]{1,0:T(8,128)(2,1)S(1)}, u32[]{:S(2)}, u32[]{:S(2)}) collective-permute-start(bf16[1024,256]{1,0:T(8,128)(2,1)S(1)} %get-tuple-element.25), channel_id=1, source_target_pairs={{0,576},{192,0},{384,192},{576,384},{1,577},{193,1},{385,193},{577... | collective-permute-start | bytes 1572872 | tf_op jit(solution)/shard_map/ppermute | solution.py:244
  73.5 34.2 %all_to_all.5.arrived = f32[192,1,64]{2,1,0:T(1,128)S(1)} all-to-all(f32[192,1,64]{2,1,0:T(1,128)S(1)} %get-tuple-element.21), channel_id=1, replica_groups=mesh['edata'=4,'ey'=8,'core'=2,'tensor'=12] {'ey','core','tensor'}, dimensions={0} | all-to-all | bytes 98304 | tf_op jit(solution)/shard_map/all_to_all | solution.py:245
  107.7 0.0 copy-done.4
  107.7 0.7 gates_home.1
  108.4 0.0 collective-permute-done.9.refs_1_
  108.4 0.0 collective-permute-done.10.refs_2_
  108.4 0.0 collective-permute-done.11.refs_3_
  108.4 0.0 copy-done.2
  108.5 0.0 copy-done.3
  108.5 2.6 %adam.1 = (bf16[2048,128]{1,0:T(8,128)(2,1)}, bf16[2048,128]{1,0:T(8,128)(2,1)}, f32[2048,128]{1,0:T(8,128)}) custom-call(bf16[1024,256]{1,0:T(8,128)(2,1)S(1)} %get-tuple-element.22.refs_0_, bf16[1024,256]{1,0:T(8,128)(2,1)S(1)} %collective-permute-done.9.refs_1_, bf16[1024,256]{1,0:T(8,128)(2,1)S(1)} %collective-permute-done.10.refs_2_, ...), custom_call_target="tpu_custom_call" | custom-call | flops 524288 | bytes 8388608 | tf_op jit(solution)/shard_map/adam/pallas_call | solution.py:247
  (4 shorter events, 0.1 us)
Async XLA Ops:
  2.3 24.6 %copy-start.1 = (bf16[32,4224]{1,0:T(8,128)(2,1)S(1)}, bf16[32,4224]{1,0:T(8,128)(2,1)}, u32[]{:S(2)}) copy-start(bf16[32,4224]{1,0:T(8,128)(2,1)} %pack.1.refs_0_) | copy-start | bytes 811012
  2.3 9.8 %collective-permute-start.1 = (bf16[32,4224]{1,0:T(8,128)(2,1)}, bf16[32,4224]{1,0:T(8,128)(2,1)S(1)}, u32[]{:S(2)}, u32[]{:S(2)}) collective-permute-start(bf16[32,4224]{1,0:T(8,128)(2,1)} %pack.1.refs_0_), channel_id=1, source_target_pairs={{0,168},{24,0},{48,24},{72,48},{96,72},{120,96},{144,120},{168,144... | collective-permute-start | bytes 811016 | tf_op jit(solution)/shard_map/ppermute | solution.py:187
  8.4 8.6 %collective-permute-start = (bf16[32,4224]{1,0:T(8,128)(2,1)}, bf16[32,4224]{1,0:T(8,128)(2,1)S(1)}, u32[]{:S(2)}, u32[]{:S(2)}) collective-permute-start(bf16[32,4224]{1,0:T(8,128)(2,1)} %pack.1.refs_0_), channel_id=1, source_target_pairs={{0,24},{24,48},{48,72},{72,96},{96,120},{120,144},{144,168},{168,0... | collective-permute-start | bytes 811016 | tf_op jit(solution)/shard_map/ppermute | solution.py:187
  12.1 9.8 %collective-permute-start.3 = (bf16[32,4224]{1,0:T(8,128)(2,1)S(1)}, bf16[32,4224]{1,0:T(8,128)(2,1)S(1)}, u32[]{:S(2)}, u32[]{:S(2)}) collective-permute-start(bf16[32,4224]{1,0:T(8,128)(2,1)S(1)} %collective-permute-done.1.refs_2_), channel_id=1, source_target_pairs={{0,168},{24,0},{48,24},{72,48},{96,72},{120,96},{144,120},{168,144... | collective-permute-start | bytes 811016 | tf_op jit(solution)/shard_map/ppermute | solution.py:187
  17.0 9.9 %collective-permute-start.2 = (bf16[32,4224]{1,0:T(8,128)(2,1)S(1)}, bf16[32,4224]{1,0:T(8,128)(2,1)S(1)}, u32[]{:S(2)}, u32[]{:S(2)}) collective-permute-start(bf16[32,4224]{1,0:T(8,128)(2,1)S(1)} %collective-permute-done.refs_1_), channel_id=1, source_target_pairs={{0,24},{24,48},{48,72},{72,96},{96,120},{120,144},{144,168},{168,0... | collective-permute-start | bytes 811016 | tf_op jit(solution)/shard_map/ppermute | solution.py:187
  19.0 41.4 %copy-start = (bf16[2,128,4096]{2,1,0:T(8,128)(2,1)S(1)}, bf16[2,128,4096]{2,1,0:T(8,128)(2,1)}, u32[]{:S(2)}) copy-start(bf16[2,128,4096]{2,1,0:T(8,128)(2,1)} %param.11) | copy-start | bytes 6291460
  19.0 41.4 %copy-start.5 = (bf16[1,16,2,12,128]{4,2,3,1,0:T(2,128)(2,1)S(1)}, bf16[1,16,2,12,128]{4,2,3,1,0:T(2,128)(2,1)}, u32[]{:S(2)}) copy-start(bf16[1,16,2,12,128]{4,2,3,1,0:T(2,128)(2,1)} %param.10) | copy-start | bytes 294916
  26.9 26.2 %collective-permute-start.4 = (bf16[32,4224]{1,0:T(8,128)(2,1)S(1)}, bf16[32,4224]{1,0:T(8,128)(2,1)S(1)}, u32[]{:S(2)}, u32[]{:S(2)}) collective-permute-start(bf16[32,4224]{1,0:T(8,128)(2,1)S(1)} %copy-done.1), channel_id=1, source_target_pairs={{0,96},{24,120},{48,144},{72,168},{96,0},{120,24},{144,48},{168,72... | collective-permute-start | bytes 811016 | tf_op jit(solution)/shard_map/ppermute | solution.py:187
  32.7 20.4 %collective-permute-start.5 = (bf16[32,4224]{1,0:T(8,128)(2,1)S(1)}, bf16[32,4224]{1,0:T(8,128)(2,1)S(1)}, u32[]{:S(2)}, u32[]{:S(2)}) collective-permute-start(bf16[32,4224]{1,0:T(8,128)(2,1)S(1)} %collective-permute-done.2.refs_3_), channel_id=1, source_target_pairs={{0,24},{24,48},{48,72},{72,96},{96,120},{120,144},{144,168},{168,0... | collective-permute-start | bytes 811016 | tf_op jit(solution)/shard_map/ppermute | solution.py:187
  34.7 18.5 %collective-permute-start.6 = (bf16[32,4224]{1,0:T(8,128)(2,1)S(1)}, bf16[32,4224]{1,0:T(8,128)(2,1)S(1)}, u32[]{:S(2)}, u32[]{:S(2)}) collective-permute-start(bf16[32,4224]{1,0:T(8,128)(2,1)S(1)} %collective-permute-done.3.refs_4_), channel_id=1, source_target_pairs={{0,168},{24,0},{48,24},{72,48},{96,72},{120,96},{144,120},{168,144... | collective-permute-start | bytes 811016 | tf_op jit(solution)/shard_map/ppermute | solution.py:187
  39.3 21.1 %collective-permute-start.7 = (bf16[160,4224]{1,0:T(8,128)(2,1)S(1)}, bf16[160,4224]{1,0:T(8,128)(2,1)S(1)}, u32[]{:S(2)}, u32[]{:S(2)}) collective-permute-start(bf16[160,4224]{1,0:T(8,128)(2,1)S(1)} %constant_dynamic-update-slice_fusion), channel_id=1, source_target_pairs={{0,12},{12,0},{1,13},{13,1},{2,14},{14,2},{3,15},{15,3},{4,16},{16... | collective-permute-start | bytes 4055048 | tf_op jit(solution)/shard_map/ppermute | solution.py:199
  53.2 7.2 %collective-permute-start.8 = (bf16[96,4224]{1,0:T(8,128)(2,1)S(1)}, bf16[96,4224]{1,0:T(8,128)(2,1)S(1)}, u32[]{:S(2)}, u32[]{:S(2)}) collective-permute-start(bf16[96,4224]{1,0:T(8,128)(2,1)S(1)} %pad_maximum_fusion), channel_id=1, source_target_pairs={{0,12},{12,0},{1,13},{13,1},{2,14},{14,2},{3,15},{15,3},{4,16},{16... | collective-permute-start | bytes 2433032 | tf_op jit(solution)/shard_map/ppermute | solution.py:199
  60.4 47.3 %copy-start.4 = (s32[32,8]{0,1:T(8,128)S(1)}, s32[32,8]{0,1:T(8,128)}, u32[]{:S(2)}) copy-start(s32[32,8]{0,1:T(8,128)} %param.9) | copy-start | bytes 3076
  60.4 48.0 %copy-start.2 = (f32[1024,2,128]{2,1,0:T(2,128)S(1)}, f32[1024,2,128]{2,1,0:T(2,128)}, u32[]{:S(2)}) copy-start(f32[1024,2,128]{2,1,0:T(2,128)} %param.13) | copy-start | bytes 3145732
  60.5 48.0 %copy-start.3 = (bf16[1024,2,128]{2,1,0:T(2,128)(2,1)S(1)}, bf16[1024,2,128]{2,1,0:T(2,128)(2,1)}, u32[]{:S(2)}) copy-start(bf16[1024,2,128]{2,1,0:T(2,128)(2,1)} %param.12) | copy-start | bytes 1572868
  65.0 43.4 %collective-permute-start.9 = (bf16[1024,256]{1,0:T(8,128)(2,1)S(1)}, bf16[1024,256]{1,0:T(8,128)(2,1)S(1)}, u32[]{:S(2)}, u32[]{:S(2)}) collective-permute-start(bf16[1024,256]{1,0:T(8,128)(2,1)S(1)} %get-tuple-element.23), channel_id=1, source_target_pairs={{0,192},{192,384},{384,576},{576,0},{1,193},{193,385},{385,577},{5... | collective-permute-start | bytes 1572872 | tf_op jit(solution)/shard_map/ppermute | solution.py:244
  67.0 41.5 %collective-permute-start.10 = (bf16[1024,256]{1,0:T(8,128)(2,1)S(1)}, bf16[1024,256]{1,0:T(8,128)(2,1)S(1)}, u32[]{:S(2)}, u32[]{:S(2)}) collective-permute-start(bf16[1024,256]{1,0:T(8,128)(2,1)S(1)} %get-tuple-element.24), channel_id=1, source_target_pairs={{0,384},{192,576},{384,0},{576,192},{1,385},{193,577},{385,1},{577... | collective-permute-start | bytes 1572872 | tf_op jit(solution)/shard_map/ppermute | solution.py:244
  68.9 39.5 %collective-permute-start.11 = (bf16[1024,256]{1,0:T(8,128)(2,1)S(1)}, bf16[1024,256]{1,0:T(8,128)(2,1)S(1)}, u32[]{:S(2)}, u32[]{:S(2)}) collective-permute-start(bf16[1024,256]{1,0:T(8,128)(2,1)S(1)} %get-tuple-element.25), channel_id=1, source_target_pairs={{0,576},{192,0},{384,192},{576,384},{1,577},{193,1},{385,193},{577... | collective-permute-start | bytes 1572872 | tf_op jit(solution)/shard_map/ppermute | solution.py:244

commit v8 on v7

--- a/solution.py
+++ b/solution.py
@@ -191,7 +191,7 @@
     for _ in range(2, size // 2 - 1):
         up, down = turn(up, 1), turn(down, -1)
         mine += [up, down]
-    again, up, down = lax.optimization_barrier((own, up, down))
+    again, down = lax.optimization_barrier((own, down))
     far = turn(again, size // 2)
     mine[-2:] = [up, down]
     last = [far, turn(up, 1), turn(down, -1)]

time: 112 us -> 108 us (0.964)
  waiting for transfers between devices: 10.6 us -> 7.36 us
  blocking collectives: 34.2 us -> 36.1 us
  starting transfers between devices: 54.6 us -> 52.7 us
    ppermute x7, waiting for transfers between devices: 8.65 us -> 5.43 us  [turn(): lax.ppermute(block, 'ey', [(i, (i + by) % size) for i in range(size)])]
    ppermute x2, starting transfers between devices: 19.1 us -> 16.5 us  [gathered(): lax.ppermute(jnp.concatenate(g, axis=0), 'core', swap)]
    all_to_all x1, blocking collectives: 34.2 us -> 36.1 us  [shards(): lax.all_to_all(gate_part, ('ey', 'core', 'tensor'), 0, 0, tiled=True)]
where the time goes in v8:
time: 108 us
  starting transfers between devices  52.7 us (49%)
  blocking collectives  36.1 us (33%)
  Pallas kernels  9.5 us (9%)
  waiting for transfers between devices  7.36 us (7%)
  local copies, waits for them, and re-layouts  1.13 us (1%)
    all_to_all x1, blocking collectives, shards(): lax.all_to_all(gate_part, ('ey', 'core', 'tensor'), 0, 0, tiled=True)  36.1 us
    ppermute x7, starting transfers between devices, turn(): lax.ppermute(block, 'ey', [(i, (i + by) % size) for i in range(size)])  27.8 us
    ppermute x2, starting transfers between devices, gathered(): lax.ppermute(jnp.concatenate(g, axis=0), 'core', swap)  16.5 us
    ppermute x3, starting transfers between devices, shards(): grads[step] = lax.ppermute(grads[step], 'edata', to_owner)  8.41 us
    ppermute x7, waiting for transfers between devices, turn(): lax.ppermute(block, 'ey', [(i, (i + by) % size) for i in range(size)])  5.43 us
    pallas_call x1, Pallas kernels, shards(): pl.pallas_call(functools.partial(own_kernel, tokens, rows, width, planes,...  4.56 us
    pallas_call x1, Pallas kernels, shards(): pl.pallas_call(functools.partial(adam_kernel, part, replicas), out_shape=...  2.55 us
  transfers between devices with their start and end apart: 12, of which 4 were waited for; matrix products, arithmetic and copies ran while one was open for 1% of the time, Pallas kernels for 1%

profile of v8, /device:TPU:1, one launch (start us, length us, event | category | flops | bytes accessed | tf_op | source)
XLA Modules:
  0.0 107.8 jit_solution(136831496517676183)
XLA Ops:
  0.6 1.7 %pack.1.refs_0_ = bf16[32,4224]{1,0:T(8,128)(2,1)} custom-call(bf16[32,4096]{1,0:T(8,128)(2,1)} %rows_in.1, s32[8,32]{1,0:T(8,128)} %bitcast.21, bf16[8,32]{1,0:T(8,128)(2,1)} %bitcast.25), custom_call_target="tpu_custom_call" | custom-call | tf_op jit(solution)/shard_map/pack/pallas_call | solution.py:214
  2.3 0.0 copy-start.1
  2.3 6.1 %collective-permute-start.1 = (bf16[32,4224]{1,0:T(8,128)(2,1)}, bf16[32,4224]{1,0:T(8,128)(2,1)S(1)}, u32[]{:S(2)}, u32[]{:S(2)}) collective-permute-start(bf16[32,4224]{1,0:T(8,128)(2,1)} %pack.1.refs_0_), channel_id=1, source_target_pairs={{0,168},{24,0},{48,24},{72,48},{96,72},{120,96},{144,120},{168,144... | collective-permute-start | bytes 811016 | tf_op jit(solution)/shard_map/ppermute | solution.py:187
  8.4 1.9 %collective-permute-start = (bf16[32,4224]{1,0:T(8,128)(2,1)}, bf16[32,4224]{1,0:T(8,128)(2,1)S(1)}, u32[]{:S(2)}, u32[]{:S(2)}) collective-permute-start(bf16[32,4224]{1,0:T(8,128)(2,1)} %pack.1.refs_0_), channel_id=1, source_target_pairs={{0,24},{24,48},{48,72},{72,96},{96,120},{120,144},{144,168},{168,0... | collective-permute-start | bytes 811016 | tf_op jit(solution)/shard_map/ppermute | solution.py:187
  10.3 1.0 constant_dynamic-update-slice_fusion.4
  11.3 0.8 collective-permute-done.1.refs_2_
  12.1 4.9 %collective-permute-start.3 = (bf16[32,4224]{1,0:T(8,128)(2,1)S(1)}, bf16[32,4224]{1,0:T(8,128)(2,1)S(1)}, u32[]{:S(2)}, u32[]{:S(2)}) collective-permute-start(bf16[32,4224]{1,0:T(8,128)(2,1)S(1)} %collective-permute-done.1.refs_2_), channel_id=1, source_target_pairs={{0,168},{24,0},{48,24},{72,48},{96,72},{120,96},{144,120},{168,144... | collective-permute-start | bytes 811016 | tf_op jit(solution)/shard_map/ppermute | solution.py:187
  17.0 0.0 collective-permute-done.refs_1_
  17.0 1.9 %collective-permute-start.2 = (bf16[32,4224]{1,0:T(8,128)(2,1)S(1)}, bf16[32,4224]{1,0:T(8,128)(2,1)S(1)}, u32[]{:S(2)}, u32[]{:S(2)}) collective-permute-start(bf16[32,4224]{1,0:T(8,128)(2,1)S(1)} %collective-permute-done.refs_1_), channel_id=1, source_target_pairs={{0,24},{24,48},{48,72},{72,96},{96,120},{120,144},{144,168},{168,0... | collective-permute-start | bytes 811016 | tf_op jit(solution)/shard_map/ppermute | solution.py:187
  19.0 0.0 copy-start
  19.0 0.0 copy-start.5
  19.0 2.9 %collective-permute-done.3.refs_4_ = bf16[32,4224]{1,0:T(8,128)(2,1)S(1)} collective-permute-done((bf16[32,4224]{1,0:T(8,128)(2,1)S(1)}, bf16[32,4224]{1,0:T(8,128)(2,1)S(1)}, u32[]{:S(2)}, u32[]{:S(2)}) %collective-permute-start.3) | collective-permute-done | bytes 270368 | tf_op jit(solution)/shard_map/ppermute | solution.py:187
  21.9 0.0 copy-done.1
  21.9 6.6 %collective-permute-start.4 = (bf16[32,4224]{1,0:T(8,128)(2,1)S(1)}, bf16[32,4224]{1,0:T(8,128)(2,1)S(1)}, u32[]{:S(2)}, u32[]{:S(2)}) collective-permute-start(bf16[32,4224]{1,0:T(8,128)(2,1)S(1)} %copy-done.1), channel_id=1, source_target_pairs={{0,96},{24,120},{48,144},{72,168},{96,0},{120,24},{144,48},{168,72... | collective-permute-start | bytes 811016 | tf_op jit(solution)/shard_map/ppermute | solution.py:187
  28.5 4.5 %collective-permute-start.6 = (bf16[32,4224]{1,0:T(8,128)(2,1)S(1)}, bf16[32,4224]{1,0:T(8,128)(2,1)S(1)}, u32[]{:S(2)}, u32[]{:S(2)}) collective-permute-start(bf16[32,4224]{1,0:T(8,128)(2,1)S(1)} %collective-permute-done.3.refs_4_), channel_id=1, source_target_pairs={{0,168},{24,0},{48,24},{72,48},{96,72},{120,96},{144,120},{168,144... | collective-permute-start | bytes 811016 | tf_op jit(solution)/shard_map/ppermute | solution.py:187
  33.0 0.0 collective-permute-done.2.refs_3_
  33.0 1.9 %collective-permute-start.5 = (bf16[32,4224]{1,0:T(8,128)(2,1)S(1)}, bf16[32,4224]{1,0:T(8,128)(2,1)S(1)}, u32[]{:S(2)}, u32[]{:S(2)}) collective-permute-start(bf16[32,4224]{1,0:T(8,128)(2,1)S(1)} %collective-permute-done.2.refs_3_), channel_id=1, source_target_pairs={{0,24},{24,48},{48,72},{72,96},{96,120},{120,144},{144,168},{168,0... | collective-permute-start | bytes 811016 | tf_op jit(solution)/shard_map/ppermute | solution.py:187
  35.0 11.0 %collective-permute-start.7 = (bf16[160,4224]{1,0:T(8,128)(2,1)S(1)}, bf16[160,4224]{1,0:T(8,128)(2,1)S(1)}, u32[]{:S(2)}, u32[]{:S(2)}) collective-permute-start(bf16[160,4224]{1,0:T(8,128)(2,1)S(1)} %constant_dynamic-update-slice_fusion), channel_id=1, source_target_pairs={{0,12},{12,0},{1,13},{13,1},{2,14},{14,2},{3,15},{15,3},{4,16},{16... | collective-permute-start | bytes 4055048 | tf_op jit(solution)/shard_map/ppermute | solution.py:199
  46.0 0.0 collective-permute-done.4.refs_5_
  46.0 0.0 collective-permute-done.6.refs_7_
  46.0 1.8 %collective-permute-done.5.refs_6_ = bf16[32,4224]{1,0:T(8,128)(2,1)S(1)} collective-permute-done((bf16[32,4224]{1,0:T(8,128)(2,1)S(1)}, bf16[32,4224]{1,0:T(8,128)(2,1)S(1)}, u32[]{:S(2)}, u32[]{:S(2)}) %collective-permute-start.5) | collective-permute-done | bytes 270368 | tf_op jit(solution)/shard_map/ppermute | solution.py:187
  47.8 0.1 pad_maximum_fusion
  47.9 5.5 %collective-permute-start.8 = (bf16[96,4224]{1,0:T(8,128)(2,1)S(1)}, bf16[96,4224]{1,0:T(8,128)(2,1)S(1)}, u32[]{:S(2)}, u32[]{:S(2)}) collective-permute-start(bf16[96,4224]{1,0:T(8,128)(2,1)S(1)} %pad_maximum_fusion), channel_id=1, source_target_pairs={{0,12},{12,0},{1,13},{13,1},{2,14},{14,2},{3,15},{15,3},{4,16},{16... | collective-permute-start | bytes 2433032 | tf_op jit(solution)/shard_map/ppermute | solution.py:199
  53.4 1.9 %collective-permute-done.8.refs_9_ = bf16[96,4224]{1,0:T(8,128)(2,1)S(1)} collective-permute-done((bf16[96,4224]{1,0:T(8,128)(2,1)S(1)}, bf16[96,4224]{1,0:T(8,128)(2,1)S(1)}, u32[]{:S(2)}, u32[]{:S(2)}) %collective-permute-start.8) | collective-permute-done | bytes 811040 | tf_op jit(solution)/shard_map/ppermute | solution.py:199
  55.3 0.0 collective-permute-done.7.refs_8_
  55.3 0.0 copy-done
  55.3 0.0 copy-done.5
  55.3 0.0 copy-start.4
  55.3 0.0 copy-start.2
  55.3 0.0 copy-start.3
  55.3 4.6 %own_tokens.1 = (bf16[8,2,24,128]{3,2,1,0:T(8,128)(2,1)}, f32[192,1,64]{2,1,0:T(1,128)S(1)}, bf16[1024,256]{1,0:T(8,128)(2,1)S(1)}, bf16[1024,256]{1,0:T(8,128)(...) custom-call(bf16[32,4224]{1,0:T(8,128)(2,1)S(1)} %copy-done.1, ...), custom_call_target="tpu_custom_call" | custom-call | flops 2147483648 | bytes 8388608 | tf_op jit(solution)/shard_map/own_tokens/pallas_call | solution.py:229
  59.9 1.9 %collective-permute-start.9 = (bf16[1024,256]{1,0:T(8,128)(2,1)S(1)}, bf16[1024,256]{1,0:T(8,128)(2,1)S(1)}, u32[]{:S(2)}, u32[]{:S(2)}) collective-permute-start(bf16[1024,256]{1,0:T(8,128)(2,1)S(1)} %get-tuple-element.21), channel_id=1, source_target_pairs={{0,192},{192,384},{384,576},{576,0},{1,193},{193,385},{385,577},{5... | collective-permute-start | bytes 1572872 | tf_op jit(solution)/shard_map/ppermute | solution.py:244
  61.8 3.1 %collective-permute-start.10 = (bf16[1024,256]{1,0:T(8,128)(2,1)S(1)}, bf16[1024,256]{1,0:T(8,128)(2,1)S(1)}, u32[]{:S(2)}, u32[]{:S(2)}) collective-permute-start(bf16[1024,256]{1,0:T(8,128)(2,1)S(1)} %get-tuple-element.22), channel_id=1, source_target_pairs={{0,384},{192,576},{384,0},{576,192},{1,385},{193,577},{385,1},{577... | collective-permute-start | bytes 1572872 | tf_op jit(solution)/shard_map/ppermute | solution.py:244
  64.9 3.4 %collective-permute-start.11 = (bf16[1024,256]{1,0:T(8,128)(2,1)S(1)}, bf16[1024,256]{1,0:T(8,128)(2,1)S(1)}, u32[]{:S(2)}, u32[]{:S(2)}) collective-permute-start(bf16[1024,256]{1,0:T(8,128)(2,1)S(1)} %get-tuple-element.23), channel_id=1, source_target_pairs={{0,576},{192,0},{384,192},{576,384},{1,577},{193,1},{385,193},{577... | collective-permute-start | bytes 1572872 | tf_op jit(solution)/shard_map/ppermute | solution.py:244
  68.3 36.1 %all_to_all.5.arrived = f32[192,1,64]{2,1,0:T(1,128)S(1)} all-to-all(f32[192,1,64]{2,1,0:T(1,128)S(1)} %get-tuple-element.19), channel_id=1, replica_groups=mesh['edata'=4,'ey'=8,'core'=2,'tensor'=12] {'ey','core','tensor'}, dimensions={0} | all-to-all | bytes 98304 | tf_op jit(solution)/shard_map/all_to_all | solution.py:245
  104.5 0.0 copy-done.4
  104.5 0.7 gates_home.1
  105.2 0.0 collective-permute-done.9.refs_1_
  105.2 0.0 collective-permute-done.10.refs_2_
  105.2 0.0 collective-permute-done.11.refs_3_
  105.2 0.0 copy-done.2
  105.2 0.0 copy-done.3
  105.2 2.6 %adam.1 = (bf16[2048,128]{1,0:T(8,128)(2,1)}, bf16[2048,128]{1,0:T(8,128)(2,1)}, f32[2048,128]{1,0:T(8,128)}) custom-call(bf16[1024,256]{1,0:T(8,128)(2,1)S(1)} %get-tuple-element.20.refs_0_, bf16[1024,256]{1,0:T(8,128)(2,1)S(1)} %collective-permute-done.9.refs_1_, bf16[1024,256]{1,0:T(8,128)(2,1)S(1)} %collective-permute-done.10.refs_2_, ...), custom_call_target="tpu_custom_call" | custom-call | flops 524288 | bytes 8388608 | tf_op jit(solution)/shard_map/adam/pallas_call | solution.py:247
  (4 shorter events, 0.1 us)
Async XLA Ops:
  2.3 19.6 %copy-start.1 = (bf16[32,4224]{1,0:T(8,128)(2,1)S(1)}, bf16[32,4224]{1,0:T(8,128)(2,1)}, u32[]{:S(2)}) copy-start(bf16[32,4224]{1,0:T(8,128)(2,1)} %pack.1.refs_0_) | copy-start | bytes 811012
  2.3 9.8 %collective-permute-start.1 = (bf16[32,4224]{1,0:T(8,128)(2,1)}, bf16[32,4224]{1,0:T(8,128)(2,1)S(1)}, u32[]{:S(2)}, u32[]{:S(2)}) collective-permute-start(bf16[32,4224]{1,0:T(8,128)(2,1)} %pack.1.refs_0_), channel_id=1, source_target_pairs={{0,168},{24,0},{48,24},{72,48},{96,72},{120,96},{144,120},{168,144... | collective-permute-start | bytes 811016 | tf_op jit(solution)/shard_map/ppermute | solution.py:187
  8.4 8.6 %collective-permute-start = (bf16[32,4224]{1,0:T(8,128)(2,1)}, bf16[32,4224]{1,0:T(8,128)(2,1)S(1)}, u32[]{:S(2)}, u32[]{:S(2)}) collective-permute-start(bf16[32,4224]{1,0:T(8,128)(2,1)} %pack.1.refs_0_), channel_id=1, source_target_pairs={{0,24},{24,48},{48,72},{72,96},{96,120},{120,144},{144,168},{168,0... | collective-permute-start | bytes 811016 | tf_op jit(solution)/shard_map/ppermute | solution.py:187
  12.1 9.8 %collective-permute-start.3 = (bf16[32,4224]{1,0:T(8,128)(2,1)S(1)}, bf16[32,4224]{1,0:T(8,128)(2,1)S(1)}, u32[]{:S(2)}, u32[]{:S(2)}) collective-permute-start(bf16[32,4224]{1,0:T(8,128)(2,1)S(1)} %collective-permute-done.1.refs_2_), channel_id=1, source_target_pairs={{0,168},{24,0},{48,24},{72,48},{96,72},{120,96},{144,120},{168,144... | collective-permute-start | bytes 811016 | tf_op jit(solution)/shard_map/ppermute | solution.py:187
  17.0 16.0 %collective-permute-start.2 = (bf16[32,4224]{1,0:T(8,128)(2,1)S(1)}, bf16[32,4224]{1,0:T(8,128)(2,1)S(1)}, u32[]{:S(2)}, u32[]{:S(2)}) collective-permute-start(bf16[32,4224]{1,0:T(8,128)(2,1)S(1)} %collective-permute-done.refs_1_), channel_id=1, source_target_pairs={{0,24},{24,48},{48,72},{72,96},{96,120},{120,144},{144,168},{168,0... | collective-permute-start | bytes 811016 | tf_op jit(solution)/shard_map/ppermute | solution.py:187
  19.0 36.3 %copy-start = (bf16[2,128,4096]{2,1,0:T(8,128)(2,1)S(1)}, bf16[2,128,4096]{2,1,0:T(8,128)(2,1)}, u32[]{:S(2)}) copy-start(bf16[2,128,4096]{2,1,0:T(8,128)(2,1)} %param.11) | copy-start | bytes 6291460
  19.0 36.3 %copy-start.5 = (bf16[1,16,2,12,128]{4,2,3,1,0:T(2,128)(2,1)S(1)}, bf16[1,16,2,12,128]{4,2,3,1,0:T(2,128)(2,1)}, u32[]{:S(2)}) copy-start(bf16[1,16,2,12,128]{4,2,3,1,0:T(2,128)(2,1)} %param.10) | copy-start | bytes 294916
  21.9 24.1 %collective-permute-start.4 = (bf16[32,4224]{1,0:T(8,128)(2,1)S(1)}, bf16[32,4224]{1,0:T(8,128)(2,1)S(1)}, u32[]{:S(2)}, u32[]{:S(2)}) collective-permute-start(bf16[32,4224]{1,0:T(8,128)(2,1)S(1)} %copy-done.1), channel_id=1, source_target_pairs={{0,96},{24,120},{48,144},{72,168},{96,0},{120,24},{144,48},{168,72... | collective-permute-start | bytes 811016 | tf_op jit(solution)/shard_map/ppermute | solution.py:187
  28.5 17.5 %collective-permute-start.6 = (bf16[32,4224]{1,0:T(8,128)(2,1)S(1)}, bf16[32,4224]{1,0:T(8,128)(2,1)S(1)}, u32[]{:S(2)}, u32[]{:S(2)}) collective-permute-start(bf16[32,4224]{1,0:T(8,128)(2,1)S(1)} %collective-permute-done.3.refs_4_), channel_id=1, source_target_pairs={{0,168},{24,0},{48,24},{72,48},{96,72},{120,96},{144,120},{168,144... | collective-permute-start | bytes 811016 | tf_op jit(solution)/shard_map/ppermute | solution.py:187
  33.0 14.8 %collective-permute-start.5 = (bf16[32,4224]{1,0:T(8,128)(2,1)S(1)}, bf16[32,4224]{1,0:T(8,128)(2,1)S(1)}, u32[]{:S(2)}, u32[]{:S(2)}) collective-permute-start(bf16[32,4224]{1,0:T(8,128)(2,1)S(1)} %collective-permute-done.2.refs_3_), channel_id=1, source_target_pairs={{0,24},{24,48},{48,72},{72,96},{96,120},{120,144},{144,168},{168,0... | collective-permute-start | bytes 811016 | tf_op jit(solution)/shard_map/ppermute | solution.py:187
  35.0 20.3 %collective-permute-start.7 = (bf16[160,4224]{1,0:T(8,128)(2,1)S(1)}, bf16[160,4224]{1,0:T(8,128)(2,1)S(1)}, u32[]{:S(2)}, u32[]{:S(2)}) collective-permute-start(bf16[160,4224]{1,0:T(8,128)(2,1)S(1)} %constant_dynamic-update-slice_fusion), channel_id=1, source_target_pairs={{0,12},{12,0},{1,13},{13,1},{2,14},{14,2},{3,15},{15,3},{4,16},{16... | collective-permute-start | bytes 4055048 | tf_op jit(solution)/shard_map/ppermute | solution.py:199
  47.9 7.4 %collective-permute-start.8 = (bf16[96,4224]{1,0:T(8,128)(2,1)S(1)}, bf16[96,4224]{1,0:T(8,128)(2,1)S(1)}, u32[]{:S(2)}, u32[]{:S(2)}) collective-permute-start(bf16[96,4224]{1,0:T(8,128)(2,1)S(1)} %pad_maximum_fusion), channel_id=1, source_target_pairs={{0,12},{12,0},{1,13},{13,1},{2,14},{14,2},{3,15},{15,3},{4,16},{16... | collective-permute-start | bytes 2433032 | tf_op jit(solution)/shard_map/ppermute | solution.py:199
  55.3 49.2 %copy-start.4 = (s32[32,8]{0,1:T(8,128)S(1)}, s32[32,8]{0,1:T(8,128)}, u32[]{:S(2)}) copy-start(s32[32,8]{0,1:T(8,128)} %param.9) | copy-start | bytes 3076
  55.3 49.9 %copy-start.2 = (f32[1024,2,128]{2,1,0:T(2,128)S(1)}, f32[1024,2,128]{2,1,0:T(2,128)}, u32[]{:S(2)}) copy-start(f32[1024,2,128]{2,1,0:T(2,128)} %param.13) | copy-start | bytes 3145732
  55.3 49.9 %copy-start.3 = (bf16[1024,2,128]{2,1,0:T(2,128)(2,1)S(1)}, bf16[1024,2,128]{2,1,0:T(2,128)(2,1)}, u32[]{:S(2)}) copy-start(bf16[1024,2,128]{2,1,0:T(2,128)(2,1)} %param.12) | copy-start | bytes 1572868
  59.9 45.3 %collective-permute-start.9 = (bf16[1024,256]{1,0:T(8,128)(2,1)S(1)}, bf16[1024,256]{1,0:T(8,128)(2,1)S(1)}, u32[]{:S(2)}, u32[]{:S(2)}) collective-permute-start(bf16[1024,256]{1,0:T(8,128)(2,1)S(1)} %get-tuple-element.21), channel_id=1, source_target_pairs={{0,192},{192,384},{384,576},{576,0},{1,193},{193,385},{385,577},{5... | collective-permute-start | bytes 1572872 | tf_op jit(solution)/shard_map/ppermute | solution.py:244
  61.8 43.4 %collective-permute-start.10 = (bf16[1024,256]{1,0:T(8,128)(2,1)S(1)}, bf16[1024,256]{1,0:T(8,128)(2,1)S(1)}, u32[]{:S(2)}, u32[]{:S(2)}) collective-permute-start(bf16[1024,256]{1,0:T(8,128)(2,1)S(1)} %get-tuple-element.22), channel_id=1, source_target_pairs={{0,384},{192,576},{384,0},{576,192},{1,385},{193,577},{385,1},{577... | collective-permute-start | bytes 1572872 | tf_op jit(solution)/shard_map/ppermute | solution.py:244
  64.9 40.3 %collective-permute-start.11 = (bf16[1024,256]{1,0:T(8,128)(2,1)S(1)}, bf16[1024,256]{1,0:T(8,128)(2,1)S(1)}, u32[]{:S(2)}, u32[]{:S(2)}) collective-permute-start(bf16[1024,256]{1,0:T(8,128)(2,1)S(1)} %get-tuple-element.23), channel_id=1, source_target_pairs={{0,576},{192,0},{384,192},{576,384},{1,577},{193,1},{385,193},{577... | collective-permute-start | bytes 1572872 | tf_op jit(solution)/shard_map/ppermute | solution.py:244

commit v9 on v8

--- a/solution.py
+++ b/solution.py
@@ -191,10 +191,8 @@
     for _ in range(2, size // 2 - 1):
         up, down = turn(up, 1), turn(down, -1)
         mine += [up, down]
-    again, down = lax.optimization_barrier((own, down))
-    far = turn(again, size // 2)
-    mine[-2:] = [up, down]
-    last = [far, turn(up, 1), turn(down, -1)]
+    half = own.shape[0] // 2
+    last = [turn(up[:half], 2), turn(down[half:], -2), turn(up, 1), turn(down, -1)]
     swap = [(0, 1), (1, 0)]
     theirs = [lax.ppermute(jnp.concatenate(g, axis=0), "core", swap) for g in (mine, last)]
     return mine + last + theirs

time: 108 us -> 108 us (level)
  starting transfers between devices: 52.7 us -> 57.7 us
  blocking collectives: 36.1 us -> 31.2 us
    ppermute x2, starting transfers between devices: 16.5 us -> 21.5 us  [gathered(): lax.ppermute(jnp.concatenate(g, axis=0), 'core', swap)]
    all_to_all x1, blocking collectives: 36.1 us -> 31.2 us  [shards(): lax.all_to_all(gate_part, ('ey', 'core', 'tensor'), 0, 0, tiled=True)]
    ppermute x7 -> x8, waiting for transfers between devices: 5.43 us -> 4.73 us  [turn(): lax.ppermute(block, 'ey', [(i, (i + by) % size) for i in range(size)])]
    ppermute x7 -> x8, starting transfers between devices: 27.8 us -> 27.8 us  [turn(): lax.ppermute(block, 'ey', [(i, (i + by) % size) for i in range(size)])]
  transfers between devices with their start and end apart: 12 -> 13, of which waited for: 4 -> 4; matrix products, arithmetic and copies ran while one was open for 1% -> 1% of each run, Pallas kernels for 1% -> 1%
where the time goes in v9:
time: 108 us; the launch traced here: 107 us
  starting transfers between devices  57.7 us (53%)
  blocking collectives  31.2 us (29%)
  Pallas kernels  9.5 us (9%)
  waiting for transfers between devices  6.67 us (6%)
  local copies, waits for them, and re-layouts  1.15 us (1%)
    all_to_all x1, blocking collectives, shards(): lax.all_to_all(gate_part, ('ey', 'core', 'tensor'), 0, 0, tiled=True)  31.2 us
    ppermute x8, starting transfers between devices, turn(): lax.ppermute(block, 'ey', [(i, (i + by) % size) for i in range(size)])  27.8 us
    ppermute x2, starting transfers between devices, gathered(): lax.ppermute(jnp.concatenate(g, axis=0), 'core', swap)  21.5 us
    ppermute x3, starting transfers between devices, shards(): grads[step] = lax.ppermute(grads[step], 'edata', to_owner)  8.41 us
    ppermute x8, waiting for transfers between devices, turn(): lax.ppermute(block, 'ey', [(i, (i + by) % size) for i in range(size)])  4.73 us
    pallas_call x1, Pallas kernels, shards(): pl.pallas_call(functools.partial(own_kernel, tokens, rows, width, planes,...  4.56 us
    pallas_call x1, Pallas kernels, shards(): pl.pallas_call(functools.partial(adam_kernel, part, replicas), out_shape=...  2.55 us
  transfers between devices with their start and end apart: 13, of which 4 were waited for; matrix products, arithmetic and copies ran while one was open for 1% of the time, Pallas kernels for 1%

profile of v9, /device:TPU:1, one launch (start us, length us, event | category | flops | bytes accessed | tf_op | source)
XLA Modules:
  0.0 107.2 jit_solution(2198771736321770803)
XLA Ops:
  0.6 1.7 %pack.1.refs_0_ = bf16[32,4224]{1,0:T(8,128)(2,1)} custom-call(bf16[32,4096]{1,0:T(8,128)(2,1)} %rows_in.1, s32[8,32]{1,0:T(8,128)} %bitcast.21, bf16[8,32]{1,0:T(8,128)(2,1)} %bitcast.25), custom_call_target="tpu_custom_call" | custom-call | tf_op jit(solution)/shard_map/pack/pallas_call | solution.py:212
  2.3 5.9 %collective-permute-start.1 = (bf16[32,4224]{1,0:T(8,128)(2,1)}, bf16[32,4224]{1,0:T(8,128)(2,1)S(1)}, u32[]{:S(2)}, u32[]{:S(2)}) collective-permute-start(bf16[32,4224]{1,0:T(8,128)(2,1)} %pack.1.refs_0_), channel_id=1, source_target_pairs={{0,168},{24,0},{48,24},{72,48},{96,72},{120,96},{144,120},{168,144... | collective-permute-start | bytes 811016 | tf_op jit(solution)/shard_map/ppermute | solution.py:187
  8.3 1.9 %collective-permute-start = (bf16[32,4224]{1,0:T(8,128)(2,1)}, bf16[32,4224]{1,0:T(8,128)(2,1)S(1)}, u32[]{:S(2)}, u32[]{:S(2)}) collective-permute-start(bf16[32,4224]{1,0:T(8,128)(2,1)} %pack.1.refs_0_), channel_id=1, source_target_pairs={{0,24},{24,48},{48,72},{72,96},{96,120},{120,144},{144,168},{168,0... | collective-permute-start | bytes 811016 | tf_op jit(solution)/shard_map/ppermute | solution.py:187
  10.2 1.0 constant_dynamic-update-slice_fusion.4
  11.2 0.8 collective-permute-done.1.refs_2_
  12.0 4.9 %collective-permute-start.3 = (bf16[32,4224]{1,0:T(8,128)(2,1)S(1)}, bf16[32,4224]{1,0:T(8,128)(2,1)S(1)}, u32[]{:S(2)}, u32[]{:S(2)}) collective-permute-start(bf16[32,4224]{1,0:T(8,128)(2,1)S(1)} %collective-permute-done.1.refs_2_), channel_id=1, source_target_pairs={{0,168},{24,0},{48,24},{72,48},{96,72},{120,96},{144,120},{168,144... | collective-permute-start | bytes 811016 | tf_op jit(solution)/shard_map/ppermute | solution.py:187
  16.9 0.0 collective-permute-done.refs_1_
  16.9 1.9 %collective-permute-start.2 = (bf16[32,4224]{1,0:T(8,128)(2,1)S(1)}, bf16[32,4224]{1,0:T(8,128)(2,1)S(1)}, u32[]{:S(2)}, u32[]{:S(2)}) collective-permute-start(bf16[32,4224]{1,0:T(8,128)(2,1)S(1)} %collective-permute-done.refs_1_), channel_id=1, source_target_pairs={{0,24},{24,48},{48,72},{72,96},{96,120},{120,144},{144,168},{168,0... | collective-permute-start | bytes 811016 | tf_op jit(solution)/shard_map/ppermute | solution.py:187
  18.9 2.9 %collective-permute-done.3.refs_4_ = bf16[32,4224]{1,0:T(8,128)(2,1)S(1)} collective-permute-done((bf16[32,4224]{1,0:T(8,128)(2,1)S(1)}, bf16[32,4224]{1,0:T(8,128)(2,1)S(1)}, u32[]{:S(2)}, u32[]{:S(2)}) %collective-permute-start.3) | collective-permute-done | bytes 270368 | tf_op jit(solution)/shard_map/ppermute | solution.py:187
  21.8 3.9 %collective-permute-start.5 = (bf16[16,4224]{1,0:T(8,128)(2,1)S(1)}, bf16[16,4224]{1,0:T(8,128)(2,1)S(1)}, u32[]{:S(2)}, u32[]{:S(2)}) collective-permute-start(bf16[16,4224]{1,0:T(8,128)(2,1)S(1)} %slice.9), channel_id=1, source_target_pairs={{0,144},{24,168},{48,0},{72,24},{96,48},{120,72},{144,96},{168,120... | collective-permute-start | bytes 405512 | tf_op jit(solution)/shard_map/ppermute | solution.py:187
  25.7 1.0 collective-permute-done.2.refs_3_
  26.8 0.0 copy-start
  26.8 0.0 copy-start.1
  26.8 0.0 copy-start.5
  26.8 2.1 %collective-permute-start.4 = (bf16[16,4224]{1,0:T(8,128)(2,1)S(1)}, bf16[16,4224]{1,0:T(8,128)(2,1)S(1)}, u32[]{:S(2)}, u32[]{:S(2)}) collective-permute-start(bf16[16,4224]{1,0:T(8,128)(2,1)S(1)} %slice.8), channel_id=1, source_target_pairs={{0,48},{24,72},{48,96},{72,120},{96,144},{120,168},{144,0},{168,24... | collective-permute-start | bytes 405512 | tf_op jit(solution)/shard_map/ppermute | solution.py:187
  28.9 5.2 %collective-permute-start.7 = (bf16[32,4224]{1,0:T(8,128)(2,1)S(1)}, bf16[32,4224]{1,0:T(8,128)(2,1)S(1)}, u32[]{:S(2)}, u32[]{:S(2)}) collective-permute-start(bf16[32,4224]{1,0:T(8,128)(2,1)S(1)} %collective-permute-done.3.refs_4_), channel_id=1, source_target_pairs={{0,168},{24,0},{48,24},{72,48},{96,72},{120,96},{144,120},{168,144... | collective-permute-start | bytes 811016 | tf_op jit(solution)/shard_map/ppermute | solution.py:187
  34.1 1.9 %collective-permute-start.6 = (bf16[32,4224]{1,0:T(8,128)(2,1)S(1)}, bf16[32,4224]{1,0:T(8,128)(2,1)S(1)}, u32[]{:S(2)}, u32[]{:S(2)}) collective-permute-start(bf16[32,4224]{1,0:T(8,128)(2,1)S(1)} %collective-permute-done.2.refs_3_), channel_id=1, source_target_pairs={{0,24},{24,48},{48,72},{72,96},{96,120},{120,144},{144,168},{168,0... | collective-permute-start | bytes 811016 | tf_op jit(solution)/shard_map/ppermute | solution.py:187
  36.1 14.0 %collective-permute-start.8 = (bf16[160,4224]{1,0:T(8,128)(2,1)S(1)}, bf16[160,4224]{1,0:T(8,128)(2,1)S(1)}, u32[]{:S(2)}, u32[]{:S(2)}) collective-permute-start(bf16[160,4224]{1,0:T(8,128)(2,1)S(1)} %constant_dynamic-update-slice_fusion), channel_id=1, source_target_pairs={{0,12},{12,0},{1,13},{13,1},{2,14},{14,2},{3,15},{15,3},{4,16},{16... | collective-permute-start | bytes 4055048 | tf_op jit(solution)/shard_map/ppermute | solution.py:197
  50.1 0.0 collective-permute-done.5.refs_6_
  50.1 0.0 collective-permute-done.4.refs_5_
  50.1 0.0 collective-permute-done.7.refs_8_
  50.1 0.0 collective-permute-done.6.refs_7_
  50.1 0.1 pad_maximum_fusion
  50.2 7.5 %collective-permute-start.9 = (bf16[96,4224]{1,0:T(8,128)(2,1)S(1)}, bf16[96,4224]{1,0:T(8,128)(2,1)S(1)}, u32[]{:S(2)}, u32[]{:S(2)}) collective-permute-start(bf16[96,4224]{1,0:T(8,128)(2,1)S(1)} %pad_maximum_fusion), channel_id=1, source_target_pairs={{0,12},{12,0},{1,13},{13,1},{2,14},{14,2},{3,15},{15,3},{4,16},{16... | collective-permute-start | bytes 2433032 | tf_op jit(solution)/shard_map/ppermute | solution.py:197
  57.7 1.9 %collective-permute-done.9.refs_10_ = bf16[96,4224]{1,0:T(8,128)(2,1)S(1)} collective-permute-done((bf16[96,4224]{1,0:T(8,128)(2,1)S(1)}, bf16[96,4224]{1,0:T(8,128)(2,1)S(1)}, u32[]{:S(2)}, u32[]{:S(2)}) %collective-permute-start.9) | collective-permute-done | bytes 811040 | tf_op jit(solution)/shard_map/ppermute | solution.py:197
  59.6 0.0 collective-permute-done.8.refs_9_
  59.6 0.0 copy-done
  59.6 0.0 copy-done.1
  59.6 0.0 copy-done.5
  59.6 0.0 copy-start.4
  59.7 0.0 copy-start.2
  59.7 0.0 copy-start.3
  59.7 4.6 %own_tokens.1 = (bf16[8,2,24,128]{3,2,1,0:T(8,128)(2,1)}, f32[192,1,64]{2,1,0:T(1,128)S(1)}, bf16[1024,256]{1,0:T(8,128)(2,1)S(1)}, bf16[1024,256]{1,0:T(8,128)(...) custom-call(bf16[32,4224]{1,0:T(8,128)(2,1)S(1)} %copy-done.1, ...), custom_call_target="tpu_custom_call" | custom-call | flops 2147483648 | bytes 8388608 | tf_op jit(solution)/shard_map/own_tokens/pallas_call | solution.py:227
  64.3 1.9 %collective-permute-start.10 = (bf16[1024,256]{1,0:T(8,128)(2,1)S(1)}, bf16[1024,256]{1,0:T(8,128)(2,1)S(1)}, u32[]{:S(2)}, u32[]{:S(2)}) collective-permute-start(bf16[1024,256]{1,0:T(8,128)(2,1)S(1)} %get-tuple-element.17), channel_id=1, source_target_pairs={{0,192},{192,384},{384,576},{576,0},{1,193},{193,385},{385,577},{5... | collective-permute-start | bytes 1572872 | tf_op jit(solution)/shard_map/ppermute | solution.py:242
  66.2 1.9 %collective-permute-start.11 = (bf16[1024,256]{1,0:T(8,128)(2,1)S(1)}, bf16[1024,256]{1,0:T(8,128)(2,1)S(1)}, u32[]{:S(2)}, u32[]{:S(2)}) collective-permute-start(bf16[1024,256]{1,0:T(8,128)(2,1)S(1)} %get-tuple-element.18), channel_id=1, source_target_pairs={{0,384},{192,576},{384,0},{576,192},{1,385},{193,577},{385,1},{577... | collective-permute-start | bytes 1572872 | tf_op jit(solution)/shard_map/ppermute | solution.py:242
  68.1 4.6 %collective-permute-start.12 = (bf16[1024,256]{1,0:T(8,128)(2,1)S(1)}, bf16[1024,256]{1,0:T(8,128)(2,1)S(1)}, u32[]{:S(2)}, u32[]{:S(2)}) collective-permute-start(bf16[1024,256]{1,0:T(8,128)(2,1)S(1)} %get-tuple-element.19), channel_id=1, source_target_pairs={{0,576},{192,0},{384,192},{576,384},{1,577},{193,1},{385,193},{577... | collective-permute-start | bytes 1572872 | tf_op jit(solution)/shard_map/ppermute | solution.py:242
  72.7 31.2 %all_to_all.5.arrived = f32[192,1,64]{2,1,0:T(1,128)S(1)} all-to-all(f32[192,1,64]{2,1,0:T(1,128)S(1)} %get-tuple-element.15), channel_id=1, replica_groups=mesh['edata'=4,'ey'=8,'core'=2,'tensor'=12] {'ey','core','tensor'}, dimensions={0} | all-to-all | bytes 98304 | tf_op jit(solution)/shard_map/all_to_all | solution.py:243
  103.9 0.0 copy-done.4
  103.9 0.7 gates_home.1
  104.6 0.0 collective-permute-done.10.refs_1_
  104.6 0.0 collective-permute-done.11.refs_2_
  104.6 0.0 collective-permute-done.12.refs_3_
  104.7 0.0 copy-done.2
  104.7 0.0 copy-done.3
  104.7 2.5 %adam.1 = (bf16[2048,128]{1,0:T(8,128)(2,1)}, bf16[2048,128]{1,0:T(8,128)(2,1)}, f32[2048,128]{1,0:T(8,128)}) custom-call(bf16[1024,256]{1,0:T(8,128)(2,1)S(1)} %get-tuple-element.16.refs_0_, bf16[1024,256]{1,0:T(8,128)(2,1)S(1)} %collective-permute-done.10.refs_1_, bf16[1024,256]{1,0:T(8,128)(2,1)S(1)} %collective-permute-done.11.refs_2_, ...), custom_call_target="tpu_custom_call" | custom-call | flops 524288 | bytes 8388608 | tf_op jit(solution)/shard_map/adam/pallas_call | solution.py:245
  (6 shorter events, 0.1 us)
Async XLA Ops:
  2.3 9.6 %collective-permute-start.1 = (bf16[32,4224]{1,0:T(8,128)(2,1)}, bf16[32,4224]{1,0:T(8,128)(2,1)S(1)}, u32[]{:S(2)}, u32[]{:S(2)}) collective-permute-start(bf16[32,4224]{1,0:T(8,128)(2,1)} %pack.1.refs_0_), channel_id=1, source_target_pairs={{0,168},{24,0},{48,24},{72,48},{96,72},{120,96},{144,120},{168,144... | collective-permute-start | bytes 811016 | tf_op jit(solution)/shard_map/ppermute | solution.py:187
  8.3 8.6 %collective-permute-start = (bf16[32,4224]{1,0:T(8,128)(2,1)}, bf16[32,4224]{1,0:T(8,128)(2,1)S(1)}, u32[]{:S(2)}, u32[]{:S(2)}) collective-permute-start(bf16[32,4224]{1,0:T(8,128)(2,1)} %pack.1.refs_0_), channel_id=1, source_target_pairs={{0,24},{24,48},{48,72},{72,96},{96,120},{120,144},{144,168},{168,0... | collective-permute-start | bytes 811016 | tf_op jit(solution)/shard_map/ppermute | solution.py:187
  12.0 9.8 %collective-permute-start.3 = (bf16[32,4224]{1,0:T(8,128)(2,1)S(1)}, bf16[32,4224]{1,0:T(8,128)(2,1)S(1)}, u32[]{:S(2)}, u32[]{:S(2)}) collective-permute-start(bf16[32,4224]{1,0:T(8,128)(2,1)S(1)} %collective-permute-done.1.refs_2_), channel_id=1, source_target_pairs={{0,168},{24,0},{48,24},{72,48},{96,72},{120,96},{144,120},{168,144... | collective-permute-start | bytes 811016 | tf_op jit(solution)/shard_map/ppermute | solution.py:187
  16.9 9.9 %collective-permute-start.2 = (bf16[32,4224]{1,0:T(8,128)(2,1)S(1)}, bf16[32,4224]{1,0:T(8,128)(2,1)S(1)}, u32[]{:S(2)}, u32[]{:S(2)}) collective-permute-start(bf16[32,4224]{1,0:T(8,128)(2,1)S(1)} %collective-permute-done.refs_1_), channel_id=1, source_target_pairs={{0,24},{24,48},{48,72},{72,96},{96,120},{120,144},{144,168},{168,0... | collective-permute-start | bytes 811016 | tf_op jit(solution)/shard_map/ppermute | solution.py:187
  21.8 28.3 %collective-permute-start.5 = (bf16[16,4224]{1,0:T(8,128)(2,1)S(1)}, bf16[16,4224]{1,0:T(8,128)(2,1)S(1)}, u32[]{:S(2)}, u32[]{:S(2)}) collective-permute-start(bf16[16,4224]{1,0:T(8,128)(2,1)S(1)} %slice.9), channel_id=1, source_target_pairs={{0,144},{24,168},{48,0},{72,24},{96,48},{120,72},{144,96},{168,120... | collective-permute-start | bytes 405512 | tf_op jit(solution)/shard_map/ppermute | solution.py:187
  26.8 32.9 %copy-start = (bf16[2,128,4096]{2,1,0:T(8,128)(2,1)S(1)}, bf16[2,128,4096]{2,1,0:T(8,128)(2,1)}, u32[]{:S(2)}) copy-start(bf16[2,128,4096]{2,1,0:T(8,128)(2,1)} %param.11) | copy-start | bytes 6291460
  26.8 32.9 %copy-start.1 = (bf16[32,4224]{1,0:T(8,128)(2,1)S(1)}, bf16[32,4224]{1,0:T(8,128)(2,1)}, u32[]{:S(2)}) copy-start(bf16[32,4224]{1,0:T(8,128)(2,1)} %pack.1.refs_0_) | copy-start | bytes 811012
  26.8 32.9 %copy-start.5 = (bf16[1,16,2,12,128]{4,2,3,1,0:T(2,128)(2,1)S(1)}, bf16[1,16,2,12,128]{4,2,3,1,0:T(2,128)(2,1)}, u32[]{:S(2)}) copy-start(bf16[1,16,2,12,128]{4,2,3,1,0:T(2,128)(2,1)} %param.10) | copy-start | bytes 294916
  26.8 23.3 %collective-permute-start.4 = (bf16[16,4224]{1,0:T(8,128)(2,1)S(1)}, bf16[16,4224]{1,0:T(8,128)(2,1)S(1)}, u32[]{:S(2)}, u32[]{:S(2)}) collective-permute-start(bf16[16,4224]{1,0:T(8,128)(2,1)S(1)} %slice.8), channel_id=1, source_target_pairs={{0,48},{24,72},{48,96},{72,120},{96,144},{120,168},{144,0},{168,24... | collective-permute-start | bytes 405512 | tf_op jit(solution)/shard_map/ppermute | solution.py:187
  28.9 21.2 %collective-permute-start.7 = (bf16[32,4224]{1,0:T(8,128)(2,1)S(1)}, bf16[32,4224]{1,0:T(8,128)(2,1)S(1)}, u32[]{:S(2)}, u32[]{:S(2)}) collective-permute-start(bf16[32,4224]{1,0:T(8,128)(2,1)S(1)} %collective-permute-done.3.refs_4_), channel_id=1, source_target_pairs={{0,168},{24,0},{48,24},{72,48},{96,72},{120,96},{144,120},{168,144... | collective-permute-start | bytes 811016 | tf_op jit(solution)/shard_map/ppermute | solution.py:187
  34.1 16.0 %collective-permute-start.6 = (bf16[32,4224]{1,0:T(8,128)(2,1)S(1)}, bf16[32,4224]{1,0:T(8,128)(2,1)S(1)}, u32[]{:S(2)}, u32[]{:S(2)}) collective-permute-start(bf16[32,4224]{1,0:T(8,128)(2,1)S(1)} %collective-permute-done.2.refs_3_), channel_id=1, source_target_pairs={{0,24},{24,48},{48,72},{72,96},{96,120},{120,144},{144,168},{168,0... | collective-permute-start | bytes 811016 | tf_op jit(solution)/shard_map/ppermute | solution.py:187
  36.1 23.6 %collective-permute-start.8 = (bf16[160,4224]{1,0:T(8,128)(2,1)S(1)}, bf16[160,4224]{1,0:T(8,128)(2,1)S(1)}, u32[]{:S(2)}, u32[]{:S(2)}) collective-permute-start(bf16[160,4224]{1,0:T(8,128)(2,1)S(1)} %constant_dynamic-update-slice_fusion), channel_id=1, source_target_pairs={{0,12},{12,0},{1,13},{13,1},{2,14},{14,2},{3,15},{15,3},{4,16},{16... | collective-permute-start | bytes 4055048 | tf_op jit(solution)/shard_map/ppermute | solution.py:197
  50.2 9.5 %collective-permute-start.9 = (bf16[96,4224]{1,0:T(8,128)(2,1)S(1)}, bf16[96,4224]{1,0:T(8,128)(2,1)S(1)}, u32[]{:S(2)}, u32[]{:S(2)}) collective-permute-start(bf16[96,4224]{1,0:T(8,128)(2,1)S(1)} %pad_maximum_fusion), channel_id=1, source_target_pairs={{0,12},{12,0},{1,13},{13,1},{2,14},{14,2},{3,15},{15,3},{4,16},{16... | collective-permute-start | bytes 2433032 | tf_op jit(solution)/shard_map/ppermute | solution.py:197
  59.6 44.3 %copy-start.4 = (s32[32,8]{0,1:T(8,128)S(1)}, s32[32,8]{0,1:T(8,128)}, u32[]{:S(2)}) copy-start(s32[32,8]{0,1:T(8,128)} %param.9) | copy-start | bytes 3076
  59.7 45.0 %copy-start.2 = (f32[1024,2,128]{2,1,0:T(2,128)S(1)}, f32[1024,2,128]{2,1,0:T(2,128)}, u32[]{:S(2)}) copy-start(f32[1024,2,128]{2,1,0:T(2,128)} %param.13) | copy-start | bytes 3145732
  59.7 45.0 %copy-start.3 = (bf16[1024,2,128]{2,1,0:T(2,128)(2,1)S(1)}, bf16[1024,2,128]{2,1,0:T(2,128)(2,1)}, u32[]{:S(2)}) copy-start(bf16[1024,2,128]{2,1,0:T(2,128)(2,1)} %param.12) | copy-start | bytes 1572868
  64.3 40.4 %collective-permute-start.10 = (bf16[1024,256]{1,0:T(8,128)(2,1)S(1)}, bf16[1024,256]{1,0:T(8,128)(2,1)S(1)}, u32[]{:S(2)}, u32[]{:S(2)}) collective-permute-start(bf16[1024,256]{1,0:T(8,128)(2,1)S(1)} %get-tuple-element.17), channel_id=1, source_target_pairs={{0,192},{192,384},{384,576},{576,0},{1,193},{193,385},{385,577},{5... | collective-permute-start | bytes 1572872 | tf_op jit(solution)/shard_map/ppermute | solution.py:242
  66.2 38.5 %collective-permute-start.11 = (bf16[1024,256]{1,0:T(8,128)(2,1)S(1)}, bf16[1024,256]{1,0:T(8,128)(2,1)S(1)}, u32[]{:S(2)}, u32[]{:S(2)}) collective-permute-start(bf16[1024,256]{1,0:T(8,128)(2,1)S(1)} %get-tuple-element.18), channel_id=1, source_target_pairs={{0,384},{192,576},{384,0},{576,192},{1,385},{193,577},{385,1},{577... | collective-permute-start | bytes 1572872 | tf_op jit(solution)/shard_map/ppermute | solution.py:242
  68.1 36.5 %collective-permute-start.12 = (bf16[1024,256]{1,0:T(8,128)(2,1)S(1)}, bf16[1024,256]{1,0:T(8,128)(2,1)S(1)}, u32[]{:S(2)}, u32[]{:S(2)}) collective-permute-start(bf16[1024,256]{1,0:T(8,128)(2,1)S(1)} %get-tuple-element.19), channel_id=1, source_target_pairs={{0,576},{192,0},{384,192},{576,384},{1,577},{193,1},{385,193},{577... | collective-permute-start | bytes 1572872 | tf_op jit(solution)/shard_map/ppermute | solution.py:242
